TPU v7x, 128 devices: a whole 4x4x4 slice. The times are simulated.
128 devices in a mesh: seq: 8 (over x, core), dp: 4 (over z), tensor: 4 (over y).
Axes of the slice: x: 4, y: 4, z: 4, core: 2. Of those that a mesh axis runs over, the one named last changes fastest.
Arguments:
- tokens: bfloat16 [16, 1024, 2048], P('dp', 'seq'), may hold values from -6 to 6
- init_state: float32 [16, 2560], P('dp', 'tensor'), may hold values from -6 to 6
- conv_state: bfloat16 [16, 3, 2560], P('dp', None, 'tensor'), may hold values from -6 to 6
- fresh_rows: int32 [16], P('dp'), may hold values 0 or 1
- doc_start: int32 [16], P('dp'), may hold values from 1 to 1024, as said below
- norm_gains: bfloat16 [2, 2048], replicated, may hold values from 0.5 to 1.5
- mix_in: bfloat16 [2, 2048, 2560], P(None, ('seq', 'dp'), 'tensor'), may hold values from -0.125 to 0.125
- mix_out: bfloat16 [2560, 2048], P('tensor', ('seq', 'dp')), may hold values from -0.25 to 0.25
- conv_weight: bfloat16 [4, 2560], P(None, 'tensor'), may hold values from -3 to 3
- conv_bias: bfloat16 [2560], P('tensor'), may hold values from -3 to 3
- gate_blocks: bfloat16 [2, 16, 160, 160], P(None, 'tensor'), may hold values from -0.5 to 0.5
- gate_bias: bfloat16 [2, 2560], P(None, 'tensor'), may hold values from -4 to 4
- decay_param: bfloat16 [2560], P('tensor'), may hold values from -8 to -3
- mlp_in: bfloat16 [2, 2048, 6144], P(None, ('seq', 'dp'), 'tensor'), may hold values from -0.125 to 0.125
- mlp_out: bfloat16 [6144, 2048], P('tensor', ('seq', 'dp')), may hold values from -0.078125 to 0.078125
- cotangent: bfloat16 [16, 1024, 2048], P('dp', 'seq'), may hold values from -6 to 6
Outputs:
- block_out: bfloat16 [16, 1024, 2048], P('dp', 'seq')
- lru_states: float32 [16, 1024, 2560], P('dp', 'seq', 'tensor')
- grad_tokens: bfloat16 [16, 1024, 2048], P('dp', 'seq')
- grad_gains: float32 [2, 2048], replicated
- grad_mix_in: float32 [2, 2048, 2560], P(None, ('seq', 'dp'), 'tensor')
- grad_mix_out: float32 [2560, 2048], P('tensor', ('seq', 'dp'))
- grad_conv_weight: float32 [4, 2560], P(None, 'tensor')
- grad_conv_bias: float32 [2560], P('tensor')
- grad_gate_blocks: float32 [2, 16, 160, 160], P(None, 'tensor')
- grad_gate_bias: float32 [2, 2560], P(None, 'tensor')
- grad_decay: float32 [2560], P('tensor')
- grad_mlp_in: float32 [2, 2048, 6144], P(None, ('seq', 'dp'), 'tensor')
- grad_mlp_out: float32 [6144, 2048], P('tensor', ('seq', 'dp'))
Inputs may be any that keep to these rules, and one draw needn't show every extreme that they name: Positions at (doc_start) and later form a second document that starts from zero states; 1024 means the sequence holds one document. Among the 4 sequences of each index of dp, one has 1024. `fresh_rows`: 1 marks a sequence whose initial recurrence and convolution states are zero whatever init_state and conv_state hold.
All inputs are finite; a program needn't handle non-finite values. No bound on the sum of `fresh_rows` on one device may be relied on, other than what follows from the above.
Results may differ from a plain program's by a relative error of at most 0.025.
Values may be sent and summed in bfloat16 or wider, within the bound.
A program may use at most 192 MiB of HBM per device.

v0:
```python
import jax
import jax.numpy as jnp
from jax import lax
from jax.sharding import PartitionSpec as P

CONV = 4


epsilon = 1e-06
root_floor = 0.001
rate_scale = 8.0


def from_behind(block, axis, distance):
    devices = range(lax.axis_size(axis))
    route = [(i - distance, i) for i in devices if i - distance in devices]
    return lax.ppermute(block, axis, route)


def entering_2(part, axis, combine, identity, reverse):
    count = lax.axis_size(axis)
    place = lax.axis_index(axis)
    ahead = count - 1 - place if reverse else place
    gathered = jax.tree.map(lambda a: lax.all_gather(a, axis), part)
    state = jax.tree.map(lambda a, e: jnp.zeros_like(a) + jnp.asarray(e, a.dtype), part, identity)

    def one(lap, state):
        source = count - 1 - lap if reverse else lap
        return combine(
            state, jax.tree.map(lambda a: lax.dynamic_index_in_dim(a, source, 0, False), gathered)
        )

    return lax.fori_loop(0, ahead, one, state)


def smooth_gate(values):
    return jax.nn.gelu(values, approximate=True)


def linear_step(earlier, later_pair):
    return (earlier[0] * later_pair[0], later_pair[0] * earlier[1] + later_pair[1])


def normalize(stream, gain_row):
    scale_row = lax.rsqrt(jnp.mean(stream * stream, axis=-1, keepdims=True) + epsilon)
    unit_rows = stream * scale_row
    return (unit_rows * gain_row, unit_rows, scale_row)


def normalize_back(upstream, unit_rows, scale_row, gain_row):
    d_unit = upstream * gain_row
    inner = jnp.mean(d_unit * unit_rows, axis=-1, keepdims=True)
    return (scale_row * (d_unit - unit_rows * inner), jnp.sum(upstream * unit_rows, axis=0))


def matmul(left_side, right_side):
    return jnp.dot(left_side, right_side, preferred_element_type=jnp.float32)


def outer_sum(left_side, right_side):
    return lax.dot_general(
        left_side, right_side, (((0,), (0,)), ((), ())), preferred_element_type=jnp.float32
    )


def back_product(left_side, right_side):
    return lax.dot_general(
        left_side, right_side, (((1,), (1,)), ((), ())), preferred_element_type=jnp.float32
    )


def per_device(
    tokens,
    init_state,
    conv_state,
    fresh_rows,
    doc_start,
    norm_gains,
    mix_in,
    mix_out,
    conv_weight,
    conv_bias,
    gate_blocks,
    gate_bias,
    decay_param,
    mlp_in,
    mlp_out,
    cotangent,
):
    row_count, span_len, model_width = tokens.shape
    lru_width = mix_out.shape[0]
    head_count = gate_blocks.shape[1]
    block_size = gate_blocks.shape[2]
    token_count = row_count * span_len
    rim_len = CONV - 1
    mix_full, out_full, mlp_full, down_full = (
        lax.all_gather(mix_in, ("seq", "dp"), axis=1, tiled=True),
        lax.all_gather(mix_out, ("seq", "dp"), axis=1, tiled=True),
        lax.all_gather(mlp_in, ("seq", "dp"), axis=1, tiled=True),
        lax.all_gather(mlp_out, ("seq", "dp"), axis=1, tiled=True),
    )
    stream = tokens.reshape(token_count, model_width).astype(jnp.float32)
    gain_rows = norm_gains.astype(jnp.float32)
    normed_in, unit_in, scale_in = normalize(stream, gain_rows[0])
    normed_in = normed_in.astype(jnp.bfloat16)
    branch_pre = matmul(normed_in, mix_full[0])
    conv_input = (
        matmul(normed_in, mix_full[1]).astype(jnp.bfloat16).reshape(row_count, span_len, lru_width)
    )
    arrived = from_behind(conv_input[:, span_len - rim_len :], "seq", 1)
    seq_index = lax.axis_index("seq")
    keep_init = (1 - fresh_rows).astype(jnp.float32)
    start_rim = conv_state.astype(jnp.float32) * keep_init[:, None, None]
    rim_rows = jnp.where(seq_index == 0, start_rim, arrived.astype(jnp.float32))
    extended = jnp.concatenate([rim_rows, conv_input.astype(jnp.float32)], axis=1)
    offset = seq_index * span_len
    places = offset + jnp.arange(-rim_len, span_len)
    in_second = places[None, :] >= doc_start[:, None]
    conv_taps = conv_weight.astype(jnp.float32)
    same_docs = []
    conv_sum = jnp.zeros((row_count, span_len, lru_width), jnp.float32) + conv_bias.astype(
        jnp.float32
    )
    for tap_index in range(CONV):
        same_doc = (
            in_second[:, tap_index : tap_index + span_len] == in_second[:, rim_len:]
        ).astype(jnp.float32)[:, :, None]
        same_docs.append(same_doc)
        conv_sum = (
            conv_sum
            + conv_taps[tap_index] * extended[:, tap_index : tap_index + span_len] * same_doc
        )
    conv_low = conv_sum.astype(jnp.bfloat16)
    conv_out = conv_low.astype(jnp.float32)
    grouped = conv_low.reshape(token_count, head_count, block_size)
    gate_pre = jnp.einsum(
        "thi,ghij->gthj", grouped, gate_blocks, preferred_element_type=jnp.float32
    )
    gate_pre = (
        gate_pre.reshape(2, row_count, span_len, lru_width)
        + gate_bias.astype(jnp.float32)[:, None, None, :]
    )
    gate_values = jax.nn.sigmoid(gate_pre)
    decay_gate = gate_values[0]
    input_gate = gate_values[1]
    decay_float = decay_param.astype(jnp.float32)
    softened = jax.nn.softplus(decay_float)
    decay_now = jnp.exp(-rate_scale * decay_gate * softened)
    headroom = 1.0 - decay_now * decay_now
    input_root = jnp.sqrt(jnp.maximum(headroom, root_floor))
    fed_value = input_root * input_gate * conv_out
    positions = offset + jnp.arange(span_len)
    keep_step = (positions[None, :] != doc_start[:, None]).astype(jnp.float32)[:, :, None]
    carried = decay_now * keep_step
    cum_decay, local_states = lax.associative_scan(linear_step, (carried, fed_value), axis=1)
    identity = (
        jnp.ones((row_count, lru_width), jnp.float32),
        jnp.zeros((row_count, lru_width), jnp.float32),
    )
    before_decay, before_state = entering_2(
        (cum_decay[:, -1], local_states[:, -1]), "seq", linear_step, identity, False
    )
    entering = before_decay * (init_state * keep_init[:, None]) + before_state
    states = local_states + cum_decay * entering[:, None, :]
    previous = jnp.concatenate([entering[:, None, :], states[:, :-1]], axis=1)
    branch, branch_pull = jax.vjp(smooth_gate, branch_pre)
    branch = branch.reshape(row_count, span_len, lru_width)
    mixed_low = (states * branch).astype(jnp.bfloat16).reshape(token_count, lru_width)
    after_mix = stream + lax.psum(
        matmul(mixed_low, out_full).astype(jnp.bfloat16), "tensor"
    ).astype(jnp.float32)
    normed_mid, unit_mid, scale_mid = normalize(after_mix, gain_rows[1])
    normed_mid = normed_mid.astype(jnp.bfloat16)
    gate_in = matmul(normed_mid, mlp_full[0])
    up_in = matmul(normed_mid, mlp_full[1])
    gate_act, gate_pull = jax.vjp(smooth_gate, gate_in)
    hidden = (gate_act * up_in).astype(jnp.bfloat16)
    result = after_mix + lax.psum(matmul(hidden, down_full).astype(jnp.bfloat16), "tensor").astype(
        jnp.float32
    )
    block_out = result.astype(jnp.bfloat16).reshape(row_count, span_len, model_width)
    mix_full, out_full, mlp_full, down_full = (
        lax.all_gather(mix_in, ("seq", "dp"), axis=1, tiled=True),
        lax.all_gather(mix_out, ("seq", "dp"), axis=1, tiled=True),
        lax.all_gather(mlp_in, ("seq", "dp"), axis=1, tiled=True),
        lax.all_gather(mlp_out, ("seq", "dp"), axis=1, tiled=True),
    )
    upstream = cotangent.reshape(token_count, model_width)
    d_hidden = back_product(upstream, down_full)
    grad_down = outer_sum(hidden, upstream)
    d_gate = gate_pull(d_hidden * up_in)[0].astype(jnp.bfloat16)
    d_up = (d_hidden * gate_act).astype(jnp.bfloat16)
    grad_mlp = jnp.stack([outer_sum(normed_mid, d_gate), outer_sum(normed_mid, d_up)])
    d_mid = lax.psum(
        (back_product(d_gate, mlp_full[0]) + back_product(d_up, mlp_full[1])).astype(jnp.bfloat16),
        "tensor",
    ).astype(jnp.float32)
    d_mid_in, grad_gain_mid = normalize_back(d_mid, unit_mid, scale_mid, gain_rows[1])
    d_after = upstream.astype(jnp.float32) + d_mid_in
    d_after_low = d_after.astype(jnp.bfloat16)
    d_mixed = back_product(d_after_low, out_full).reshape(row_count, span_len, lru_width)
    grad_out = outer_sum(mixed_low, d_after_low)
    d_states = d_mixed * branch
    d_branch = branch_pull((d_mixed * states).reshape(token_count, lru_width))[0].astype(
        jnp.bfloat16
    )
    next_decay = jnp.concatenate(
        [carried[:, 1:], jnp.ones((row_count, 1, lru_width), jnp.float32)], axis=1
    )
    tail_decay, local_grads = lax.associative_scan(
        linear_step, (next_decay, d_states), axis=1, reverse=True
    )
    own_decay = carried[:, 0] * tail_decay[:, 0]
    own_grad = carried[:, 0] * local_grads[:, 0]
    after_decay, after_grad = entering_2((own_decay, own_grad), "seq", linear_step, identity, True)
    state_grads = local_grads + tail_decay * after_grad[:, None, :]
    d_carried = state_grads * previous
    d_root = state_grads * input_gate * conv_out
    open_root = (headroom > root_floor).astype(jnp.float32)
    d_decay = d_carried * keep_step - d_root * decay_now / input_root * open_root
    d_log = d_decay * decay_now
    d_gate_pre = jnp.stack(
        [
            d_log * (-rate_scale * softened) * decay_gate * (1.0 - decay_gate),
            state_grads * input_root * conv_out * input_gate * (1.0 - input_gate),
        ]
    )
    grad_decay = jnp.sum(d_log * (-rate_scale * decay_gate), axis=(0, 1)) * jax.nn.sigmoid(
        decay_float
    )
    grad_gate_bias = jnp.sum(d_gate_pre, axis=(1, 2))
    d_gate_low = d_gate_pre.astype(jnp.bfloat16).reshape(2, token_count, head_count, block_size)
    grad_blocks = jnp.einsum(
        "thi,gthj->ghij", grouped, d_gate_low, preferred_element_type=jnp.float32
    )
    through_gates = jnp.einsum(
        "gthj,ghij->thi", d_gate_low, gate_blocks, preferred_element_type=jnp.float32
    )
    d_conv = state_grads * input_root * input_gate + through_gates.reshape(
        row_count, span_len, lru_width
    )
    grad_conv_bias = jnp.sum(d_conv, axis=(0, 1))
    tap_grads = []
    d_extended = jnp.zeros((row_count, span_len + rim_len, lru_width), jnp.float32)
    for tap_index in range(CONV):
        tap_grads.append(
            jnp.sum(
                d_conv * extended[:, tap_index : tap_index + span_len] * same_docs[tap_index],
                axis=(0, 1),
            )
        )
        d_extended = d_extended + jnp.pad(
            d_conv * conv_taps[tap_index] * same_docs[tap_index],
            ((0, 0), (tap_index, rim_len - tap_index), (0, 0)),
        )
    grad_conv_weight = jnp.stack(tap_grads)
    returned = from_behind(d_extended[:, :rim_len], "seq", -1)
    d_input = d_extended[:, rim_len:] + jnp.pad(returned, ((0, 0), (span_len - rim_len, 0), (0, 0)))
    d_input_low = d_input.astype(jnp.bfloat16).reshape(token_count, lru_width)
    grad_mix = jnp.stack([outer_sum(normed_in, d_branch), outer_sum(normed_in, d_input_low)])
    d_first = lax.psum(
        (back_product(d_branch, mix_full[0]) + back_product(d_input_low, mix_full[1])).astype(
            jnp.bfloat16
        ),
        "tensor",
    ).astype(jnp.float32)
    d_first_in, grad_gain_in = normalize_back(d_first, unit_in, scale_in, gain_rows[0])
    grad_tokens = (
        (d_after + d_first_in).astype(jnp.bfloat16).reshape(row_count, span_len, model_width)
    )
    grad_mix, grad_out, grad_mlp, grad_down = (
        lax.psum_scatter(
            grad_mix.astype(jnp.bfloat16), ("seq", "dp"), scatter_dimension=1, tiled=True
        ).astype(jnp.float32),
        lax.psum_scatter(
            grad_out.astype(jnp.bfloat16), ("seq", "dp"), scatter_dimension=1, tiled=True
        ).astype(jnp.float32),
        lax.psum_scatter(
            grad_mlp.astype(jnp.bfloat16), ("seq", "dp"), scatter_dimension=1, tiled=True
        ).astype(jnp.float32),
        lax.psum_scatter(
            grad_down.astype(jnp.bfloat16), ("seq", "dp"), scatter_dimension=1, tiled=True
        ).astype(jnp.float32),
    )
    small_sums = (
        lax.psum(
            jnp.stack([grad_gain_in, grad_gain_mid]).astype(jnp.bfloat16), ("seq", "dp")
        ).astype(jnp.float32),
        lax.psum(grad_conv_weight.astype(jnp.bfloat16), ("seq", "dp")).astype(jnp.float32),
        lax.psum(grad_conv_bias.astype(jnp.bfloat16), ("seq", "dp")).astype(jnp.float32),
        lax.psum(grad_blocks.astype(jnp.bfloat16), ("seq", "dp")).astype(jnp.float32),
        lax.psum(grad_gate_bias.astype(jnp.bfloat16), ("seq", "dp")).astype(jnp.float32),
        lax.psum(grad_decay.astype(jnp.bfloat16), ("seq", "dp")).astype(jnp.float32),
    )
    return (
        block_out,
        states,
        grad_tokens,
        small_sums[0],
        grad_mix,
        grad_out,
        small_sums[1],
        small_sums[2],
        small_sums[3],
        small_sums[4],
        small_sums[5],
        grad_mlp,
        grad_down,
    )


def solution(mesh):
    in_specs = (
        P("dp", "seq", None),
        P("dp", "tensor"),
        P("dp", None, "tensor"),
        P("dp"),
        P("dp"),
        P(),
        P(None, ("seq", "dp"), "tensor"),
        P("tensor", ("seq", "dp")),
        P(None, "tensor"),
        P("tensor"),
        P(None, "tensor", None, None),
        P(None, "tensor"),
        P("tensor"),
        P(None, ("seq", "dp"), "tensor"),
        P("tensor", ("seq", "dp")),
        P("dp", "seq", None),
    )
    out_specs = (
        P("dp", "seq", None),
        P("dp", "seq", "tensor"),
        P("dp", "seq", None),
        P(),
        P(None, ("seq", "dp"), "tensor"),
        P("tensor", ("seq", "dp")),
        P(None, "tensor"),
        P("tensor"),
        P(None, "tensor", None, None),
        P(None, "tensor"),
        P("tensor"),
        P(None, ("seq", "dp"), "tensor"),
        P("tensor", ("seq", "dp")),
    )
    return jax.shard_map(
        per_device, mesh=mesh, in_specs=in_specs, out_specs=out_specs, check_vma=False
    )
```

profile of v0, /device:TPU:1, one launch (start us, length us, event | category | flops | bytes accessed | tf_op | source)
XLA Modules:
  0.0 1378.1 jit_solution(1529056429788935038)
XLA Ops:
  14.6 47.0 %all-gather.9.cloned.1.call-done = bf16[2,2048,640]{2,1,0:T(8,128)(2,1)} async-done(((bf16[2,64,640]{2,1,0:T(8,128)(2,1)}), bf16[2,2048,640]{2,1,0:T(8,128)(2,1)}) %all-gather.9.cloned.1.call-update) | async-done | bytes 5242896 | tf_op jit(solution)/shard_map/all_gather | solution.py:97
  79.0 4.9 copy.359
  84.0 5.5 reshape.248
  244.2 12.1 all-gather
  268.9 13.2 all-gather.1
  286.8 5.1 convolution_convert_fusion.6
  293.1 56.4 %all-reduce.70.cloned.1.call-done = bf16[512,2048]{1,0:T(8,128)(2,1)} async-done(((bf16[512,2048]{1,0:T(8,128)(2,1)}), bf16[512,2048]{1,0:T(8,128)(2,1)}) %all-reduce.70.cloned.1.call-update) | async-done | bytes 2097168 | tf_op jit(solution)/shard_map/psum | solution.py:169
  354.4 60.7 %all-gather.13.cloned.1.call-done = bf16[2,2048,1536]{2,1,0:T(8,128)(2,1)} async-done(((bf16[2,64,1536]{2,1,0:T(8,128)(2,1)}), bf16[2,2048,1536]{2,1,0:T(8,128)(2,1)}) %all-gather.13.cloned.1.call-update) | async-done | bytes 12582928 | tf_op jit(solution)/shard_map/all_gather | solution.py:99
  415.1 8.6 fusion.3
  423.7 5.1 fusion.5
  428.8 37.5 %all-gather.15.cloned.1.call-done = bf16[1536,2048]{0,1:T(8,128)(2,1)} async-done(((bf16[1536,64]{0,1:T(8,128)(2,1)}), bf16[1536,2048]{0,1:T(8,128)(2,1)}) %all-gather.15.cloned.1.call-update) | async-done | bytes 6291472 | tf_op jit(solution)/shard_map/all_gather | solution.py:100
  466.3 11.9 multiply_convert_fusion.1
  478.1 7.0 fusion.2
  511.3 8.2 convolution_convert_fusion.5
  519.5 27.6 %all-reduce.72.cloned.1.call-done = bf16[512,2048]{1,0:T(8,128)(2,1)} async-done(((bf16[512,2048]{1,0:T(8,128)(2,1)}), bf16[512,2048]{1,0:T(8,128)(2,1)}) %all-reduce.72.cloned.1.call-update) | async-done | bytes 2097168 | tf_op jit(solution)/shard_map/psum | solution.py:194
  716.4 10.7 rev.8
  727.1 10.7 rev.9
  737.8 13.5 all-gather.2
  751.6 12.8 all-gather.3
  764.9 5.8 multiply_reduce_fusion.1
  806.5 5.7 convolution_convert_fusion.3
  812.3 8.1 convolution_convert_fusion
  821.5 4.9 fusion.34
  826.4 68.6 %all-reduce.76.cloned.1.call-done = (bf16[512,2048]{1,0:T(8,128)(2,1)}, bf16[512,2048]{1,0:T(8,128)(2,1)}) async-done(((bf16[512,2048]{1,0:T(8,128)(2,1)}, bf16[512,2048]{1,0:T(8,128)(2,1)}), (bf16[512,2048]{1,0:T(8,128)(2,1)}, bf16[512,2048]{1,0:T(8,128)(2,1)})) %all-reduce.76.cloned.1.call-update) | async-done | bytes 4194320 | tf_op jit(solution)/shard_map/psum | solution.py:178
  898.1 6.3 fusion.21
  910.8 5.2 fusion.1
  919.7 5.6 pad_maximum_fusion
  927.3 74.9 %all-reduce.74.cloned.1.call-done = bf16[2,4,160,160]{2,3,0,1:T(8,128)(2,1)} async-done(((bf16[2,4,160,160]{2,3,0,1:T(8,128)(2,1)}), bf16[2,4,160,160]{2,3,0,1:T(8,128)(2,1)}) %all-reduce.74.cloned.1.call-update) | async-done | bytes 409616 | tf_op jit(solution)/shard_map/psum | solution.py:291
  1004.6 79.0 %reduce-scatter.7.cloned.1.call-done = bf16[640,64]{0,1:T(8,128)(2,1)} async-done(((bf16[640,2048]{0,1:T(8,128)(2,1)}), bf16[640,64]{0,1:T(8,128)(2,1)}) %reduce-scatter.7.cloned.1.call-update) | async-done | bytes 81936 | tf_op jit(solution)/shard_map/reduce_scatter | solution.py:275
  1085.3 122.7 %all-reduce.63 = (bf16[2,2048]{1,0:T(2,128)(2,1)S(1)}, bf16[4,640]{1,0:T(4,128)(2,1)S(1)}, bf16[640]{0:T(1024)(128)(2,1)S(1)}, bf16[2,640]{1,0:T(2,128)(2,1)S(1)}, bf16[640]{0:T(1024)(128)(2,1)S(1)}) all-reduce(bf16[2,2048]{1,0:T(2,128)(2,1)S(1)} %pad_maximum_fusion.29, ...), channel_id=1, replica_groups=mesh['seq'=8,'dp'=4,'tensor'=4] {'seq','dp'}, use_global_device_ids=true, to_apply=%region_14.15 | all-reduce | flops 9216 | bytes 36864 | tf_op jit(solution)/shard_map/psum | solution.py:286
  1212.7 48.5 %reduce-scatter.5.cloned.1.call-done = bf16[2,64,640]{2,1,0:T(8,128)(2,1)} async-done(((bf16[2,2048,640]{2,1,0:T(8,128)(2,1)}), bf16[2,64,640]{2,1,0:T(8,128)(2,1)}) %reduce-scatter.5.cloned.1.call-update) | async-done | bytes 163856 | tf_op jit(solution)/shard_map/reduce_scatter | solution.py:272
  1262.9 106.3 %reduce-scatter.9.cloned.1.call-done = bf16[2,64,1536]{2,1,0:T(8,128)(2,1)} async-done(((bf16[2,2048,1536]{2,1,0:T(8,128)(2,1)}), bf16[2,64,1536]{2,1,0:T(8,128)(2,1)}) %reduce-scatter.9.cloned.1.call-update) | async-done | bytes 393232 | tf_op jit(solution)/shard_map/reduce_scatter | solution.py:278
  (575 shorter events, 462.2 us)
Async XLA Ops:
  7.3 54.3 %all-gather.9.cloned.1.call-start = ((), (), s32[]{:S(2)}) async-start(), calls=%async_computation.4 | async-start | bytes 5406720 | tf_op jit(solution)/shard_map/all_gather | solution.py:97
  8.0 278.8 %all-gather.11.cloned.1.call-start = ((), (), s32[]{:S(2)}) async-start(), calls=%async_computation.5 | async-start | bytes 2703360 | tf_op jit(solution)/shard_map/all_gather | solution.py:98
  8.7 340.8 %all-reduce.70.cloned.1.call-start = ((), (), s32[]{:S(2)}) async-start(), calls=%async_computation.6 | async-start | bytes 4194304 | tf_op jit(solution)/shard_map/psum | solution.py:169
  12.3 60.3 %copy-start.95 = (f32[4]{0:T(128)}, f32[4]{0:T(128)S(1)}, u32[]{:S(2)}) copy-start(f32[4]{0:T(128)S(1)} %subtract_convert_fusion) | copy-start | bytes 52
  12.5 60.2 %copy-start.76 = (f32[4,128]{1,0:T(4,128)}, f32[4,128]{1,0:T(4,128)S(1)}, u32[]{:S(2)}) copy-start(f32[4,128]{1,0:T(4,128)S(1)} %get-tuple-element.388) | copy-start | bytes 6148
  12.5 60.3 %copy-start.78 = (f32[4,128]{1,0:T(4,128)}, f32[4,128]{1,0:T(4,128)S(1)}, u32[]{:S(2)}) copy-start(f32[4,128]{1,0:T(4,128)S(1)} %get-tuple-element.389) | copy-start | bytes 6148
  12.5 60.3 %copy-start.80 = (f32[4,128]{1,0:T(4,128)}, f32[4,128]{1,0:T(4,128)S(1)}, u32[]{:S(2)}) copy-start(f32[4,128]{1,0:T(4,128)S(1)} %get-tuple-element.390) | copy-start | bytes 6148
  12.5 60.3 %copy-start.82 = (f32[4,128]{1,0:T(4,128)}, f32[4,128]{1,0:T(4,128)S(1)}, u32[]{:S(2)}) copy-start(f32[4,128]{1,0:T(4,128)S(1)} %get-tuple-element.391) | copy-start | bytes 6148
  12.6 60.2 %copy-start.68 = (f32[640]{0:T(1024)}, f32[640]{0:T(1024)S(1)}, u32[]{:S(2)}) copy-start(f32[640]{0:T(1024)S(1)} %get-tuple-element.261) | copy-start | bytes 7684
  12.6 60.2 %copy-start.70 = (f32[640]{0:T(1024)}, f32[640]{0:T(1024)S(1)}, u32[]{:S(2)}) copy-start(f32[640]{0:T(1024)S(1)} %get-tuple-element.262) | copy-start | bytes 7684
  12.6 60.2 %copy-start.72 = (f32[640]{0:T(1024)}, f32[640]{0:T(1024)S(1)}, u32[]{:S(2)}) copy-start(f32[640]{0:T(1024)S(1)} %get-tuple-element.263) | copy-start | bytes 7684
  12.6 60.2 %copy-start.74 = (f32[640]{0:T(1024)}, f32[640]{0:T(1024)S(1)}, u32[]{:S(2)}) copy-start(f32[640]{0:T(1024)S(1)} %get-tuple-element.264) | copy-start | bytes 7684
  12.7 79.2 %copy-start.85 = (f32[4,128]{1,0:T(4,128)}, f32[4,128]{1,0:T(4,128)S(1)}, u32[]{:S(2)}) copy-start(f32[4,128]{1,0:T(4,128)S(1)} %compare_convert_fusion) | copy-start | bytes 6148
  66.0 6.6 collective-permute-start
  243.2 19.3 %copy-start.28 = (f32[4,63,640]{2,1,0:T(8,128)S(1)}, f32[4,63,640]{2,1,0:T(8,128)}, u32[]{:S(2)}) copy-start(f32[4,63,640]{2,1,0:T(8,128)} %get-tuple-element.328) | copy-start | bytes 1935364
  263.4 19.0 %copy-start.89 = (f32[4,640]{1,0:T(4,128)S(1)}, f32[4,640]{1,0:T(4,128)}, u32[]{:S(2)}) copy-start(f32[4,640]{1,0:T(4,128)} %param.21) | copy-start | bytes 30724
  263.4 19.0 %copy-start.96 = (f32[4]{0:T(128)S(1)}, f32[4]{0:T(128)}, u32[]{:S(2)}) copy-start(f32[4]{0:T(128)} %copy-done.95) | copy-start | bytes 52
  291.9 123.2 %all-gather.13.cloned.1.call-start = ((), (), s32[]{:S(2)}) async-start(), calls=%async_computation.7 | async-start | bytes 12976128 | tf_op jit(solution)/shard_map/all_gather | solution.py:99
  292.5 173.7 %all-gather.15.cloned.1.call-start = ((), (), s32[]{:S(2)}) async-start(), calls=%async_computation.8 | async-start | bytes 6488064 | tf_op jit(solution)/shard_map/all_gather | solution.py:100
  293.1 254.0 %all-reduce.72.cloned.1.call-start = ((), (), s32[]{:S(2)}) async-start(), calls=%async_computation.9 | async-start | bytes 4194304 | tf_op jit(solution)/shard_map/psum | solution.py:194
  466.3 18.9 %slice-start.1 = ((s8[12582912]{0:T(1024)(128)(4,1)}), s8[4194304]{0:T(1024)(128)(4,1)S(1)}, s32[]{:S(2)}) async-start(s8[12582912]{0:T(1024)(128)(4,1)} %bitcast.280), calls=%async_computation.17 | async-start | bytes 8388608
  489.8 405.1 %all-reduce.76.cloned.1.call-start = ((), (), s32[]{:S(2)}) async-start(), calls=%async_computation.15 | async-start | bytes 8388608 | tf_op jit(solution)/shard_map/psum | solution.py:178
  727.1 37.8 %copy-start.55 = (f32[4,1,640]{2,1,0:T(1,128)S(1)}, f32[4,1,640]{2,1,0:T(1,128)}, u32[]{:S(2)}) copy-start(f32[4,1,640]{2,1,0:T(1,128)} %copy.343) | copy-start | bytes 30724
  727.1 37.8 %copy-start.86 = (f32[4,128]{1,0:T(4,128)S(1)}, f32[4,128]{1,0:T(4,128)}, u32[]{:S(2)}) copy-start(f32[4,128]{1,0:T(4,128)} %copy-done.85) | copy-start | bytes 6148
  791.7 6.7 collective-permute-start.1
  802.7 199.5 %all-reduce.74.cloned.1.call-start = ((), (), s32[]{:S(2)}) async-start(), calls=%async_computation.12 | async-start | bytes 1310720 | tf_op jit(solution)/shard_map/psum | solution.py:291
  806.4 277.2 %reduce-scatter.7.cloned.1.call-start = ((), (), s32[]{:S(2)}) async-start(), calls=%async_computation.11 | async-start | bytes 2703360 | tf_op jit(solution)/shard_map/reduce_scatter | solution.py:275
  812.2 398.8 %reduce-scatter.11.cloned.1.call-start = ((), (), s32[]{:S(2)}) async-start(), calls=%async_computation.14 | async-start | bytes 6488064 | tf_op jit(solution)/shard_map/reduce_scatter | solution.py:281
  820.4 74.6 %copy-start.54 = (f32[1,2048]{1,0:T(1,128)S(1)}, f32[1,2048]{1,0:T(1,128)}, u32[]{:S(2)}) copy-start(f32[1,2048]{1,0:T(1,128)} %copy-done.53) | copy-start | bytes 24580
  820.4 74.6 %copy-start.84 = (f32[512]{0:T(512)S(1)}, f32[512]{0:T(512)}, u32[]{:S(2)}) copy-start(f32[512]{0:T(512)} %get-tuple-element.386) | copy-start | bytes 6148
  820.4 440.8 %reduce-scatter.5.cloned.1.call-start = ((), (), s32[]{:S(2)}) async-start(), calls=%async_computation.10 | async-start | bytes 5406720 | tf_op jit(solution)/shard_map/reduce_scatter | solution.py:272
  909.2 459.9 %reduce-scatter.9.cloned.1.call-start = ((), (), s32[]{:S(2)}) async-start(), calls=%async_computation.13 | async-start | bytes 12976128 | tf_op jit(solution)/shard_map/reduce_scatter | solution.py:278
  (92 other events, 435.5 us)
Sparse Core Ops, SparseCore 0:
  10.4 51.1 all-gather.8
  63.9 43.8 all-gather.10
  292.1 57.4 all-reduce.69
  351.9 63.1 all-gather.12
  417.5 48.6 all-gather.14
  489.9 57.1 all-reduce.71
  802.8 92.1 all-reduce.75
  899.1 102.9 all-reduce.73
  1006.2 77.4 reduce-scatter.6
  1087.2 85.7 reduce-scatter.10
  1177.2 83.9 reduce-scatter.4
  1264.9 104.1 reduce-scatter.8
where the time goes:
time: 1390 us; the launch traced here: 1380 us
  waiting for transfers between devices  609 us (44%)
  local copies, waits for them, and re-layouts  317 us (23%)
  blocking collectives  174 us (13%)
  other arithmetic  153 us (11%)
  matrix products  102 us (7%)
  between operations  16 us (1%)
    psum x1, blocking collectives, per_device(): lax.psum(jnp.stack([grad_gain_in, grad_gain_mid]).astype(jnp.bfloat16), (...  123 us
    reduce_scatter x1, waiting for transfers between devices, per_device(): lax.psum_scatter(grad_mlp.astype(jnp.bfloat16), ('seq', 'dp'), scatter_di...  106 us
    slice x49, local copies, waits for them, and re-layouts, per_device(): lax.associative_scan(linear_step, (next_decay, d_states), axis=1, reverse...  86.6 us
    reduce_scatter x1, waiting for transfers between devices, per_device(): lax.psum_scatter(grad_out.astype(jnp.bfloat16), ('seq', 'dp'), scatter_di...  79 us
    psum x1, waiting for transfers between devices, per_device(): lax.psum(grad_blocks.astype(jnp.bfloat16), ('seq', 'dp'))  74.9 us
    slice x44, local copies, waits for them, and re-layouts, per_device(): lax.associative_scan(linear_step, (carried, fed_value), axis=1)  71.9 us
    psum x1, waiting for transfers between devices, per_device(): lax.psum(matmul(hidden, down_full).astype(jnp.bfloat16), 'tensor')  68.6 us
    all_gather x1, waiting for transfers between devices, per_device(): lax.all_gather(mlp_in, ('seq', 'dp'), axis=1, tiled=True)  60.7 us
  transfers between devices with their start and end apart: 14, of which 10 were waited for; matrix products, arithmetic and copies ran while one was open for 23% of the time, Pallas kernels for 0%

commit v1 on v0

v1 whole, which is shorter than its diff:
```python
import functools

import jax
import jax.numpy as jnp
from jax import lax
from jax.experimental import pallas as pl
from jax.experimental.pallas import tpu as pltpu
from jax.sharding import PartitionSpec as P

MESH = pl.DeviceIdType.MESH
F32 = jnp.float32
BF16 = jnp.bfloat16
VMEM_BYTES = 60 * 2**20

CONV = 4
ROWS = 4
SPAN = 128
TOKENS = ROWS * SPAN
WIDTH = 2048
CHAN = 640
HEADS = 4
BLK = 160
MLP = 1536
MIX_COLS = 3 * CHAN
MLP_COLS = 3 * MLP
LANES = 128
GROUPS = CHAN // LANES
PAD = 8

epsilon = 1e-06
root_floor = 0.001
rate_scale = 8.0


class Place:
    def __init__(self):
        self.s = lax.axis_index("seq")
        self.z = lax.axis_index("dp")
        self.y = lax.axis_index("tensor")
        self.x, self.c = lax.div(self.s, 2), lax.rem(self.s, 2)
        x, c, z, y = self.x, self.c, self.z, self.y
        self.xr, self.xl = lax.rem(x + 1, 4), lax.rem(x + 3, 4)
        self.zr, self.zl = lax.rem(z + 1, 4), lax.rem(z + 3, 4)
        self.yr, self.yl, self.y2 = lax.rem(y + 1, 4), lax.rem(y + 3, 4), lax.rem(y + 2, 4)
        self.XR, self.XL = {"seq": self.xr * 2 + c}, {"seq": self.xl * 2 + c}
        self.ZR, self.ZL = {"dp": self.zr}, {"dp": self.zl}
        self.YR, self.YL = {"tensor": self.yr}, {"tensor": self.yl}
        self.SIB = {"seq": x * 2 + 1 - c}

    def seq_at(self, distance):
        return {"seq": lax.rem(self.s + distance + 8, 8)}


def greet(devices):
    barrier = pltpu.get_barrier_semaphore()
    for device in devices:
        pl.semaphore_signal(barrier, inc=1, device_id=device, device_id_type=MESH)
    pl.semaphore_wait(barrier, len(devices))


class Links:
    def __init__(self, send, recv):
        self.send, self.recv = send, recv
        self.count = 0
        self.started = []

    def go(self, src, dst, device):
        k = self.count
        self.count += 1
        copy = pltpu.make_async_remote_copy(
            src_ref=src,
            dst_ref=dst,
            send_sem=self.send.at[k],
            recv_sem=self.recv.at[k],
            device_id=device,
            device_id_type=MESH,
        )
        copy.start()
        self.started.append(copy)
        return k

    def arrived(self, view, k, device):
        pltpu.make_async_remote_copy(
            src_ref=view,
            dst_ref=view,
            send_sem=self.send.at[k],
            recv_sem=self.recv.at[k],
            device_id=device,
            device_id_type=MESH,
        ).wait_recv()

    def drain(self):
        for copy in self.started:
            copy.wait_send()
        self.started = []


class Gather:
    def __init__(self, links, place, out):
        self.links, self.p, self.out = links, place, out
        self.to_sibling = []

    def _pass_on(self, view_of):
        k = self.links.go(view_of(self.p.c), view_of(self.p.c), self.p.SIB)
        self.to_sibling.append((view_of, k))

    def _ring(self, blk, i, right, left, base):
        links, p = self.links, self.p
        c = p.c
        ir, il, i2 = lax.rem(i + 1, 4), lax.rem(i + 3, 4), lax.rem(i + 2, 4)
        a, b = pl.ds(base, 16), pl.ds(base + 16, 16)
        k0 = links.go(blk(c, i, a), blk(c, i, a), right)
        k1 = links.go(blk(c, i, b), blk(c, i, b), left)
        k2 = links.go(blk(c, i, b), blk(c, i, b), right)
        k3 = links.go(blk(c, i, a), blk(c, i, a), left)

        def middle():
            links.arrived(blk(c, il, a), k0, left)
            k4 = links.go(blk(c, il, a), blk(c, il, a), right)
            links.arrived(blk(c, ir, b), k1, right)
            k5 = links.go(blk(c, ir, b), blk(c, ir, b), left)
            self._pass_on(lambda cc: blk(cc, il, a))
            self._pass_on(lambda cc: blk(cc, ir, b))
            return k4, k5

        def finish(later):
            for view, k, source in (
                (lambda cc: blk(cc, il, b), k2, left),
                (lambda cc: blk(cc, ir, a), k3, right),
                (lambda cc: blk(cc, i2, a), later[0], left),
                (lambda cc: blk(cc, i2, b), later[1], right),
            ):
                links.arrived(view(c), k, source)
                self._pass_on(view)

        return middle, finish

    def first(self):
        p, out = self.p, self.out
        self.x_ring = self._ring(lambda cc, j, r: out.at[j, cc, p.z, r], p.x, p.XR, p.XL, 0)
        self.z_ring = self._ring(lambda cc, j, r: out.at[p.x, cc, j, r], p.z, p.ZR, p.ZL, 32)
        self._pass_on(lambda cc: out.at[p.x, cc, p.z])

    def second(self):
        p, out = self.p, self.out
        self.x_ring = self._ring(lambda cc, j, r: out.at[:, cc, j, r], p.z, p.ZR, p.ZL, 0)
        self.z_ring = self._ring(lambda cc, j, r: out.at[j, cc, :, r], p.x, p.XR, p.XL, 32)

    def middle(self):
        self.later = (self.x_ring[0](), self.z_ring[0]())

    def finish(self):
        self.x_ring[1](self.later[0])
        self.z_ring[1](self.later[1])

    def settle(self):
        for view_of, k in self.to_sibling:
            self.links.arrived(view_of(1 - self.p.c), k, self.p.SIB)


CA, CB = pl.ds(0, WIDTH // 2), pl.ds(WIDTH // 2, WIDTH // 2)
HALF = WIDTH // 2


class Reduce:
    def __init__(self, links, place, part, far, near):
        self.links, self.p, self.part, self.far, self.near = links, place, part, far, near

    def send_far(self):
        p, part = self.p, self.part
        self.k0 = self.links.go(part.at[p.y2, :, CA], self.far.at[0], p.YR)
        self.k1 = self.links.go(part.at[p.y2, :, CB], self.far.at[1], p.YL)

    def send_near(self):
        p, part, near = self.p, self.part, self.near
        self.k2 = self.links.go(part.at[p.yr, :, CB], near.at[0, :, CB], p.YR)
        self.k3 = self.links.go(part.at[p.yl, :, CA], near.at[1, :, CA], p.YL)

    def merge(self):
        p, part, near, far = self.p, self.part, self.near, self.far
        self.links.arrived(far.at[0], self.k0, p.YL)
        far[0] = (far[0].astype(F32) + part[p.yr, :, 0:HALF].astype(F32)).astype(BF16)
        self.k4 = self.links.go(far.at[0], near.at[0, :, CA], p.YR)
        self.links.arrived(far.at[1], self.k1, p.YR)
        far[1] = (far[1].astype(F32) + part[p.yl, :, HALF:WIDTH].astype(F32)).astype(BF16)
        self.k5 = self.links.go(far.at[1], near.at[1, :, CB], p.YL)

    def settle(self):
        p, near = self.p, self.near
        self.links.arrived(near.at[0, :, CB], self.k2, p.YL)
        self.links.arrived(near.at[1, :, CA], self.k3, p.YR)
        self.links.arrived(near.at[0, :, CA], self.k4, p.YL)
        self.links.arrived(near.at[1, :, CB], self.k5, p.YR)


class Spread:
    def __init__(self, links, place, out):
        self.links, self.p, self.out = links, place, out

    def start(self):
        go, out, y, p = self.links.go, self.out, self.p.y, self.p
        self.k0 = go(out.at[y, :, CA], out.at[y, :, CA], p.YR)
        self.k1 = go(out.at[y, :, CB], out.at[y, :, CB], p.YL)
        self.k2 = go(out.at[y, :, CB], out.at[y, :, CB], p.YR)
        self.k3 = go(out.at[y, :, CA], out.at[y, :, CA], p.YL)

    def forward(self):
        go, out, p, arrived = self.links.go, self.out, self.p, self.links.arrived
        arrived(out.at[p.yl, :, CA], self.k0, p.YL)
        self.k4 = go(out.at[p.yl, :, CA], out.at[p.yl, :, CA], p.YR)
        arrived(out.at[p.yr, :, CB], self.k1, p.YR)
        self.k5 = go(out.at[p.yr, :, CB], out.at[p.yr, :, CB], p.YL)

    def near(self):
        out, p, arrived = self.out, self.p, self.links.arrived
        arrived(out.at[p.yl, :, CB], self.k2, p.YL)
        arrived(out.at[p.yr, :, CA], self.k3, p.YR)

    def far(self):
        out, p, arrived = self.out, self.p, self.links.arrived
        arrived(out.at[p.y2, :, CA], self.k4, p.YL)
        arrived(out.at[p.y2, :, CB], self.k5, p.YR)


def dot(a, b):
    return jnp.dot(a, b, preferred_element_type=F32)


def dot_nt(a, b):
    return lax.dot_general(a, b, (((1,), (1,)), ((), ())), preferred_element_type=F32)


def dot_tn(a, b):
    return lax.dot_general(a, b, (((0,), (0,)), ((), ())), preferred_element_type=F32)


GELU_C = 0.7978845608028654
GELU_A = 0.044715


def gelu(v):
    return 0.5 * v * (1.0 + jnp.tanh(GELU_C * (v + GELU_A * v * v * v)))


def gelu_pair(v):
    t = jnp.tanh(GELU_C * (v + GELU_A * v * v * v))
    value = 0.5 * v * (1.0 + t)
    slope = 0.5 * (1.0 + t) + 0.5 * v * (1.0 - t * t) * (GELU_C * (1.0 + 3.0 * GELU_A * v * v))
    return value, slope


def tile_scan(a, b, reverse):
    row = lax.broadcasted_iota(jnp.int32, a.shape, 1)
    for step in (1, 2, 4):
        if reverse:
            shift, valid = 8 - step, row < 8 - step
        else:
            shift, valid = step, row >= step
        a_near, b_near = pltpu.roll(a, shift, 1), pltpu.roll(b, shift, 1)
        b = jnp.where(valid, a * b_near + b, b)
        a = jnp.where(valid, a * a_near, a)
    return a, b


def row_scan(a, b, reverse):
    tiles = SPAN // 8
    a, b = tile_scan(a.reshape(tiles, 8, LANES), b.reshape(tiles, 8, LANES), reverse)
    edge = 0 if reverse else 7
    order = range(tiles - 1, -1, -1) if reverse else range(tiles)
    out_a, out_b = [None] * tiles, [None] * tiles
    carry_a = carry_b = None
    for k in order:
        ak, bk = a[k], b[k]
        if carry_a is not None:
            bk = ak * carry_b + bk
            ak = ak * carry_a
        out_a[k], out_b[k] = ak, bk
        carry_a, carry_b = ak[edge : edge + 1], bk[edge : edge + 1]
    return jnp.concatenate(out_a, axis=0), jnp.concatenate(out_b, axis=0), carry_a, carry_b


def put_pair(ref, at, r, first, second):
    row = lax.broadcasted_iota(jnp.int32, (8, LANES), 0)
    ref[:, at] = jnp.where(row == r, first, jnp.where(row == ROWS + r, second, ref[:, at]))


def take_row(ref, at, r):
    row = lax.broadcasted_iota(jnp.int32, (8, LANES), 0)
    return jnp.sum(jnp.where(row == r, ref[:, at], 0.0), axis=0, keepdims=True)


def mix_forward_kernel(
    tokens,
    mix_shard,
    mlp_shard,
    init_state,
    conv_start,
    doc_start,
    gains,
    vectors,
    gate_w,
    mix_full_out,
    mlp_full,
    states_out,
    pre_out,
    ext_out,
    decay_out,
    input_out,
    conv_out,
    mixed_out,
    normed_in_out,
    entering_out,
    normed_mid,
    after_own,
    mix_full,
    normed_in,
    pre,
    ext,
    decay_g,
    input_g,
    conv_low,
    cum_a,
    loc_b,
    states,
    mixed,
    rim_send,
    rim_recv,
    totals,
    totals_in,
    entering,
    part,
    far,
    near,
    local,
    send,
    recv,
):
    p = Place()
    links = Links(send, recv)
    own_mix = pltpu.make_async_copy(mix_shard, mix_full.at[p.x, p.c, p.z], local.at[0])
    own_mlp = pltpu.make_async_copy(mlp_shard, mlp_full.at[p.x, p.c, p.z], local.at[1])
    own_mix.start()
    own_mlp.start()
    greet([p.seq_at(d) for d in range(1, 8)] + [p.ZR, p.ZL, p.YR, p.YL])
    own_mix.wait()
    mix_gather = Gather(links, p, mix_full)
    mix_gather.first()

    def norm_rows(first, last):
        def one(k, carry):
            at = pl.ds(pl.multiple_of(k * 32, 32), 32)
            stream = tokens[at, :].astype(F32)
            scale = lax.rsqrt(jnp.mean(stream * stream, axis=-1, keepdims=True) + epsilon)
            normed_in[at, :] = (stream * scale * gains[0:1, :]).astype(BF16)
            return carry

        lax.fori_loop(first, last, one, 0)

    norm_rows(0, 8)
    mix_gather.middle()
    mix_gather.finish()
    mix_gather.second()
    own_mlp.wait()
    norm_rows(8, 16)
    mix_gather.middle()
    mlp_gather = Gather(links, p, mlp_full)
    mlp_gather.first()
    mix_gather.finish()
    mix_gather.settle()
    saves = []

    def save(src, dst):
        copy = pltpu.make_async_copy(src, dst, local.at[2 + len(saves)])
        copy.start()
        saves.append(copy)

    save(mix_full, mix_full_out)
    save(normed_in, normed_in_out)

    def project(n, carry):
        at = pl.ds(pl.multiple_of(n * 256, 256), 256)
        pre[:, at] = dot(normed_in[...], mix_full[:, :, :, :, at].reshape(WIDTH, 256))
        return carry

    lax.fori_loop(0, 5, project, 0)
    mlp_gather.middle()
    mlp_gather.finish()
    mlp_gather.second()
    save(pre.at[:, pl.ds(0, CHAN)], pre_out)

    for r in range(ROWS):
        ext[r, PAD:, :] = pre[r * SPAN : (r + 1) * SPAN, CHAN : 2 * CHAN].astype(BF16).astype(F32)
        rim_send[r] = ext[r, SPAN : SPAN + PAD, :]
    k_rim = links.go(rim_send, rim_recv, p.seq_at(1))
    links.arrived(rim_recv, k_rim, p.seq_at(-1))
    at_start = p.s == 0
    for r in range(ROWS):
        ext[r, 0:PAD, :] = jnp.where(at_start, conv_start[r], rim_recv[r])
    offset = p.s * SPAN

    def conv_chunk(i, carry):
        r, g = lax.rem(i, ROWS), lax.div(i, ROWS)
        at = pl.ds(pl.multiple_of(g * LANES, LANES), LANES)
        place = offset + lax.broadcasted_iota(jnp.int32, (SPAN, LANES), 0)
        begin = doc_start[r]
        here = place >= begin
        total = jnp.zeros((SPAN, LANES), F32) + vectors[4:5, at]
        for k in range(CONV):
            value = ext[r, PAD - 3 + k : PAD - 3 + k + SPAN, at]
            same = (place - (3 - k) >= begin) == here
            total = total + vectors[k : k + 1, at] * jnp.where(same, value, 0.0)
        rows = pl.ds(pl.multiple_of(r * SPAN, SPAN), SPAN)
        conv_low[rows, at] = total.astype(BF16)
        return carry

    lax.fori_loop(0, ROWS * GROUPS, conv_chunk, 0)
    mlp_gather.middle()
    save(ext, ext_out)
    save(conv_low, conv_out)

    for j, target in ((0, decay_g), (1, input_g)):
        held = None
        for g in range(GROUPS):
            total = held
            if g < HEADS:
                product = dot(conv_low[:, g * LANES : g * LANES + 256], gate_w[j, g])
                total = product[:, :LANES] if held is None else held + product[:, :LANES]
                held = product[:, LANES:]
            target[:, g * LANES : (g + 1) * LANES] = total

    def gate_chunk(i, carry):
        r, g = lax.rem(i, ROWS), lax.div(i, ROWS)
        at = pl.ds(pl.multiple_of(g * LANES, LANES), LANES)
        rows = pl.ds(pl.multiple_of(r * SPAN, SPAN), SPAN)
        gate_d = jax.nn.sigmoid(decay_g[rows, at] + vectors[5:6, at])
        gate_i = jax.nn.sigmoid(input_g[rows, at] + vectors[6:7, at])
        decay_g[rows, at] = gate_d
        input_g[rows, at] = gate_i
        decay_now = jnp.exp(gate_d * vectors[7:8, at])
        root = jnp.sqrt(jnp.maximum(1.0 - decay_now * decay_now, root_floor))
        fed = root * gate_i * conv_low[rows, at].astype(F32)
        place = offset + lax.broadcasted_iota(jnp.int32, (SPAN, LANES), 0)
        carried = jnp.where(place == doc_start[r], 0.0, decay_now)
        a, b, last_a, last_b = row_scan(carried, fed, False)
        cum_a[rows, at] = a
        loc_b[rows, at] = b
        put_pair(totals, at, r, last_a, last_b)
        return carry

    totals[...] = jnp.zeros_like(totals)
    lax.fori_loop(0, ROWS * GROUPS, gate_chunk, 0)
    keys = [links.go(totals, totals_in.at[p.s], p.seq_at(d)) for d in range(1, 8)]
    save(decay_g, decay_out)
    save(input_g, input_out)
    mlp_gather.finish()
    state = init_state[...]
    for d in range(1, 8):
        links.arrived(totals_in.at[p.seq_at(-d)["seq"]], keys[d - 1], p.seq_at(-d))
    totals_in[p.s] = totals[...]
    for source in range(7):
        both = totals_in[source]
        state = jnp.where(source < p.s, both[0:ROWS] * state + both[ROWS:], state)
    entering[0:ROWS, :] = state
    entering[ROWS:, :] = jnp.zeros((8 - ROWS, CHAN), F32)

    def state_chunk(i, carry):
        r, g = lax.rem(i, ROWS), lax.div(i, ROWS)
        at = pl.ds(pl.multiple_of(g * LANES, LANES), LANES)
        rows = pl.ds(pl.multiple_of(r * SPAN, SPAN), SPAN)
        value = loc_b[rows, at] + cum_a[rows, at] * take_row(entering, at, r)
        states[rows, at] = value
        mixed[rows, at] = (value * gelu(pre[rows, at])).astype(BF16)
        return carry

    lax.fori_loop(0, ROWS * GROUPS, state_chunk, 0)
    save(states, states_out)
    save(mixed, mixed_out)
    save(entering, entering_out)

    def partial(row):
        left = mixed[pl.ds(pl.multiple_of(row * SPAN, SPAN), SPAN), :]

        def one(n, carry):
            weights = mix_full[lax.div(n, 2), lax.rem(n, 2), :, :, 2 * CHAN :].reshape(256, CHAN)
            part[row, :, pl.ds(pl.multiple_of(n * 256, 256), 256)] = dot_nt(left, weights).astype(BF16)
            return carry

        lax.fori_loop(0, 8, one, 0)

    reduce = Reduce(links, p, part, far, near)
    partial(p.y2)
    reduce.send_far()
    partial(p.yr)
    partial(p.yl)
    reduce.send_near()
    partial(p.y)
    reduce.merge()
    reduce.settle()

    def norm_mid(k, carry):
        at = pl.ds(pl.multiple_of(k * 16, 16), 16)
        total = part[p.y, at, :].astype(F32) + near[0, at, :].astype(F32) + near[1, at, :].astype(F32)
        row = pl.ds(pl.multiple_of(p.y * SPAN + k * 16, 16), 16)
        stream = tokens[row, :].astype(F32) + total
        scale = lax.rsqrt(jnp.mean(stream * stream, axis=-1, keepdims=True) + epsilon)
        after_own[at, :] = stream
        normed_mid[p.y, at, :] = (stream * scale * gains[1:2, :]).astype(BF16)
        return carry

    lax.fori_loop(0, SPAN // 16, norm_mid, 0)
    spread = Spread(links, p, normed_mid)
    spread.start()
    mlp_gather.settle()
    spread.forward()
    spread.near()
    spread.far()
    for copy in saves:
        copy.wait()
    links.drain()


def params(collective_id):
    return pltpu.CompilerParams(
        collective_id=collective_id, has_side_effects=True, vmem_limit_bytes=VMEM_BYTES
    )


def vmem():
    return pl.BlockSpec(memory_space=pltpu.VMEM)


def anyspace():
    return pl.BlockSpec(memory_space=pl.ANY)


def mix_forward(tokens, mix_shard, mlp_shard, init_state, conv_start, doc_start, gains, vectors, gate_w):
    shape = jax.ShapeDtypeStruct
    tc = (TOKENS, CHAN)
    ext_shape = (ROWS, PAD + SPAN, CHAN)
    outs = [
        shape((4, 2, 4, 64, MIX_COLS), BF16),
        shape((4, 2, 4, 64, MLP_COLS), BF16),
        shape(tc, F32),
        shape(tc, F32),
        shape(ext_shape, F32),
        shape(tc, F32),
        shape(tc, F32),
        shape(tc, BF16),
        shape(tc, BF16),
        shape((TOKENS, WIDTH), BF16),
        shape((8, CHAN), F32),
        shape((ROWS, SPAN, WIDTH), BF16),
        shape((SPAN, WIDTH), F32),
    ]
    scratch = [
        pltpu.VMEM((4, 2, 4, 64, MIX_COLS), BF16),
        pltpu.VMEM((TOKENS, WIDTH), BF16),
        pltpu.VMEM((TOKENS, 2 * CHAN), F32),
        pltpu.VMEM(ext_shape, F32),
        pltpu.VMEM(tc, F32),
        pltpu.VMEM(tc, F32),
        pltpu.VMEM(tc, BF16),
        pltpu.VMEM(tc, F32),
        pltpu.VMEM(tc, F32),
        pltpu.VMEM(tc, F32),
        pltpu.VMEM(tc, BF16),
        pltpu.VMEM((ROWS, PAD, CHAN), F32),
        pltpu.VMEM((ROWS, PAD, CHAN), F32),
        pltpu.VMEM((8, CHAN), F32),
        pltpu.VMEM((8, 8, CHAN), F32),
        pltpu.VMEM((8, CHAN), F32),
        pltpu.VMEM((ROWS, SPAN, WIDTH), BF16),
        pltpu.VMEM((2, SPAN, HALF), BF16),
        pltpu.VMEM((2, SPAN, WIDTH), BF16),
        pltpu.SemaphoreType.DMA((16,)),
        pltpu.SemaphoreType.DMA((128,)),
        pltpu.SemaphoreType.DMA((128,)),
    ]
    return pl.pallas_call(
        mix_forward_kernel,
        out_shape=outs,
        in_specs=[vmem(), anyspace(), anyspace(), vmem(), vmem(), pl.BlockSpec(memory_space=pltpu.SMEM)]
        + [vmem()] * 3,
        out_specs=[anyspace()] * 11 + [vmem()] * 2,
        scratch_shapes=scratch,
        compiler_params=params(0),
        name="mix_forward",
    )(tokens, mix_shard, mlp_shard, init_state, conv_start, doc_start, gains, vectors, gate_w)


def norm_back_rows(d_row, stream, gain_row):
    scale = lax.rsqrt(jnp.mean(stream * stream, axis=-1, keepdims=True) + epsilon)
    unit = stream * scale
    e = d_row * gain_row
    inner = jnp.mean(e * unit, axis=-1, keepdims=True)
    return scale * (e - unit * inner), d_row * unit


def own_sum(reduce, at):
    part, near = reduce.part, reduce.near
    return part[reduce.p.y, at, :].astype(F32) + near[0, at, :].astype(F32) + near[1, at, :].astype(F32)


def mid_back_kernel(
    part, after_own, upstream, gains, d_after_low, d_after_own, gain_mid, far, near, send, recv
):
    p = Place()
    links = Links(send, recv)
    greet([p.YR, p.YL])
    reduce = Reduce(links, p, part, far, near)
    reduce.send_far()
    reduce.send_near()
    gain_mid[...] = jnp.zeros_like(gain_mid)
    reduce.merge()
    reduce.settle()

    def one(k, carry):
        at = pl.ds(pl.multiple_of(k * 16, 16), 16)
        through, share = norm_back_rows(own_sum(reduce, at), after_own[at, :], gains[1:2, :])
        gain_mid[...] += share[0:8] + share[8:16]
        total = upstream[p.y, at, :].astype(F32) + through
        d_after_own[at, :] = total
        d_after_low[p.y, at, :] = total.astype(BF16)
        return carry

    lax.fori_loop(0, SPAN // 16, one, 0)
    spread = Spread(links, p, d_after_low)
    spread.start()
    spread.forward()
    spread.near()
    spread.far()
    links.drain()


def mid_back(part, after_own, upstream, gains):
    shape = jax.ShapeDtypeStruct
    return pl.pallas_call(
        mid_back_kernel,
        out_shape=[
            shape((ROWS, SPAN, WIDTH), BF16),
            shape((SPAN, WIDTH), F32),
            shape((8, WIDTH), F32),
        ],
        in_specs=[vmem()] * 4,
        out_specs=[vmem()] * 3,
        scratch_shapes=[
            pltpu.VMEM((2, SPAN, HALF), BF16),
            pltpu.VMEM((2, SPAN, WIDTH), BF16),
            pltpu.SemaphoreType.DMA((12,)),
            pltpu.SemaphoreType.DMA((12,)),
        ],
        compiler_params=params(1),
        name="mid_back",
    )(part, after_own, upstream, gains)


def mix_back_kernel(
    d_after_low,
    mix_full,
    states,
    pre,
    ext,
    decay_g,
    input_g,
    conv_low,
    entering,
    doc_start,
    vectors,
    gate_w,
    d_both,
    d_first,
    small,
    d_blocks,
    d_mixed,
    tail_a,
    d_gates,
    d_conv,
    body,
    rim_send,
    rim_recv,
    totals,
    totals_in,
    after,
    send,
    recv,
):
    p = Place()
    links = Links(send, recv)
    greet([p.seq_at(d) for d in range(1, 8)])
    for start, size in ((0, 256), (256, 256), (512, 128)):
        weights = mix_full[:, :, :, :, 2 * CHAN + start : 2 * CHAN + start + size].reshape(WIDTH, size)
        d_mixed[:, start : start + size] = dot(d_after_low[...], weights)
    small[...] = jnp.zeros_like(small)
    totals[...] = jnp.zeros_like(totals)
    offset = p.s * SPAN

    def chunk(i):
        r, g = lax.rem(i, ROWS), lax.div(i, ROWS)
        at = pl.ds(pl.multiple_of(g * LANES, LANES), LANES)
        rows = pl.ds(pl.multiple_of(r * SPAN, SPAN), SPAN)
        row = lax.broadcasted_iota(jnp.int32, (SPAN, LANES), 0)
        return r, g, at, rows, row

    def states_back(i, carry):
        r, g, at, rows, row = chunk(i)
        d_chunk = d_mixed[rows, at]
        value, slope = gelu_pair(pre[rows, at])
        d_both[rows, at] = (d_chunk * states[rows, at] * slope).astype(BF16)
        decay_now = jnp.exp(decay_g[rows, at] * vectors[7:8, at])
        carried = jnp.where(offset + row == doc_start[r], 0.0, decay_now)
        following = jnp.where(row == SPAN - 1, 1.0, pltpu.roll(carried, SPAN - 1, 0))
        a, b, first_a, first_b = row_scan(following, d_chunk * value, True)
        tail_a[rows, at] = a
        d_mixed[rows, at] = b
        put_pair(totals, at, r, carried[0:1] * first_a, carried[0:1] * first_b)
        return carry

    lax.fori_loop(0, ROWS * GROUPS, states_back, 0)
    keys = [links.go(totals, totals_in.at[p.s], p.seq_at(d)) for d in range(1, 8)]
    state = jnp.zeros((ROWS, CHAN), F32)
    for d in range(1, 8):
        links.arrived(totals_in.at[p.seq_at(-d)["seq"]], keys[d - 1], p.seq_at(-d))
    totals_in[p.s] = totals[...]
    for source in range(7, 0, -1):
        both = totals_in[source]
        state = jnp.where(source > p.s, both[0:ROWS] * state + both[ROWS:], state)
    after[0:ROWS, :] = state
    after[ROWS:, :] = jnp.zeros((8 - ROWS, CHAN), F32)

    def gates_back(i, carry):
        r, g, at, rows, row = chunk(i)
        grads = d_mixed[rows, at] + tail_a[rows, at] * take_row(after, at, r)
        held = states[rows, at]
        previous = jnp.where(row == 0, take_row(entering, at, r), pltpu.roll(held, 1, 0))
        gate_d, gate_i = decay_g[rows, at], input_g[rows, at]
        rate = vectors[7:8, at]
        decay_now = jnp.exp(gate_d * rate)
        headroom = 1.0 - decay_now * decay_now
        root = jnp.sqrt(jnp.maximum(headroom, root_floor))
        conv = conv_low[rows, at].astype(F32)
        d_decay = jnp.where(offset + row == doc_start[r], 0.0, grads * previous) - jnp.where(
            headroom > root_floor, grads * gate_i * conv * decay_now / root, 0.0
        )
        d_log = d_decay * decay_now
        d_zero = d_log * rate * gate_d * (1.0 - gate_d)
        fed = grads * root
        d_one = fed * conv * gate_i * (1.0 - gate_i)
        d_gates[rows, pl.ds(pl.multiple_of(g * LANES, LANES), LANES)] = d_zero.astype(BF16)
        d_gates[rows, pl.ds(pl.multiple_of(CHAN + g * LANES, LANES), LANES)] = d_one.astype(BF16)
        d_conv[rows, at] = fed * gate_i
        small[5:6, at] += jnp.sum(d_zero, axis=0, keepdims=True)
        small[6:7, at] += jnp.sum(d_one, axis=0, keepdims=True)
        small[7:8, at] += jnp.sum(d_log * (-rate_scale * gate_d), axis=0, keepdims=True)
        return carry

    lax.fori_loop(0, ROWS * GROUPS, gates_back, 0)

    held = None
    for g in range(GROUPS):
        total = d_conv[:, g * LANES : (g + 1) * LANES]
        if held is not None:
            total = total + held
        if g < HEADS:
            lo = g * LANES
            product = dot_nt(d_gates[:, lo : lo + 256], gate_w[0, g]) + dot_nt(
                d_gates[:, CHAN + lo : CHAN + lo + 256], gate_w[1, g]
            )
            total = total + product[:, :LANES]
            held = product[:, LANES:]
        d_conv[:, g * LANES : (g + 1) * LANES] = total

    def conv_back(i, carry):
        r, g, at, rows, row = chunk(i)
        d_chunk = d_conv[rows, at]
        begin = doc_start[r]
        place = offset + row
        here = place >= begin
        head = jnp.zeros((8, LANES), F32)
        total = jnp.zeros((SPAN, LANES), F32)
        for k in range(CONV):
            ahead = CONV - 1 - k
            same = (place - ahead >= begin) == here
            kept = jnp.where(same, d_chunk, 0.0)
            value = ext[r, PAD - ahead : PAD - ahead + SPAN, at]
            small[k : k + 1, at] += jnp.sum(kept * value, axis=0, keepdims=True)
            term = kept * vectors[k : k + 1, at]
            if ahead:
                total = total + jnp.where(row < SPAN - ahead, pltpu.roll(term, SPAN - ahead, 0), 0.0)
                head = head + jnp.where(row[0:8] >= 8 - ahead, pltpu.roll(term[0:8], 8 - ahead, 0), 0.0)
            else:
                total = total + term
        small[4:5, at] += jnp.sum(d_chunk, axis=0, keepdims=True)
        body[rows, at] = total
        rim_send[r, :, at] = head
        return carry

    lax.fori_loop(0, ROWS * GROUPS, conv_back, 0)
    k_rim = links.go(rim_send, rim_recv, p.seq_at(-1))
    for j in range(2):
        for h in range(HEADS):
            lo = h * LANES
            product = dot_tn(conv_low[:, lo : lo + 256], d_gates[:, j * CHAN + lo : j * CHAN + lo + 256])
            d_blocks[j, h] = product[32 * h : 32 * h + BLK, :]
    links.arrived(rim_recv, k_rim, p.seq_at(1))
    for r in range(ROWS):
        last = r * SPAN + SPAN - 8
        body[last : last + 8, :] += jnp.where(p.s == 7, 0.0, rim_recv[r])
    for r in range(ROWS):
        d_both[r * SPAN : (r + 1) * SPAN, CHAN:] = body[r * SPAN : (r + 1) * SPAN, :].astype(BF16)

    def first_part(n, carry):
        weights = mix_full[lax.div(n, 2), lax.rem(n, 2), :, :, 0 : 2 * CHAN].reshape(256, 2 * CHAN)
        d_first[:, pl.ds(pl.multiple_of(n * 256, 256), 256)] = dot_nt(d_both[...], weights).astype(BF16)
        return carry

    lax.fori_loop(0, 8, first_part, 0)
    links.drain()


def mix_back(d_after_low, saved, doc_start, vectors, gate_w):
    shape = jax.ShapeDtypeStruct
    tc = (TOKENS, CHAN)
    return pl.pallas_call(
        mix_back_kernel,
        out_shape=[
            shape((TOKENS, 2 * CHAN), BF16),
            shape((TOKENS, WIDTH), BF16),
            shape((8, CHAN), F32),
            shape((2, HEADS, BLK, 256), F32),
        ],
        in_specs=[vmem()] * 9 + [pl.BlockSpec(memory_space=pltpu.SMEM)] + [vmem()] * 2,
        out_specs=[vmem()] * 4,
        scratch_shapes=[
            pltpu.VMEM(tc, F32),
            pltpu.VMEM(tc, F32),
            pltpu.VMEM((TOKENS, 2 * CHAN), BF16),
            pltpu.VMEM(tc, F32),
            pltpu.VMEM(tc, F32),
            pltpu.VMEM((ROWS, PAD, CHAN), F32),
            pltpu.VMEM((ROWS, PAD, CHAN), F32),
            pltpu.VMEM((8, CHAN), F32),
            pltpu.VMEM((8, 8, CHAN), F32),
            pltpu.VMEM((8, CHAN), F32),
            pltpu.SemaphoreType.DMA((8,)),
            pltpu.SemaphoreType.DMA((8,)),
        ],
        compiler_params=params(2),
        name="mix_back",
    )(d_after_low, *saved, doc_start, vectors, gate_w)


def ends_kernel(
    first_part,
    out_part,
    tokens,
    after_own,
    d_after_own,
    gains,
    grad_tokens,
    block_out,
    gain_in,
    far_a,
    near_a,
    far_b,
    near_b,
    send,
    recv,
):
    p = Place()
    links = Links(send, recv)
    greet([p.YR, p.YL])
    back = Reduce(links, p, first_part, far_a, near_a)
    ahead = Reduce(links, p, out_part, far_b, near_b)
    back.send_far()
    back.send_near()
    ahead.send_far()
    ahead.send_near()
    gain_in[...] = jnp.zeros_like(gain_in)
    back.merge()
    back.settle()

    def back_rows(k, carry):
        at = pl.ds(pl.multiple_of(k * 16, 16), 16)
        through, share = norm_back_rows(
            own_sum(back, at), tokens[p.y, at, :].astype(F32), gains[0:1, :]
        )
        gain_in[...] += share[0:8] + share[8:16]
        grad_tokens[p.y, at, :] = (d_after_own[at, :] + through).astype(BF16)
        return carry

    lax.fori_loop(0, SPAN // 16, back_rows, 0)
    spread_a = Spread(links, p, grad_tokens)
    spread_a.start()
    ahead.merge()
    ahead.settle()

    def ahead_rows(k, carry):
        at = pl.ds(pl.multiple_of(k * 16, 16), 16)
        block_out[p.y, at, :] = (after_own[at, :] + own_sum(ahead, at)).astype(BF16)
        return carry

    lax.fori_loop(0, SPAN // 16, ahead_rows, 0)
    spread_b = Spread(links, p, block_out)
    spread_b.start()
    spread_a.forward()
    spread_b.forward()
    spread_a.near()
    spread_a.far()
    spread_b.near()
    spread_b.far()
    links.drain()


def ends(first_part, out_part, tokens, after_own, d_after_own, gains):
    shape = jax.ShapeDtypeStruct
    half = [pltpu.VMEM((2, SPAN, HALF), BF16), pltpu.VMEM((2, SPAN, WIDTH), BF16)]
    return pl.pallas_call(
        ends_kernel,
        out_shape=[
            shape((ROWS, SPAN, WIDTH), BF16),
            shape((ROWS, SPAN, WIDTH), BF16),
            shape((8, WIDTH), F32),
        ],
        in_specs=[vmem()] * 6,
        out_specs=[vmem()] * 3,
        scratch_shapes=half * 2 + [pltpu.SemaphoreType.DMA((24,)), pltpu.SemaphoreType.DMA((24,))],
        compiler_params=params(3),
        name="ends",
    )(first_part, out_part, tokens, after_own, d_after_own, gains)


def per_device(
    tokens,
    init_state,
    conv_state,
    fresh_rows,
    doc_start,
    norm_gains,
    mix_in,
    mix_out,
    conv_weight,
    conv_bias,
    gate_blocks,
    gate_bias,
    decay_param,
    mlp_in,
    mlp_out,
    cotangent,
):
    gains = norm_gains.astype(F32)
    keep = (1 - fresh_rows).astype(F32)
    decay_float = decay_param.astype(F32)
    mix_shard = jnp.concatenate([mix_in[0], mix_in[1], mix_out.T], axis=1)
    mlp_shard = jnp.concatenate([mlp_in[0], mlp_in[1], mlp_out.T], axis=1)
    conv_start = jnp.pad(conv_state.astype(F32) * keep[:, None, None], ((0, 0), (PAD - 3, 0), (0, 0)))
    vectors = jnp.concatenate(
        [
            conv_weight.astype(F32),
            conv_bias.astype(F32)[None],
            gate_bias.astype(F32),
            (-rate_scale * jax.nn.softplus(decay_float))[None],
        ],
        axis=0,
    )
    gate_w = jnp.stack(
        [
            jnp.pad(gate_blocks[:, h], ((0, 0), (32 * h, 96 - 32 * h), (32 * h, 96 - 32 * h)))
            for h in range(HEADS)
        ],
        axis=1,
    )
    rows = tokens.reshape(TOKENS, WIDTH)
    (
        mix_full,
        mlp_full,
        states,
        pre,
        ext,
        decay_g,
        input_g,
        conv_low,
        mixed,
        normed_in,
        entering,
        normed_mid,
        after_own,
    ) = mix_forward(
        rows, mix_shard, mlp_shard, init_state * keep[:, None], conv_start, doc_start, gains, vectors, gate_w
    )
    normed_mid = normed_mid.reshape(TOKENS, WIDTH)
    mlp_w = mlp_full.reshape(WIDTH, MLP_COLS)
    upstream = cotangent.reshape(TOKENS, WIDTH)

    gate_in = dot(normed_mid, mlp_w[:, :MLP])
    up_in = dot(normed_mid, mlp_w[:, MLP : 2 * MLP])
    d_hidden = dot(upstream, mlp_w[:, 2 * MLP :])
    act, slope = gelu_pair(gate_in)
    hidden = (act * up_in).astype(BF16)
    d_gate_up = jnp.concatenate(
        [(d_hidden * up_in * slope).astype(BF16), (d_hidden * act).astype(BF16)], axis=1
    )
    mid_part = dot_nt(d_gate_up, mlp_w[:, : 2 * MLP]).astype(BF16)
    out_part = dot_nt(hidden, mlp_w[:, 2 * MLP :]).astype(BF16)
    grad_mlp = jnp.concatenate(
        [dot_tn(normed_mid, d_gate_up).astype(BF16), dot_tn(upstream, hidden).astype(BF16)], axis=1
    )
    grad_mlp = lax.psum_scatter(grad_mlp, ("seq", "dp"), scatter_dimension=0, tiled=True).astype(F32)

    d_after_low, d_after_own, gain_mid = mid_back(
        mid_part.reshape(ROWS, SPAN, WIDTH), after_own, cotangent, gains
    )
    d_after_rows = d_after_low.reshape(TOKENS, WIDTH)
    d_both, d_first, small, d_blocks = mix_back(
        d_after_rows,
        (mix_full, states, pre, ext, decay_g, input_g, conv_low, entering),
        doc_start,
        vectors,
        gate_w,
    )
    grad_tokens, block_out, gain_in = ends(
        d_first.reshape(ROWS, SPAN, WIDTH),
        out_part.reshape(ROWS, SPAN, WIDTH),
        tokens,
        after_own,
        d_after_own,
        gains,
    )
    grad_mix = jnp.concatenate(
        [dot_tn(normed_in, d_both).astype(BF16), dot_tn(d_after_rows, mixed).astype(BF16)], axis=1
    )
    grad_mix = lax.psum_scatter(grad_mix, ("seq", "dp"), scatter_dimension=0, tiled=True).astype(F32)
    blocks = jnp.stack([d_blocks[:, h, :, 32 * h : 32 * h + BLK] for h in range(HEADS)], axis=1)
    small = lax.psum(small.astype(BF16), ("seq", "dp")).astype(F32)
    blocks = lax.psum(blocks.astype(BF16), ("seq", "dp")).astype(F32)
    grad_gains = jnp.stack([jnp.sum(gain_in, axis=0), jnp.sum(gain_mid, axis=0)])
    grad_gains = lax.psum(grad_gains.astype(BF16), ("seq", "dp", "tensor")).astype(F32)
    return (
        block_out,
        states.reshape(ROWS, SPAN, CHAN),
        grad_tokens,
        grad_gains,
        jnp.stack([grad_mix[:, :CHAN], grad_mix[:, CHAN : 2 * CHAN]]),
        grad_mix[:, 2 * CHAN :].T,
        small[0:4],
        small[4],
        blocks,
        small[5:7],
        small[7] * jax.nn.sigmoid(decay_float),
        jnp.stack([grad_mlp[:, :MLP], grad_mlp[:, MLP : 2 * MLP]]),
        grad_mlp[:, 2 * MLP :].T,
    )


def solution(mesh):
    in_specs = (
        P("dp", "seq", None),
        P("dp", "tensor"),
        P("dp", None, "tensor"),
        P("dp"),
        P("dp"),
        P(),
        P(None, ("seq", "dp"), "tensor"),
        P("tensor", ("seq", "dp")),
        P(None, "tensor"),
        P("tensor"),
        P(None, "tensor", None, None),
        P(None, "tensor"),
        P("tensor"),
        P(None, ("seq", "dp"), "tensor"),
        P("tensor", ("seq", "dp")),
        P("dp", "seq", None),
    )
    out_specs = (
        P("dp", "seq", None),
        P("dp", "seq", "tensor"),
        P("dp", "seq", None),
        P(),
        P(None, ("seq", "dp"), "tensor"),
        P("tensor", ("seq", "dp")),
        P(None, "tensor"),
        P("tensor"),
        P(None, "tensor", None, None),
        P(None, "tensor"),
        P("tensor"),
        P(None, ("seq", "dp"), "tensor"),
        P("tensor", ("seq", "dp")),
    )
    return jax.shard_map(
        per_device, mesh=mesh, in_specs=in_specs, out_specs=out_specs, check_vma=False
    )
```

time: 1390 us -> 634 us (0.46)
  waiting for transfers between devices: 609 us -> 0.05 us
  local copies, waits for them, and re-layouts: 317 us -> 30.7 us
  Pallas kernels: 0 us -> 286 us
  other arithmetic: 153 us -> 40.2 us
  matrix products: 102 us -> 60.9 us
  blocking collectives: 174 us -> 192 us
    pallas_call x0 -> x4, Pallas kernels: none -> 286 us  [the longest x1 135 us: mix_forward(): pl.pallas_call(mix_forward_kernel, out_shape=outs, in_specs=[vmem(), anys...]
    reduce_scatter x4 -> x1, waiting for transfers between devices: 234 us -> 0.01 us  [per_device(): lax.psum_scatter(grad_mlp, ('seq', 'dp'), scatter_dimension=0, tiled=True)]
    psum x4 -> x1, waiting for transfers between devices: 227 us -> 0.01 us  [per_device(): blocks = lax.psum(blocks.astype(BF16), ('seq', 'dp')).astype(F32)]
    slice x99 -> x4, local copies, waits for them, and re-layouts: 161 us -> 2.05 us  [the longest x1 0.61 us: per_device(): small[7] * jax.nn.sigmoid(decay_float)]
    all_gather x4 -> x0, waiting for transfers between devices: 145 us -> none  [the longest x1 60.7 us: per_device(): lax.all_gather(mlp_in, ('seq', 'dp'), axis=1, tiled=True)]
    pad x48 -> x1, local copies, waits for them, and re-layouts: 94.7 us -> 0.65 us  [per_device(): jnp.pad(conv_state.astype(F32) * keep[:, None, None], ((0, 0), (PAD - 3,...]
    psum x1 -> x2, blocking collectives: 123 us -> 192 us  [the longest x1 124 us: per_device(): small = lax.psum(small.astype(BF16), ('seq', 'dp')).astype(F32)]
    all_gather x4 -> x0, blocking collectives: 51.7 us -> none  [entering_2(): gathered = jax.tree.map(lambda a: lax.all_gather(a, axis), part)]
  transfers between devices with their start and end apart: 14 -> 3, of which waited for: 10 -> 0; matrix products, arithmetic and copies ran while one was open for 23% -> 12% of each run, Pallas kernels for 0% -> 12%
where the time goes in v1:
time: 634 us; the launch traced here: 626 us
  Pallas kernels  286 us (45%)
  blocking collectives  192 us (30%)
  matrix products  60.9 us (10%)
  other arithmetic  40.2 us (6%)
  local copies, waits for them, and re-layouts  30.7 us (5%)
  between operations  14.5 us (2%)
    pallas_call x1, Pallas kernels, mix_forward(): pl.pallas_call(mix_forward_kernel, out_shape=outs, in_specs=[vmem(), anys...  135 us
    psum x1, blocking collectives, per_device(): small = lax.psum(small.astype(BF16), ('seq', 'dp')).astype(F32)  124 us
    pallas_call x1, Pallas kernels, ends(): pl.pallas_call(ends_kernel, out_shape=[shape((ROWS, SPAN, WIDTH), BF16),...  72.8 us
    psum x1, blocking collectives, per_device(): lax.psum(grad_gains.astype(BF16), ('seq', 'dp', 'tensor')).astype(F32)  68.4 us
    pallas_call x1, Pallas kernels, mid_back(): pl.pallas_call(mid_back_kernel, out_shape=[shape((ROWS, SPAN, WIDTH), BF1...  42.6 us
    pallas_call x1, Pallas kernels, mix_back(): pl.pallas_call(mix_back_kernel, out_shape=[shape((TOKENS, 2 * CHAN), BF16...  35.7 us
    dot_general x4, matrix products, dot_tn(): lax.dot_general(a, b, (((0,), (0,)), ((), ())), preferred_element_type=F32)  23.7 us
    unnamed x41, local copies, waits for them, and re-layouts  22.9 us
  transfers between devices with their start and end apart: 3, of which 0 were waited for; matrix products, arithmetic and copies ran while one was open for 12% of the time, Pallas kernels for 12%

profile of v1, /device:TPU:1, one launch (start us, length us, event | category | flops | bytes accessed | tf_op | source)
XLA Modules:
  0.0 625.5 jit_solution(6111403853328301604)
XLA Ops:
  10.7 1.3 convert_element_type.81.gains
  12.8 1.4 broadcast_multiply_fusion.init_state
  15.2 1.1 slice_bitcast_fusion.7
  16.2 1.2 slice_bitcast_fusion.11
  20.6 1.1 pad_maximum_fusion.5.gate_w
  21.7 135.4 %mix_forward.1 = (bf16[4,2,4,64,1920]{4,3,2,1,0:T(8,128)(2,1)}, bf16[4,2,4,64,4608]{4,3,2,1,0:T(8,128)(2,1)}, f32[512,640]{1,0:T(8,128)}, f32[512,640]{1,0:T(8,1...) custom-call(bf16[512,2048]{1,0:T(8,128)(2,1)} %bitcast.71, ...), custom_call_target="tpu_custom_call" | custom-call | tf_op jit(solution)/shard_map/mix_forward/pallas_call | solution.py:579
  157.1 6.4 %fusion.3 = f32[512,1536]{0,1:T(8,128)S(1)} fusion(bf16[512,2048]{1,0:T(8,128)(2,1)} %bitcast.87, bf16[2048,4608]{1,0:T(8,128)(2,1)} %bitcast.82), kind=kOutput, calls=%fused_computation.8 | convolution fusion | flops 3221225472 | bytes 11534336 | tf_op jit(solution)/shard_map/dot_general | solution.py:226
  163.5 3.0 copy-done.10
  166.6 5.2 fusion.11
  171.8 8.7 %multiply_convert_fusion = (bf16[512,1536]{0,1:T(8,128)(2,1)}, bf16[512,1536]{0,1:T(8,128)(2,1)}, bf16[512,1536]{0,1:T(8,128)(2,1)}) fusion(f32[512,1536]{0,1:T(8,128)S(1)} %fusion.3, f32[512,1536]{0,1:T(8,128)} %fusion.11, bf16[512,2048]{1,0:T(8,128)(2,1)S(1)} %bitcast.89, bf16[2048,4608]{1,0:T(8,128)(2,1)S(1)} %bitcast.85), kind=kOutput, calls=%fused_computation.29 | convolution fusion | flops 3240886272 | bytes 19398656 | tf_op jit(solution)/shard_map/dot_general | solution.py:226
  180.6 9.3 %fusion.22 = bf16[512,2048]{1,0:T(8,128)(2,1)} fusion(bf16[2048,4608]{1,0:T(8,128)(2,1)S(1)} %bitcast.86, bf16[512,1536]{0,1:T(8,128)(2,1)} %get-tuple-element.102, bf16[512,1536]{0,1:T(8,128)(2,1)} %get-tuple-element.101), kind=kOutput, calls=%fused_computation.31 | convolution fusion | flops 6449790976 | bytes 17825792 | tf_op jit(solution)/shard_map/dot_general | solution.py:230
  189.9 42.6 %mid_back.1 = (bf16[4,128,2048]{2,1,0:T(8,128)(2,1)}, f32[128,2048]{1,0:T(8,128)}, f32[8,2048]{1,0:T(8,128)}) custom-call(bf16[4,128,2048]{2,1,0:T(8,128)(2,1)} %bitcast.75, f32[128,2048]{1,0:T(8,128)} %get-tuple-element.38.after_own, bf16[4,128,2048]{2,1,0:T(8,128)(2,1)} %upstream.1, f32[2,2048]{1,0:T(2,128)} %convert_element_type.81.gains), custom_call_target="tpu_custom_call" | custom-call | tf_op jit(solution)/shard_map/mid_back/pallas_call | solution.py:637
  232.5 35.7 %mix_back.1 = (bf16[512,1280]{1,0:T(8,128)(2,1)}, bf16[512,2048]{1,0:T(8,128)(2,1)}, f32[8,640]{1,0:T(8,128)}, f32[2,4,160,256]{3,2,1,0:T(8,128)}) custom-call(bf16[512,2048]{1,0:T(8,128)(2,1)} %bitcast.78, bf16[4,2,4,64,1920]{4,3,2,1,0:T(8,128)(2,1)} %get-tuple-element.40.mix_full, f32[512,640]{1,0:T(8,128)} %get-tuple-element.41.states, ...), custom_call_target="tpu_custom_call" | custom-call | tf_op jit(solution)/shard_map/mix_back/pallas_call | solution.py:823
  268.1 1.5 convert.21
  271.1 3.3 convolution_convert_fusion.3
  274.5 4.7 convolution_convert_fusion.1
  279.2 7.1 %pad_maximum_fusion.1 = bf16[2048,1920]{0,1:T(8,128)(2,1)} fusion(bf16[2048,640]{0,1:T(8,128)(2,1)S(1)} %convolution_convert_fusion.3, bf16[2048,1280]{0,1:T(8,128)(2,1)} %convolution_convert_fusion.1), kind=kLoop, calls=%fused_computation.4 | loop fusion | flops 15728640 | bytes 15728640 | tf_op jit(solution)/shard_map/concatenate | solution.py:1028
  286.3 10.7 %copy.83 = bf16[2048,1920]{1,0:T(8,128)(2,1)} copy(bf16[2048,1920]{0,1:T(8,128)(2,1)} %pad_maximum_fusion.1) | data formatting | bytes 15728640
  297.1 1.5 copy-done.2
  298.6 6.8 %fusion.2 = bf16[2048,1536]{1,0:T(8,128)(2,1)} fusion(bf16[512,1536]{0,1:T(8,128)(2,1)} %get-tuple-element.100, bf16[512,2048]{1,0:T(8,128)(2,1)S(1)} %bitcast.74), kind=kOutput, calls=%fused_computation.7 | convolution fusion | flops 3224371200 | bytes 9961472 | tf_op jit(solution)/shard_map/dot_general | solution.py:234
  305.4 8.8 %convolution_convert_fusion = bf16[2048,3072]{1,0:T(8,128)(2,1)S(1)} fusion(bf16[512,2048]{1,0:T(8,128)(2,1)} %bitcast.88, bf16[512,1536]{0,1:T(8,128)(2,1)} %get-tuple-element.102, bf16[512,1536]{0,1:T(8,128)(2,1)S(1)} %copy-done.16), kind=kOutput, calls=%fused_computation.3 | convolution fusion | flops 6455033856 | bytes 17825792 | tf_op jit(solution)/shard_map/dot_general | solution.py:234
  314.2 14.5 %pad_maximum_fusion = bf16[2048,4608]{1,0:T(8,128)(2,1)} fusion(bf16[2048,1536]{1,0:T(8,128)(2,1)} %fusion.2, bf16[2048,3072]{1,0:T(8,128)(2,1)S(1)} %convolution_convert_fusion), kind=kLoop, calls=%fused_computation | loop fusion | flops 37748736 | bytes 37748736 | tf_op jit(solution)/shard_map/concatenate | solution.py:1004
  329.4 124.1 %psum.22 = bf16[8,640]{1,0:T(8,128)(2,1)S(1)} all-reduce(bf16[8,640]{1,0:T(8,128)(2,1)S(1)} %convert_element_type.94), channel_id=1, replica_groups=mesh['seq'=8,'dp'=4,'tensor'=4] {'seq','dp'}, use_global_device_ids=true, to_apply=%region_4.5 | all-reduce | flops 5120 | bytes 20480 | tf_op jit(solution)/shard_map/psum | solution.py:1033
  454.7 7.5 %fusion.25 = bf16[512,2048]{1,0:T(8,128)(2,1)} fusion(bf16[512,1536]{0,1:T(8,128)(2,1)S(1)} %copy-done.15, bf16[2048,4608]{1,0:T(8,128)(2,1)} %bitcast.83), kind=kOutput, calls=%fused_computation.32 | convolution fusion | flops 3222274048 | bytes 9961472 | tf_op jit(solution)/shard_map/dot_general | solution.py:230
  462.3 72.8 %ends.1 = (bf16[4,128,2048]{2,1,0:T(8,128)(2,1)}, bf16[4,128,2048]{2,1,0:T(8,128)(2,1)}, f32[8,2048]{1,0:T(8,128)}) custom-call(bf16[4,128,2048]{2,1,0:T(8,128)(2,1)} %bitcast.76, bf16[4,128,2048]{2,1,0:T(8,128)(2,1)} %bitcast.77, bf16[4,128,2048]{2,1,0:T(8,128)(2,1)} %tokens.1, f32[128,2048]{1,0:T(8,128)} %get-tuple-element.38.after_own, ...), custom_call_target="tpu_custom_call" | custom-call | tf_op jit(solution)/shard_map/ends/pallas_call | solution.py:917
  536.1 68.4 %psum.21 = bf16[2,2048]{1,0:T(2,128)(2,1)S(1)} all-reduce(bf16[2,2048]{1,0:T(2,128)(2,1)S(1)} %pad_maximum_fusion.12), channel_id=1, replica_groups=mesh['seq'=8,'dp'=4,'tensor'=4] {'seq','dp','tensor'}, use_global_device_ids=true, to_apply=%region_2.3 | all-reduce | flops 4096 | bytes 16384 | tf_op jit(solution)/shard_map/psum | solution.py:1036
  606.3 2.3 convert_element_type.96
  608.6 1.2 copy.84
  611.7 1.1 convert_element_type.100
  614.7 1.3 copy.94
  616.0 1.1 copy.95
  617.2 1.3 copy.96
  (77 shorter events, 18.6 us)
Async XLA Ops:
  7.2 11.2 %copy-start.6 = (bf16[640,64]{0,1:T(8,128)(2,1)S(1)}, bf16[640,64]{0,1:T(8,128)(2,1)}, u32[]{:S(2)}) copy-start(bf16[640,64]{0,1:T(8,128)(2,1)} %param.23) | copy-start | bytes 245764
  7.2 11.9 %copy-start.5 = (bf16[1536,64]{0,1:T(8,128)(2,1)S(1)}, bf16[1536,64]{0,1:T(8,128)(2,1)}, u32[]{:S(2)}) copy-start(bf16[1536,64]{0,1:T(8,128)(2,1)} %param.30) | copy-start | bytes 589828
  7.2 599.1 %all-reduce.7.cloned.1.call-start = ((), (), s32[]{:S(2)}) async-start(), calls=%async_computation.2 | async-start | bytes 1310720 | tf_op jit(solution)/shard_map/psum | solution.py:1034
  157.1 6.5 %copy-start.1 = (bf16[4,128,2048]{2,1,0:T(8,128)(2,1)S(1)}, bf16[4,128,2048]{2,1,0:T(8,128)(2,1)}, u32[]{:S(2)}) copy-start(bf16[4,128,2048]{2,1,0:T(8,128)(2,1)} %upstream.1) | copy-start | bytes 6291460
  157.1 9.5 %copy-start.10 = (bf16[4,2,4,64,4608]{4,3,2,1,0:T(8,128)(2,1)S(1)}, bf16[4,2,4,64,4608]{4,3,2,1,0:T(8,128)(2,1)}, u32[]{:S(2)}) copy-start(bf16[4,2,4,64,4608]{4,3,2,1,0:T(8,128)(2,1)} %get-tuple-element.36) | copy-start | bytes 56623108
  166.6 5.2 copy-start.11
  268.1 3.0 copy-start.14
  270.8 337.7 %reduce-scatter.7.cloned.1.call-start = ((), (), s32[]{:S(2)}) async-start(), calls=%async_computation.4 | async-start | bytes 8110080
  271.1 3.3 copy-start.12
  271.1 3.3 copy-start.13
  297.0 1.6 copy-start.2
  297.0 314.7 %reduce-scatter.5.cloned.1.call-start = ((), (), s32[]{:S(2)}) async-start(), calls=%async_computation.3 | async-start | bytes 19464192 | tf_op jit(solution)/shard_map/reduce_scatter | solution.py:1007
  298.6 6.9 %copy-start.16 = (bf16[512,1536]{0,1:T(8,128)(2,1)S(1)}, bf16[512,1536]{0,1:T(8,128)(2,1)}, u32[]{:S(2)}) copy-start(bf16[512,1536]{0,1:T(8,128)(2,1)} %get-tuple-element.101) | copy-start | bytes 4718596
  328.7 0.7 copy-start.8
  328.7 126.0 %copy-start.15 = (bf16[512,1536]{0,1:T(8,128)(2,1)S(1)}, bf16[512,1536]{0,1:T(8,128)(2,1)}, u32[]{:S(2)}) copy-start(bf16[512,1536]{0,1:T(8,128)(2,1)} %get-tuple-element.100) | copy-start | bytes 4718596
  462.3 73.7 %copy-start.7 = (f32[8,2048]{1,0:T(8,128)S(1)}, f32[8,2048]{1,0:T(8,128)}, u32[]{:S(2)}) copy-start(f32[8,2048]{1,0:T(8,128)} %get-tuple-element.53) | copy-start | bytes 196612
  462.3 143.4 %copy-start.9 = (bf16[640]{0:T(1024)(128)(2,1)S(1)}, bf16[640]{0:T(1024)(128)(2,1)}, u32[]{:S(2)}) copy-start(bf16[640]{0:T(1024)(128)(2,1)} %param.28) | copy-start | bytes 3844
  610.8 3.9 copy-start.4
  613.7 2.3 copy-start
  614.7 2.6 copy-start.3
Sparse Core Ops, SparseCore 0:
  271.0 101.0 all-reduce.6
  375.9 88.0 reduce-scatter.6
  468.5 122.5 reduce-scatter.4

commit v2 on v1

--- a/solution.py
+++ b/solution.py
@@ -23,6 +23,10 @@
 MLP = 1536
 MIX_COLS = 3 * CHAN
 MLP_COLS = 3 * MLP
+CHUNK = 256
+CHUNKS = MLP // CHUNK
+SMALL = 256
+RS_COLS = MIX_COLS + SMALL
 LANES = 128
 GROUPS = CHAN // LANES
 PAD = 8
@@ -289,15 +293,28 @@
     return jnp.sum(jnp.where(row == r, ref[:, at], 0.0), axis=0, keepdims=True)
 
 
+def assemble_vectors(vectors, conv_weight, conv_bias, gate_bias, decay_param):
+    vectors[0:4, :] = conv_weight[...].astype(F32)
+    vectors[4:5, :] = conv_bias[...].astype(F32)
+    vectors[5:7, :] = gate_bias[...].astype(F32)
+    vectors[7:8, :] = -rate_scale * jnp.log1p(jnp.exp(decay_param[...].astype(F32)))
+
+
 def mix_forward_kernel(
     tokens,
-    mix_shard,
-    mlp_shard,
+    mix_in,
+    mix_out,
+    mlp_in,
+    mlp_out,
     init_state,
-    conv_start,
+    conv_state,
+    fresh_rows,
     doc_start,
-    gains,
-    vectors,
+    gain_rows,
+    conv_weight,
+    conv_bias,
+    gate_bias,
+    decay_param,
     gate_w,
     mix_full_out,
     mlp_full,
@@ -310,8 +327,12 @@
     mixed_out,
     normed_in_out,
     entering_out,
+    vectors_out,
     normed_mid,
     after_own,
+    mlp_own,
+    gains,
+    vectors,
     mix_full,
     normed_in,
     pre,
@@ -337,14 +358,23 @@
 ):
     p = Place()
     links = Links(send, recv)
-    own_mix = pltpu.make_async_copy(mix_shard, mix_full.at[p.x, p.c, p.z], local.at[0])
-    own_mlp = pltpu.make_async_copy(mlp_shard, mlp_full.at[p.x, p.c, p.z], local.at[1])
-    own_mix.start()
-    own_mlp.start()
+    mine = mix_full.at[p.x, p.c, p.z]
+    for j in range(2):
+        mine[:, j * CHAN : (j + 1) * CHAN] = mix_in[j]
+    mine[:, 2 * CHAN :] = mix_out[...].astype(F32).T.astype(BF16)
     greet([p.seq_at(d) for d in range(1, 8)] + [p.ZR, p.ZL, p.YR, p.YL])
-    own_mix.wait()
     mix_gather = Gather(links, p, mix_full)
     mix_gather.first()
+    down = mlp_out[...].astype(F32).T.astype(BF16)
+    for f in range(CHUNKS):
+        lo, to = f * CHUNK, 3 * f * CHUNK
+        mlp_own[:, to : to + CHUNK] = mlp_in[0, :, lo : lo + CHUNK]
+        mlp_own[:, to + CHUNK : to + 2 * CHUNK] = mlp_in[1, :, lo : lo + CHUNK]
+        mlp_own[:, to + 2 * CHUNK : to + 3 * CHUNK] = down[:, lo : lo + CHUNK]
+    own_mlp = pltpu.make_async_copy(mlp_own, mlp_full.at[p.x, p.c, p.z], local.at[0])
+    own_mlp.start()
+    gains[...] = gain_rows[...].astype(F32)
+    assemble_vectors(vectors, conv_weight, conv_bias, gate_bias, decay_param)
 
     def norm_rows(first, last):
         def one(k, carry):
@@ -376,6 +406,7 @@
 
     save(mix_full, mix_full_out)
     save(normed_in, normed_in_out)
+    save(vectors, vectors_out)
 
     def project(n, carry):
         at = pl.ds(pl.multiple_of(n * 256, 256), 256)
@@ -395,7 +426,10 @@
     links.arrived(rim_recv, k_rim, p.seq_at(-1))
     at_start = p.s == 0
     for r in range(ROWS):
-        ext[r, 0:PAD, :] = jnp.where(at_start, conv_start[r], rim_recv[r])
+        keep = (1 - fresh_rows[r]).astype(F32)
+        ext[r, 0:PAD, :] = jnp.where(at_start, 0.0, rim_recv[r])
+        first_rim = conv_state[r].astype(F32) * keep
+        ext[r, PAD - 3 : PAD, :] = jnp.where(at_start, first_rim, rim_recv[r, PAD - 3 : PAD, :])
     offset = p.s * SPAN
 
     def conv_chunk(i, carry):
@@ -414,7 +448,6 @@
         return carry
 
     lax.fori_loop(0, ROWS * GROUPS, conv_chunk, 0)
-    mlp_gather.middle()
     save(ext, ext_out)
     save(conv_low, conv_out)
 
@@ -452,8 +485,11 @@
     keys = [links.go(totals, totals_in.at[p.s], p.seq_at(d)) for d in range(1, 8)]
     save(decay_g, decay_out)
     save(input_g, input_out)
-    mlp_gather.finish()
-    state = init_state[...]
+    row = lax.broadcasted_iota(jnp.int32, (ROWS, CHAN), 0)
+    kept = jnp.zeros((ROWS, CHAN), F32)
+    for r in range(ROWS):
+        kept = jnp.where(row == r, (1 - fresh_rows[r]).astype(F32), kept)
+    state = init_state[...] * kept
     for d in range(1, 8):
         links.arrived(totals_in.at[p.seq_at(-d)["seq"]], keys[d - 1], p.seq_at(-d))
     totals_in[p.s] = totals[...]
@@ -494,6 +530,7 @@
     partial(p.yl)
     reduce.send_near()
     partial(p.y)
+    mlp_gather.middle()
     reduce.merge()
     reduce.settle()
 
@@ -510,10 +547,11 @@
     lax.fori_loop(0, SPAN // 16, norm_mid, 0)
     spread = Spread(links, p, normed_mid)
     spread.start()
-    mlp_gather.settle()
     spread.forward()
+    mlp_gather.finish()
     spread.near()
     spread.far()
+    mlp_gather.settle()
     for copy in saves:
         copy.wait()
     links.drain()
@@ -529,11 +567,15 @@
     return pl.BlockSpec(memory_space=pltpu.VMEM)
 
 
+def smem():
+    return pl.BlockSpec(memory_space=pltpu.SMEM)
+
+
 def anyspace():
     return pl.BlockSpec(memory_space=pl.ANY)
 
 
-def mix_forward(tokens, mix_shard, mlp_shard, init_state, conv_start, doc_start, gains, vectors, gate_w):
+def mix_forward(*operands):
     shape = jax.ShapeDtypeStruct
     tc = (TOKENS, CHAN)
     ext_shape = (ROWS, PAD + SPAN, CHAN)
@@ -549,10 +591,14 @@
         shape(tc, BF16),
         shape((TOKENS, WIDTH), BF16),
         shape((8, CHAN), F32),
+        shape((8, CHAN), F32),
         shape((ROWS, SPAN, WIDTH), BF16),
         shape((SPAN, WIDTH), F32),
     ]
     scratch = [
+        pltpu.VMEM((64, MLP_COLS), BF16),
+        pltpu.VMEM((2, WIDTH), F32),
+        pltpu.VMEM((8, CHAN), F32),
         pltpu.VMEM((4, 2, 4, 64, MIX_COLS), BF16),
         pltpu.VMEM((TOKENS, WIDTH), BF16),
         pltpu.VMEM((TOKENS, 2 * CHAN), F32),
@@ -579,13 +625,12 @@
     return pl.pallas_call(
         mix_forward_kernel,
         out_shape=outs,
-        in_specs=[vmem(), anyspace(), anyspace(), vmem(), vmem(), pl.BlockSpec(memory_space=pltpu.SMEM)]
-        + [vmem()] * 3,
-        out_specs=[anyspace()] * 11 + [vmem()] * 2,
+        in_specs=[vmem()] * 7 + [smem()] * 2 + [vmem()] * 6,
+        out_specs=[anyspace()] * 12 + [vmem()] * 2,
         scratch_shapes=scratch,
         compiler_params=params(0),
         name="mix_forward",
-    )(tokens, mix_shard, mlp_shard, init_state, conv_start, doc_start, gains, vectors, gate_w)
+    )(*operands)
 
 
 def norm_back_rows(d_row, stream, gain_row):
@@ -602,7 +647,7 @@
 
 
 def mid_back_kernel(
-    part, after_own, upstream, gains, d_after_low, d_after_own, gain_mid, far, near, send, recv
+    part, after_own, upstream, gain_rows, d_after_low, d_after_own, gain_mid, far, near, send, recv
 ):
     p = Place()
     links = Links(send, recv)
@@ -611,12 +656,13 @@
     reduce.send_far()
     reduce.send_near()
     gain_mid[...] = jnp.zeros_like(gain_mid)
+    gain = gain_rows[1:2, :].astype(F32)
     reduce.merge()
     reduce.settle()
 
     def one(k, carry):
         at = pl.ds(pl.multiple_of(k * 16, 16), 16)
-        through, share = norm_back_rows(own_sum(reduce, at), after_own[at, :], gains[1:2, :])
+        through, share = norm_back_rows(own_sum(reduce, at), after_own[at, :], gain)
         gain_mid[...] += share[0:8] + share[8:16]
         total = upstream[p.y, at, :].astype(F32) + through
         d_after_own[at, :] = total
@@ -654,7 +700,193 @@
     )(part, after_own, upstream, gains)
 
 
-def mix_back_kernel(
+def mlp_kernel(
+    normed, upstream, weights, mid_part, out_part, grads, normed_t, upstream_t, d_both, mid_sum, out_sum
+):
+    step = pl.program_id(0)
+
+    @pl.when(step == 0)
+    def _():
+        def turn(n, carry):
+            at = pl.ds(pl.multiple_of(n * 256, 256), 256)
+            normed_t[at, :] = normed[:, at].T
+            upstream_t[at, :] = upstream[:, at].T
+            return carry
+
+        lax.fori_loop(0, WIDTH // 256, turn, 0)
+        mid_sum[...] = jnp.zeros_like(mid_sum)
+        out_sum[...] = jnp.zeros_like(out_sum)
+
+    gate = dot(normed[...], weights[:, 0:CHUNK])
+    up = dot(normed[...], weights[:, CHUNK : 2 * CHUNK])
+    d_hidden = dot(upstream[...], weights[:, 2 * CHUNK :])
+    act, slope = gelu_pair(gate)
+    hidden = (act * up).astype(BF16)
+    d_both[:, 0:CHUNK] = (d_hidden * up * slope).astype(BF16)
+    d_both[:, CHUNK : 2 * CHUNK] = (d_hidden * act).astype(BF16)
+    d_both[:, 2 * CHUNK :] = hidden
+
+    def tile(n, carry):
+        at = pl.ds(pl.multiple_of(n * 256, 256), 256)
+        grads[at, 0 : 2 * CHUNK] = dot(normed_t[at, :], d_both[:, 0 : 2 * CHUNK]).astype(BF16)
+        grads[at, 2 * CHUNK :] = dot(upstream_t[at, :], d_both[:, 2 * CHUNK :]).astype(BF16)
+        mid_sum[:, at] += dot_nt(d_both[:, 0 : 2 * CHUNK], weights[at, 0 : 2 * CHUNK])
+        out_sum[:, at] += dot_nt(d_both[:, 2 * CHUNK :], weights[at, 2 * CHUNK :])
+        return carry
+
+    lax.fori_loop(0, WIDTH // 256, tile, 0)
+
+    @pl.when(step == CHUNKS - 1)
+    def _():
+        mid_part[...] = mid_sum[...].astype(BF16)
+        out_part[...] = out_sum[...].astype(BF16)
+
+
+def mlp_all(normed, upstream, weights):
+    shape = jax.ShapeDtypeStruct
+    whole = pl.BlockSpec((TOKENS, WIDTH), lambda f: (0, 0))
+    block = pl.BlockSpec((WIDTH, 3 * CHUNK), lambda f: (0, f))
+    return pl.pallas_call(
+        mlp_kernel,
+        grid=(CHUNKS,),
+        out_shape=[
+            shape((TOKENS, WIDTH), BF16),
+            shape((TOKENS, WIDTH), BF16),
+            shape((WIDTH, MLP_COLS), BF16),
+        ],
+        in_specs=[whole, whole, block],
+        out_specs=[whole, whole, block],
+        scratch_shapes=[
+            pltpu.VMEM((WIDTH, TOKENS), BF16),
+            pltpu.VMEM((WIDTH, TOKENS), BF16),
+            pltpu.VMEM((TOKENS, 3 * CHUNK), BF16),
+            pltpu.VMEM((TOKENS, WIDTH), F32),
+            pltpu.VMEM((TOKENS, WIDTH), F32),
+        ],
+        compiler_params=pltpu.CompilerParams(vmem_limit_bytes=VMEM_BYTES),
+        cost_estimate=pl.CostEstimate(
+            flops=18 * TOKENS * WIDTH * MLP, bytes_accessed=4 * WIDTH * MLP_COLS, transcendentals=TOKENS * MLP
+        ),
+        name="mlp_all",
+    )(normed, upstream, weights)
+
+
+class Scatter:
+    def __init__(self, links, place, grads, sib, far, near, half_a, half_b, far_2, near_2):
+        self.links, self.p = links, place
+        self.grads, self.sib = grads, sib
+        self.far, self.near, self.far_2, self.near_2 = far, near, far_2, near_2
+        self.half_a, self.half_b = half_a, half_b
+        self.sib_keys = {}
+
+    def give(self, xx):
+        p = self.p
+        self.sib_keys[xx] = self.links.go(self.grads.at[xx, 1 - p.c], self.sib.at[xx], p.SIB)
+
+    def take(self, xx):
+        p, sib, grads = self.p, self.sib, self.grads
+        self.links.arrived(sib.at[xx], self.sib_keys[xx], p.SIB)
+
+        def one(j, carry):
+            sib[xx, j] = (sib[xx, j].astype(F32) + grads[xx, p.c, j].astype(F32)).astype(BF16)
+            return carry
+
+        lax.fori_loop(0, 4, one, 0)
+
+    def _ring(self, view, i, right, left, far, near, base):
+        links = self.links
+        ir, il, i2 = lax.rem(i + 1, 4), lax.rem(i + 3, 4), lax.rem(i + 2, 4)
+        a, b = pl.ds(base, 16), pl.ds(base + 16, 16)
+        na, nb = pl.ds(0, 16), pl.ds(16, 16)
+        k0 = links.go(view(i2, a), far.at[0], right)
+        k1 = links.go(view(i2, b), far.at[1], left)
+        k2 = links.go(view(ir, b), near.at[0, :, nb], right)
+        k3 = links.go(view(il, a), near.at[1, :, na], left)
+        keys = []
+
+        def merge():
+            for way, k, row, at, source, target, to in (
+                (0, k0, ir, a, left, right, na),
+                (1, k1, il, b, right, left, nb),
+            ):
+                links.arrived(far.at[way], k, source)
+                mine = view(row, at)
+
+                def one(j, carry):
+                    far[way, j] = (far[way, j].astype(F32) + mine[j].astype(F32)).astype(BF16)
+                    return carry
+
+                lax.fori_loop(0, far.shape[1], one, 0)
+                keys.append(links.go(far.at[way], near.at[way, :, to], target))
+
+        def settle():
+            links.arrived(near.at[0, :, nb], k2, left)
+            links.arrived(near.at[1, :, na], k3, right)
+            links.arrived(near.at[0, :, na], keys[0], left)
+            links.arrived(near.at[1, :, nb], keys[1], right)
+
+        return merge, settle
+
+    def first(self):
+        p, sib = self.p, self.sib
+        self.x_ring = self._ring(lambda j, r: sib.at[j, :, r], p.x, p.XR, p.XL, self.far.at[0], self.near.at[0], 0)
+        self.z_ring = self._ring(lambda j, r: sib.at[:, j, r], p.z, p.ZR, p.ZL, self.far.at[1], self.near.at[1], 32)
+
+    def merge(self):
+        self.x_ring[0]()
+        self.z_ring[0]()
+
+    def turn(self):
+        p, sib, near = self.p, self.sib, self.near
+        self.x_ring[1]()
+
+        def one_a(j, carry):
+            total = sib[p.x, j, 0:32].astype(F32) + near[0, 0, j].astype(F32) + near[0, 1, j].astype(F32)
+            self.half_a[j, 0] = total.astype(BF16)
+            return carry
+
+        lax.fori_loop(0, 4, one_a, 0)
+        half_a, half_b = self.half_a, self.half_b
+        self.ring_a = self._ring(
+            lambda j, r: half_a.at[j, :, r], p.z, p.ZR, p.ZL, self.far_2.at[0], self.near_2.at[0], 0
+        )
+        self.z_ring[1]()
+
+        def one_b(j, carry):
+            total = sib[j, p.z, 32:64].astype(F32) + near[1, 0, j].astype(F32) + near[1, 1, j].astype(F32)
+            self.half_b[j, 0] = total.astype(BF16)
+            return carry
+
+        lax.fori_loop(0, 4, one_b, 0)
+        self.ring_b = self._ring(
+            lambda j, r: half_b.at[j, :, r], p.x, p.XR, p.XL, self.far_2.at[1], self.near_2.at[1], 0
+        )
+
+    def merge_2(self):
+        self.ring_a[0]()
+        self.ring_b[0]()
+
+    def finish(self, store):
+        p, near = self.p, self.near_2
+        self.ring_a[1]()
+        store(0, self.half_a[p.z, 0].astype(F32) + near[0, 0, 0].astype(F32) + near[0, 1, 0].astype(F32))
+        self.ring_b[1]()
+        store(32, self.half_b[p.x, 0].astype(F32) + near[1, 0, 0].astype(F32) + near[1, 1, 0].astype(F32))
+
+    @staticmethod
+    def scratch(columns):
+        return [
+            pltpu.VMEM((4, 4, 64, columns), BF16),
+            pltpu.VMEM((2, 2, 4, 16, columns), BF16),
+            pltpu.VMEM((2, 2, 4, 32, columns), BF16),
+            pltpu.VMEM((4, 1, 32, columns), BF16),
+            pltpu.VMEM((4, 1, 32, columns), BF16),
+            pltpu.VMEM((2, 2, 1, 16, columns), BF16),
+            pltpu.VMEM((2, 2, 1, 32, columns), BF16),
+        ]
+
+
+def back_kernel(
     d_after_low,
     mix_full,
     states,
@@ -664,34 +896,76 @@
     input_g,
     conv_low,
     entering,
-    doc_start,
+    mixed,
+    normed_in,
+    out_part,
+    tokens,
+    after_own,
+    d_after_own,
+    gain_mid,
+    gain_rows,
     vectors,
     gate_w,
+    doc_start,
+    grad_tokens,
+    block_out,
+    grad_mix,
+    small_sums,
+    block_sums,
+    gain_sums,
+    work,
+    own_tokens,
+    d_mixed,
+    tail_a,
+    d_gates,
     d_both,
     d_first,
     small,
-    d_blocks,
-    d_mixed,
-    tail_a,
-    d_gates,
-    d_conv,
-    body,
     rim_send,
     rim_recv,
     totals,
     totals_in,
     after,
+    far_a,
+    near_a,
+    far_b,
+    near_b,
+    sib,
+    far_s,
+    near_s,
+    half_a,
+    half_b,
+    far_2,
+    near_2,
+    small_all,
+    gain_in,
+    gain_y,
+    gain_s,
+    gain_z,
+    local,
     send,
     recv,
 ):
     p = Place()
     links = Links(send, recv)
-    greet([p.seq_at(d) for d in range(1, 8)])
+    load = pltpu.make_async_copy(mix_full, work.at[:, :, :, :, pl.ds(0, MIX_COLS)], local.at[0])
+    load.start()
+    load_tokens = pltpu.make_async_copy(tokens.at[p.y], own_tokens, local.at[1])
+    load_tokens.start()
+    others_y = [{"tensor": lax.rem(p.y + d, 4)} for d in (1, 2, 3)]
+    others_z = [{"dp": lax.rem(p.z + d, 4)} for d in (1, 2, 3)]
+    greet([p.seq_at(d) for d in range(1, 8)] + others_y + others_z)
+    ahead = Reduce(links, p, out_part, far_b, near_b)
+    ahead.send_far()
+    ahead.send_near()
+    load.wait()
+    rows_low = d_after_low.reshape(TOKENS, WIDTH)
     for start, size in ((0, 256), (256, 256), (512, 128)):
-        weights = mix_full[:, :, :, :, 2 * CHAN + start : 2 * CHAN + start + size].reshape(WIDTH, size)
-        d_mixed[:, start : start + size] = dot(d_after_low[...], weights)
+        weights = work[:, :, :, :, 2 * CHAN + start : 2 * CHAN + start + size].reshape(WIDTH, size)
+        d_mixed[:, start : start + size] = dot(rows_low[...], weights)
     small[...] = jnp.zeros_like(small)
     totals[...] = jnp.zeros_like(totals)
+    gain_in[...] = jnp.zeros_like(gain_in)
     offset = p.s * SPAN
 
     def chunk(i):
@@ -717,6 +991,7 @@
 
     lax.fori_loop(0, ROWS * GROUPS, states_back, 0)
     keys = [links.go(totals, totals_in.at[p.s], p.seq_at(d)) for d in range(1, 8)]
+    ahead.merge()
     state = jnp.zeros((ROWS, CHAN), F32)
     for d in range(1, 8):
         links.arrived(totals_in.at[p.seq_at(-d)["seq"]], keys[d - 1], p.seq_at(-d))
@@ -747,14 +1022,25 @@
         d_one = fed * conv * gate_i * (1.0 - gate_i)
         d_gates[rows, pl.ds(pl.multiple_of(g * LANES, LANES), LANES)] = d_zero.astype(BF16)
         d_gates[rows, pl.ds(pl.multiple_of(CHAN + g * LANES, LANES), LANES)] = d_one.astype(BF16)
-        d_conv[rows, at] = fed * gate_i
+        tail_a[rows, at] = fed * gate_i
         small[5:6, at] += jnp.sum(d_zero, axis=0, keepdims=True)
         small[6:7, at] += jnp.sum(d_one, axis=0, keepdims=True)
         small[7:8, at] += jnp.sum(d_log * (-rate_scale * gate_d), axis=0, keepdims=True)
         return carry
 
     lax.fori_loop(0, ROWS * GROUPS, gates_back, 0)
-
+    ahead.settle()
+
+    def ahead_rows(k, carry):
+        at = pl.ds(pl.multiple_of(k * 16, 16), 16)
+        block_out[p.y, at, :] = (after_own[at, :] + own_sum(ahead, at)).astype(BF16)
+        return carry
+
+    lax.fori_loop(0, SPAN // 16, ahead_rows, 0)
+    spread_b = Spread(links, p, block_out)
+    spread_b.start()
+
+    d_conv = tail_a
     held = None
     for g in range(GROUPS):
         total = d_conv[:, g * LANES : (g + 1) * LANES]
@@ -769,6 +1055,8 @@
             held = product[:, LANES:]
         d_conv[:, g * LANES : (g + 1) * LANES] = total
 
+    body = d_mixed
+
     def conv_back(i, carry):
         r, g, at, rows, row = chunk(i)
         d_chunk = d_conv[rows, at]
@@ -778,15 +1066,17 @@
         head = jnp.zeros((8, LANES), F32)
         total = jnp.zeros((SPAN, LANES), F32)
         for k in range(CONV):
-            ahead = CONV - 1 - k
-            same = (place - ahead >= begin) == here
+            before = CONV - 1 - k
+            same = (place - before >= begin) == here
             kept = jnp.where(same, d_chunk, 0.0)
-            value = ext[r, PAD - ahead : PAD - ahead + SPAN, at]
+            value = ext[r, PAD - before : PAD - before + SPAN, at]
             small[k : k + 1, at] += jnp.sum(kept * value, axis=0, keepdims=True)
             term = kept * vectors[k : k + 1, at]
-            if ahead:
-                total = total + jnp.where(row < SPAN - ahead, pltpu.roll(term, SPAN - ahead, 0), 0.0)
-                head = head + jnp.where(row[0:8] >= 8 - ahead, pltpu.roll(term[0:8], 8 - ahead, 0), 0.0)
+            if before:
+                total = total + jnp.where(row < SPAN - before, pltpu.roll(term, SPAN - before, 0), 0.0)
+                head = head + jnp.where(
+                    row[0:8] >= 8 - before, pltpu.roll(term[0:8], 8 - before, 0), 0.0
+                )
             else:
                 total = total + term
         small[4:5, at] += jnp.sum(d_chunk, axis=0, keepdims=True)
@@ -796,11 +1086,7 @@
 
     lax.fori_loop(0, ROWS * GROUPS, conv_back, 0)
     k_rim = links.go(rim_send, rim_recv, p.seq_at(-1))
-    for j in range(2):
-        for h in range(HEADS):
-            lo = h * LANES
-            product = dot_tn(conv_low[:, lo : lo + 256], d_gates[:, j * CHAN + lo : j * CHAN + lo + 256])
-            d_blocks[j, h] = product[32 * h : 32 * h + BLK, :]
+    spread_b.forward()
     links.arrived(rim_recv, k_rim, p.seq_at(1))
     for r in range(ROWS):
         last = r * SPAN + SPAN - 8
@@ -809,124 +1095,170 @@
         d_both[r * SPAN : (r + 1) * SPAN, CHAN:] = body[r * SPAN : (r + 1) * SPAN, :].astype(BF16)
 
     def first_part(n, carry):
-        weights = mix_full[lax.div(n, 2), lax.rem(n, 2), :, :, 0 : 2 * CHAN].reshape(256, 2 * CHAN)
-        d_first[:, pl.ds(pl.multiple_of(n * 256, 256), 256)] = dot_nt(d_both[...], weights).astype(BF16)
+        weights = work[lax.div(n, 2), lax.rem(n, 2), :, :, 0 : 2 * CHAN].reshape(256, 2 * CHAN)
+        product = dot_nt(d_both[...], weights).astype(BF16)
+        d_first[:, :, pl.ds(pl.multiple_of(n * 256, 256), 256)] = product.reshape(ROWS, SPAN, 256)
         return carry
 
     lax.fori_loop(0, 8, first_part, 0)
+    back = Reduce(links, p, d_first, far_a, near_a)
+    back.send_far()
+    back.send_near()
+
+    def weight_grads(n):
+        at = pl.ds(pl.multiple_of(n * 256, 256), 256)
+        to = work.at[lax.div(n, 2), lax.rem(n, 2)]
+        both = dot_tn(normed_in[:, at], d_both[...])
+        to[:, :, 0 : 2 * CHAN] = both.astype(BF16).reshape(4, 64, 2 * CHAN)
+        out = dot_tn(rows_low[:, at], mixed[...])
+        to[:, :, 2 * CHAN : MIX_COLS] = out.astype(BF16).reshape(4, 64, CHAN)
+
+    def blocks(j, h):
+        lo = h * LANES
+        product = dot_tn(conv_low[:, lo : lo + 256], d_gates[:, j * CHAN + lo : j * CHAN + lo + 256])
+        for q in range(BLK // 32):
+            row = (j * HEADS + h) * BLK + 32 * q
+            n, inner = row // 64, row % 64
+            piece = product[32 * (h + q) : 32 * (h + q + 1), :].astype(BF16)
+            work[n // 8, (n // 4) % 2, n % 4, inner : inner + 32, MIX_COLS:] = piece
+
+    for j in range(2):
+        for h in range(HEADS):
+            blocks(j, h)
+    for n in range(20, 32):
+        work[n // 8, (n // 4) % 2, n % 4, :, MIX_COLS:] = jnp.zeros((64, SMALL), BF16)
+    for k, n in enumerate((20, 21, 22)):
+        width = min(256, CHAN - 256 * k)
+        both = jnp.concatenate([small[:, 256 * k : 256 * k + width], jnp.zeros((8, width), F32)], axis=0)
+        work[n // 8, (n // 4) % 2, n % 4, 0:16, MIX_COLS : MIX_COLS + width] = both.astype(BF16)
+    scatter = Scatter(links, p, work, sib, far_s, near_s, half_a, half_b, far_2, near_2)
+
+    def give(xx, carry):
+        weight_grads(xx * 2 + 1 - p.c)
+        return carry
+
+    def keep(xx, carry):
+        weight_grads(xx * 2 + p.c)
+        return carry
+
+    lax.fori_loop(0, 4, give, 0)
+    for xx in range(4):
+        scatter.give(xx)
+    back.merge()
+    lax.fori_loop(0, 4, keep, 0)
+    for xx in range(4):
+        scatter.take(xx)
+    scatter.first()
+    back.settle()
+    load_tokens.wait()
+    gain = gain_rows[0:1, :].astype(F32)
+
+    def back_rows(k, carry):
+        at = pl.ds(pl.multiple_of(k * 16, 16), 16)
+        through, share = norm_back_rows(own_sum(back, at), own_tokens[at, :].astype(F32), gain)
+        gain_in[...] += share[0:8] + share[8:16]
+        grad_tokens[p.y, at, :] = (d_after_own[at, :] + through).astype(BF16)
+        return carry
+
+    lax.fori_loop(0, SPAN // 16, back_rows, 0)
+    spread_a = Spread(links, p, grad_tokens)
+    spread_a.start()
+    gain_y[p.y] = jnp.concatenate(
+        [jnp.sum(gain_in[...], axis=0, keepdims=True), jnp.sum(gain_mid[...], axis=0, keepdims=True)], axis=0
+    )
+    y_keys = [links.go(gain_y.at[p.y], gain_y.at[p.y], device) for device in others_y]
+    scatter.merge()
+    for d in (1, 2, 3):
+        links.arrived(gain_y.at[lax.rem(p.y + 4 - d, 4)], y_keys[d - 1], others_y[0])
+    gain_z[p.z] = gain_y[0] + gain_y[1] + gain_y[2] + gain_y[3]
+    z_keys = [links.go(gain_z.at[p.z], gain_z.at[p.z], device) for device in others_z]
+    scatter.turn()
+    for d in (1, 2, 3):
+        links.arrived(gain_z.at[lax.rem(p.z + 4 - d, 4)], z_keys[d - 1], others_z[0])
+    gain_s[p.s] = gain_z[0] + gain_z[1] + gain_z[2] + gain_z[3]
+    s_keys = [links.go(gain_s.at[p.s], gain_s.at[p.s], p.seq_at(d)) for d in range(1, 8)]
+    spread_a.forward()
+    scatter.merge_2()
+    for d in range(1, 8):
+        links.arrived(gain_s.at[p.seq_at(-d)["seq"]], s_keys[d - 1], p.seq_at(-d))
+    total = gain_s[0]
+    for s in range(1, 8):
+        total = total + gain_s[s]
+    gain_sums[...] = total
+
+    def store(base, value):
+        grad_mix[base : base + 32, :] = value[:, :MIX_COLS]
+        small_all[p.x, p.c, p.z, base : base + 32, :] = value[:, MIX_COLS:].astype(BF16)
+
+    scatter.finish(store)
+    small_gather = Gather(links, p, small_all)
+    small_gather.first()
+    spread_b.near()
+    spread_b.far()
+    small_gather.middle()
+    small_gather.finish()
+    small_gather.second()
+    small_gather.middle()
+    small_gather.finish()
+    small_gather.settle()
+    for k, n in enumerate((20, 21, 22)):
+        width = min(256, CHAN - 256 * k)
+        value = small_all[n // 8, (n // 4) % 2, n % 4, 0:16, 0:width].astype(F32)
+        small_sums[:, 256 * k : 256 * k + width] = value[0:8]
+    for n in range(20):
+        value = small_all[n // 8, (n // 4) % 2, n % 4].astype(F32)
+        block_sums[64 * n : 64 * (n + 1), :] = value
+    spread_a.near()
+    spread_a.far()
     links.drain()
 
 
-def mix_back(d_after_low, saved, doc_start, vectors, gate_w):
+def back_all(*operands):
     shape = jax.ShapeDtypeStruct
     tc = (TOKENS, CHAN)
+    pair = [pltpu.VMEM((2, SPAN, HALF), BF16), pltpu.VMEM((2, SPAN, WIDTH), BF16)]
     return pl.pallas_call(
-        mix_back_kernel,
+        back_kernel,
         out_shape=[
-            shape((TOKENS, 2 * CHAN), BF16),
-            shape((TOKENS, WIDTH), BF16),
+            shape((ROWS, SPAN, WIDTH), BF16),
+            shape((ROWS, SPAN, WIDTH), BF16),
+            shape((64, MIX_COLS), F32),
             shape((8, CHAN), F32),
-            shape((2, HEADS, BLK, 256), F32),
+            shape((2 * HEADS * BLK, 256), F32),
+            shape((2, WIDTH), F32),
         ],
-        in_specs=[vmem()] * 9 + [pl.BlockSpec(memory_space=pltpu.SMEM)] + [vmem()] * 2,
-        out_specs=[vmem()] * 4,
+        in_specs=[vmem(), anyspace()] + [vmem()] * 10 + [anyspace()] + [vmem()] * 6 + [smem()],
+        out_specs=[vmem()] * 6,
         scratch_shapes=[
+            pltpu.VMEM((4, 2, 4, 64, RS_COLS), BF16),
+            pltpu.VMEM((SPAN, WIDTH), BF16),
             pltpu.VMEM(tc, F32),
             pltpu.VMEM(tc, F32),
             pltpu.VMEM((TOKENS, 2 * CHAN), BF16),
-            pltpu.VMEM(tc, F32),
-            pltpu.VMEM(tc, F32),
+            pltpu.VMEM((TOKENS, 2 * CHAN), BF16),
+            pltpu.VMEM((ROWS, SPAN, WIDTH), BF16),
+            pltpu.VMEM((8, CHAN), F32),
             pltpu.VMEM((ROWS, PAD, CHAN), F32),
             pltpu.VMEM((ROWS, PAD, CHAN), F32),
             pltpu.VMEM((8, CHAN), F32),
             pltpu.VMEM((8, 8, CHAN), F32),
             pltpu.VMEM((8, CHAN), F32),
-            pltpu.SemaphoreType.DMA((8,)),
-            pltpu.SemaphoreType.DMA((8,)),
+        ]
+        + pair * 2
+        + Scatter.scratch(RS_COLS)
+        + [
+            pltpu.VMEM((4, 2, 4, 64, SMALL), BF16),
+            pltpu.VMEM((8, WIDTH), F32),
+            pltpu.VMEM((4, 2, WIDTH), F32),
+            pltpu.VMEM((8, 2, WIDTH), F32),
+            pltpu.VMEM((4, 2, WIDTH), F32),
+            pltpu.SemaphoreType.DMA((2,)),
+            pltpu.SemaphoreType.DMA((144,)),
+            pltpu.SemaphoreType.DMA((144,)),
         ],
         compiler_params=params(2),
-        name="mix_back",
-    )(d_after_low, *saved, doc_start, vectors, gate_w)
-
-
-def ends_kernel(
-    first_part,
-    out_part,
-    tokens,
-    after_own,
-    d_after_own,
-    gains,
-    grad_tokens,
-    block_out,
-    gain_in,
-    far_a,
-    near_a,
-    far_b,
-    near_b,
-    send,
-    recv,
-):
-    p = Place()
-    links = Links(send, recv)
-    greet([p.YR, p.YL])
-    back = Reduce(links, p, first_part, far_a, near_a)
-    ahead = Reduce(links, p, out_part, far_b, near_b)
-    back.send_far()
-    back.send_near()
-    ahead.send_far()
-    ahead.send_near()
-    gain_in[...] = jnp.zeros_like(gain_in)
-    back.merge()
-    back.settle()
-
-    def back_rows(k, carry):
-        at = pl.ds(pl.multiple_of(k * 16, 16), 16)
-        through, share = norm_back_rows(
-            own_sum(back, at), tokens[p.y, at, :].astype(F32), gains[0:1, :]
-        )
-        gain_in[...] += share[0:8] + share[8:16]
-        grad_tokens[p.y, at, :] = (d_after_own[at, :] + through).astype(BF16)
-        return carry
-
-    lax.fori_loop(0, SPAN // 16, back_rows, 0)
-    spread_a = Spread(links, p, grad_tokens)
-    spread_a.start()
-    ahead.merge()
-    ahead.settle()
-
-    def ahead_rows(k, carry):
-        at = pl.ds(pl.multiple_of(k * 16, 16), 16)
-        block_out[p.y, at, :] = (after_own[at, :] + own_sum(ahead, at)).astype(BF16)
-        return carry
-
-    lax.fori_loop(0, SPAN // 16, ahead_rows, 0)
-    spread_b = Spread(links, p, block_out)
-    spread_b.start()
-    spread_a.forward()
-    spread_b.forward()
-    spread_a.near()
-    spread_a.far()
-    spread_b.near()
-    spread_b.far()
-    links.drain()
-
-
-def ends(first_part, out_part, tokens, after_own, d_after_own, gains):
-    shape = jax.ShapeDtypeStruct
-    half = [pltpu.VMEM((2, SPAN, HALF), BF16), pltpu.VMEM((2, SPAN, WIDTH), BF16)]
-    return pl.pallas_call(
-        ends_kernel,
-        out_shape=[
-            shape((ROWS, SPAN, WIDTH), BF16),
-            shape((ROWS, SPAN, WIDTH), BF16),
-            shape((8, WIDTH), F32),
-        ],
-        in_specs=[vmem()] * 6,
-        out_specs=[vmem()] * 3,
-        scratch_shapes=half * 2 + [pltpu.SemaphoreType.DMA((24,)), pltpu.SemaphoreType.DMA((24,))],
-        compiler_params=params(3),
-        name="ends",
-    )(first_part, out_part, tokens, after_own, d_after_own, gains)
+        name="back_all",
+    )(*operands)
 
 
 def per_device(
@@ -947,21 +1279,6 @@
     mlp_out,
     cotangent,
 ):
-    gains = norm_gains.astype(F32)
-    keep = (1 - fresh_rows).astype(F32)
-    decay_float = decay_param.astype(F32)
-    mix_shard = jnp.concatenate([mix_in[0], mix_in[1], mix_out.T], axis=1)
-    mlp_shard = jnp.concatenate([mlp_in[0], mlp_in[1], mlp_out.T], axis=1)
-    conv_start = jnp.pad(conv_state.astype(F32) * keep[:, None, None], ((0, 0), (PAD - 3, 0), (0, 0)))
-    vectors = jnp.concatenate(
-        [
-            conv_weight.astype(F32),
-            conv_bias.astype(F32)[None],
-            gate_bias.astype(F32),
-            (-rate_scale * jax.nn.softplus(decay_float))[None],
-        ],
-        axis=0,
-    )
     gate_w = jnp.stack(
         [
             jnp.pad(gate_blocks[:, h], ((0, 0), (32 * h, 96 - 32 * h), (32 * h, 96 - 32 * h)))
@@ -969,7 +1286,6 @@
         ],
         axis=1,
     )
-    rows = tokens.reshape(TOKENS, WIDTH)
     (
         mix_full,
         mlp_full,
@@ -982,58 +1298,60 @@
         mixed,
         normed_in,
         entering,
+        vectors,
         normed_mid,
         after_own,
     ) = mix_forward(
-        rows, mix_shard, mlp_shard, init_state * keep[:, None], conv_start, doc_start, gains, vectors, gate_w
-    )
-    normed_mid = normed_mid.reshape(TOKENS, WIDTH)
-    mlp_w = mlp_full.reshape(WIDTH, MLP_COLS)
-    upstream = cotangent.reshape(TOKENS, WIDTH)
-
-    gate_in = dot(normed_mid, mlp_w[:, :MLP])
-    up_in = dot(normed_mid, mlp_w[:, MLP : 2 * MLP])
-    d_hidden = dot(upstream, mlp_w[:, 2 * MLP :])
-    act, slope = gelu_pair(gate_in)
-    hidden = (act * up_in).astype(BF16)
-    d_gate_up = jnp.concatenate(
-        [(d_hidden * up_in * slope).astype(BF16), (d_hidden * act).astype(BF16)], axis=1
-    )
-    mid_part = dot_nt(d_gate_up, mlp_w[:, : 2 * MLP]).astype(BF16)
-    out_part = dot_nt(hidden, mlp_w[:, 2 * MLP :]).astype(BF16)
-    grad_mlp = jnp.concatenate(
-        [dot_tn(normed_mid, d_gate_up).astype(BF16), dot_tn(upstream, hidden).astype(BF16)], axis=1
-    )
-    grad_mlp = lax.psum_scatter(grad_mlp, ("seq", "dp"), scatter_dimension=0, tiled=True).astype(F32)
-
-    d_after_low, d_after_own, gain_mid = mid_back(
-        mid_part.reshape(ROWS, SPAN, WIDTH), after_own, cotangent, gains
-    )
-    d_after_rows = d_after_low.reshape(TOKENS, WIDTH)
-    d_both, d_first, small, d_blocks = mix_back(
-        d_after_rows,
-        (mix_full, states, pre, ext, decay_g, input_g, conv_low, entering),
+        tokens.reshape(TOKENS, WIDTH),
+        mix_in,
+        mix_out,
+        mlp_in,
+        mlp_out,
+        init_state,
+        conv_state,
+        fresh_rows,
         doc_start,
-        vectors,
+        norm_gains,
+        conv_weight,
+        conv_bias[None],
+        gate_bias,
+        decay_param[None],
         gate_w,
     )
-    grad_tokens, block_out, gain_in = ends(
-        d_first.reshape(ROWS, SPAN, WIDTH),
+    mid_part, out_part, grad_mlp = mlp_all(
+        normed_mid.reshape(TOKENS, WIDTH),
+        cotangent.reshape(TOKENS, WIDTH),
+        mlp_full.reshape(WIDTH, MLP_COLS),
+    )
+    grad_mlp = lax.psum_scatter(grad_mlp, ("seq", "dp"), scatter_dimension=0, tiled=True)
+    d_after_low, d_after_own, gain_mid = mid_back(
+        mid_part.reshape(ROWS, SPAN, WIDTH), after_own, cotangent, norm_gains
+    )
+    grad_tokens, block_out, grad_mix, small, blocks, grad_gains = back_all(
+        d_after_low,
+        mix_full,
+        states,
+        pre,
+        ext,
+        decay_g,
+        input_g,
+        conv_low,
+        entering,
+        mixed,
+        normed_in,
         out_part.reshape(ROWS, SPAN, WIDTH),
         tokens,
         after_own,
         d_after_own,
-        gains,
+        gain_mid,
+        norm_gains,
+        vectors,
+        gate_w,
+        doc_start,
     )
-    grad_mix = jnp.concatenate(
-        [dot_tn(normed_in, d_both).astype(BF16), dot_tn(d_after_rows, mixed).astype(BF16)], axis=1
-    )
-    grad_mix = lax.psum_scatter(grad_mix, ("seq", "dp"), scatter_dimension=0, tiled=True).astype(F32)
-    blocks = jnp.stack([d_blocks[:, h, :, 32 * h : 32 * h + BLK] for h in range(HEADS)], axis=1)
-    small = lax.psum(small.astype(BF16), ("seq", "dp")).astype(F32)
-    blocks = lax.psum(blocks.astype(BF16), ("seq", "dp")).astype(F32)
-    grad_gains = jnp.stack([jnp.sum(gain_in, axis=0), jnp.sum(gain_mid, axis=0)])
-    grad_gains = lax.psum(grad_gains.astype(BF16), ("seq", "dp", "tensor")).astype(F32)
+    blocks = blocks.reshape(2, HEADS, BLK, 256)
+    blocks = jnp.stack([blocks[:, h, :, 32 * h : 32 * h + BLK] for h in range(HEADS)], axis=1)
+    grad_mlp = grad_mlp.astype(F32).reshape(64, CHUNKS, 3, CHUNK)
     return (
         block_out,
         states.reshape(ROWS, SPAN, CHAN),
@@ -1045,9 +1363,9 @@
         small[4],
         blocks,
         small[5:7],
-        small[7] * jax.nn.sigmoid(decay_float),
-        jnp.stack([grad_mlp[:, :MLP], grad_mlp[:, MLP : 2 * MLP]]),
-        grad_mlp[:, 2 * MLP :].T,
+        small[7] * jax.nn.sigmoid(decay_param.astype(F32)),
+        grad_mlp[:, :, 0:2].transpose(2, 0, 1, 3).reshape(2, 64, MLP),
+        grad_mlp[:, :, 2].transpose(1, 2, 0).reshape(MLP, 64),
     )
 
 

time: 634 us -> 379 us (0.60); the launches traced: 626 us -> 379 us
  blocking collectives: 192 us -> 0 us
  matrix products: 60.9 us -> 0 us
  Pallas kernels: 286 us -> 338 us
  other arithmetic: 40.2 us -> 3.66 us
  local copies, waits for them, and re-layouts: 30.7 us -> 23.1 us
    psum x2 -> x0, blocking collectives: 192 us -> none  [the longest x1 124 us: per_device(): small = lax.psum(small.astype(BF16), ('seq', 'dp')).astype(F32)]
    dot_general x9 -> x0, matrix products: 60.9 us -> none  [the longest x4 23.7 us: dot_tn(): lax.dot_general(a, b, (((0,), (0,)), ((), ())), preferred_element_type=F32)]
    pallas_call x3, Pallas kernels: 244 us -> 295 us  [the longest x1 129 us: mix_forward(): pl.pallas_call(mix_forward_kernel, out_shape=outs, in_specs=[vmem()] * 7...]
    concatenate x5 -> x0, other arithmetic: 23.8 us -> none  [the longest x1 14.5 us: per_device(): jnp.concatenate([dot_tn(normed_mid, d_gate_up).astype(BF16), dot_tn(upstr...]
    unnamed x41 -> x26, local copies, waits for them, and re-layouts: 22.9 us -> 10.2 us
    convert_element_type x11 -> x0, other arithmetic: 8.23 us -> none  [the longest x1 2.26 us: per_device(): blocks = lax.psum(blocks.astype(BF16), ('seq', 'dp')).astype(F32)]
  transfers between devices with their start and end apart: 3 -> 1, of which waited for: 0 -> 0; matrix products, arithmetic and copies ran while one was open for 12% -> 2% of each run, Pallas kernels for 12% -> 43%
where the time goes in v2:
time: 379 us
  Pallas kernels  338 us (89%)
  local copies, waits for them, and re-layouts  23.1 us (6%)
  between operations  14.2 us (4%)
    pallas_call x1, Pallas kernels, mix_forward(): pl.pallas_call(mix_forward_kernel, out_shape=outs, in_specs=[vmem()] * 7...  129 us
    pallas_call x1, Pallas kernels, back_all(): pl.pallas_call(back_kernel, out_shape=[shape((ROWS, SPAN, WIDTH), BF16),...  118 us
    pallas_call x1, Pallas kernels, mlp_all(): pl.pallas_call(mlp_kernel, grid=(CHUNKS,), out_shape=[shape((TOKENS, WIDT...  47.6 us
    pallas_call x1, Pallas kernels, mid_back(): pl.pallas_call(mid_back_kernel, out_shape=[shape((ROWS, SPAN, WIDTH), BF1...  42.9 us
    unnamed x26, local copies, waits for them, and re-layouts  10.2 us
  transfers between devices with their start and end apart: 1, of which 0 were waited for; matrix products, arithmetic and copies ran while one was open for 2% of the time, Pallas kernels for 43%

profile of v2, /device:TPU:1, one launch (start us, length us, event | category | flops | bytes accessed | tf_op | source)
XLA Modules:
  0.0 378.5 jit_solution(9586315698206155783)
XLA Ops:
  7.3 1.2 slice_bitcast_fusion.7
  8.5 1.9 copy.42.mlp_out
  10.3 0.8 copy.41.mix_out
  11.1 0.6 copy.43.conv_state
  11.8 0.6 broadcast_in_dim.6.conv_bias
  12.3 0.6 broadcast_in_dim.7.decay_param
  13.0 0.2 pad_bitcast_fusion
  13.2 1.1 pad_maximum_fusion.1.gate_w
  14.3 128.8 %mix_forward.1 = (bf16[4,2,4,64,1920]{4,3,2,1,0:T(8,128)(2,1)}, bf16[4,2,4,64,4608]{4,3,2,1,0:T(8,128)(2,1)}, f32[512,640]{1,0:T(8,128)}, f32[512,640]{1,0:T(8,1...) custom-call(bf16[512,2048]{1,0:T(8,128)(2,1)} %bitcast.47, ...), custom_call_target="tpu_custom_call" | custom-call | tf_op jit(solution)/shard_map/mix_forward/pallas_call | solution.py:625
  143.1 47.6 %mlp_all.1 = (bf16[512,2048]{1,0:T(8,128)(2,1)}, bf16[512,2048]{1,0:T(8,128)(2,1)}, bf16[2048,4608]{1,0:T(8,128)(2,1)}) custom-call(bf16[512,2048]{1,0:T(8,128)(2,1)} %bitcast.56, bf16[512,2048]{1,0:T(8,128)(2,1)} %bitcast.49, bf16[2048,4608]{1,0:T(8,128)(2,1)} %bitcast.55), custom_call_target="tpu_custom_call" | custom-call | flops 28991029248 | bytes 37748736 | tf_op jit(solution)/shard_map/mlp_all/pallas_call | solution.py:749
  190.8 42.9 %mid_back.1 = (bf16[4,128,2048]{2,1,0:T(8,128)(2,1)}, f32[128,2048]{1,0:T(8,128)}, f32[8,2048]{1,0:T(8,128)}) custom-call(bf16[4,128,2048]{2,1,0:T(8,128)(2,1)} %bitcast.51, f32[128,2048]{1,0:T(8,128)} %get-tuple-element.42.after_own, bf16[4,128,2048]{2,1,0:T(8,128)(2,1)} %upstream.1, bf16[2,2048]{1,0:T(2,128)(2,1)} %gain_rows.5), custom_call_target="tpu_custom_call" | custom-call | tf_op jit(solution)/shard_map/mid_back/pallas_call | solution.py:683
  233.7 118.2 %back_all.1 = (bf16[4,128,2048]{2,1,0:T(8,128)(2,1)}, bf16[4,128,2048]{2,1,0:T(8,128)(2,1)}, f32[64,1920]{1,0:T(8,128)}, f32[8,640]{1,0:T(8,128)}, f32[1280,256]{1,0:T(8,128)}, /*index=5*/f32[2,2048]{1,0:T(2,128)}) custom-call(bf16[4,128,2048]{2,1,0:T(8,128)(2,1)} %get-tuple-element.43.d_after_low, bf16[4,2,4,64,1920]{4,3,2,1,0:T(8,128)(2,1)} %get-tuple-element.44.mix_full, ...), custom_call_target="tpu_custom_call" | custom-call | tf_op jit(solution)/shard_map/back_all/pallas_call | solution.py:1220
  351.9 1.4 slice.58
  353.3 1.3 slice.64
  354.6 1.4 slice_reduce_fusion
  356.0 1.8 slice_bitcast_fusion.1
  357.8 0.7 pad_maximum_fusion.2
  358.6 0.3 fusion
  358.9 1.2 pad_maximum_fusion
  360.1 0.6 divide_multiply_fusion
  360.7 2.0 reshape.75
  362.7 0.3 slice_bitcast_fusion
  363.0 0.4 slice.73
  363.4 0.1 copy.44
  363.6 1.1 reshape.72
  364.8 0.9 copy.52
  365.6 1.3 copy.57
  367.0 0.8 copy-done
  367.7 1.1 copy.58
  368.8 1.0 copy-done.1
  369.8 1.3 copy.59
  371.1 0.6 copy.60
  (21 shorter events, 0.3 us)
Async XLA Ops:
  7.2 3.1 copy-start.4
  7.2 3.9 %copy-start.6 = (bf16[4,3,640]{2,0,1:T(4,128)(2,1)S(1)}, bf16[4,3,640]{2,0,1:T(4,128)(2,1)}, u32[]{:S(2)}) copy-start(bf16[4,3,640]{2,0,1:T(4,128)(2,1)} %param.18) | copy-start | bytes 46084
  7.2 4.6 %copy-start.8 = (bf16[640]{0:T(1024)(128)(2,1)S(1)}, bf16[640]{0:T(1024)(128)(2,1)}, u32[]{:S(2)}) copy-start(bf16[640]{0:T(1024)(128)(2,1)} %param.25) | copy-start | bytes 3844
  7.2 5.1 %copy-start.7 = (bf16[640]{0:T(1024)(128)(2,1)S(1)}, bf16[640]{0:T(1024)(128)(2,1)}, u32[]{:S(2)}) copy-start(bf16[640]{0:T(1024)(128)(2,1)} %param.28) | copy-start | bytes 3844
  7.2 353.5 %reduce-scatter.2.cloned.1.call-start = ((), (), s32[]{:S(2)}) async-start(), calls=%async_computation.1 | async-start | bytes 19464192 | tf_op jit(solution)/shard_map/reduce_scatter | solution.py:1326
  351.9 6.7 %copy-start.3 = (f32[1280,256]{1,0:T(8,128)S(1)}, f32[1280,256]{1,0:T(8,128)}, u32[]{:S(2)}) copy-start(f32[1280,256]{1,0:T(8,128)} %get-tuple-element.63) | copy-start | bytes 3932164
  363.5 2.1 copy-start.2
  365.6 2.1 copy-start
  367.7 2.1 copy-start.1
  369.8 1.3 copy-start.5
Sparse Core Ops, SparseCore 0:
  190.9 131.5 reduce-scatter.1

commit v3 on v2

--- a/solution.py
+++ b/solution.py
@@ -26,7 +26,6 @@
 CHUNK = 256
 CHUNKS = MLP // CHUNK
 SMALL = 256
-RS_COLS = MIX_COLS + SMALL
 LANES = 128
 GROUPS = CHAN // LANES
 PAD = 8
@@ -170,15 +169,15 @@
     def __init__(self, links, place, part, far, near):
         self.links, self.p, self.part, self.far, self.near = links, place, part, far, near
 
-    def send_far(self):
-        p, part = self.p, self.part
+    def send_first(self):
+        p, part, near = self.p, self.part, self.near
         self.k0 = self.links.go(part.at[p.y2, :, CA], self.far.at[0], p.YR)
+        self.k3 = self.links.go(part.at[p.yl, :, CA], near.at[1, :, CA], p.YL)
+
+    def send_second(self):
+        p, part, near = self.p, self.part, self.near
         self.k1 = self.links.go(part.at[p.y2, :, CB], self.far.at[1], p.YL)
-
-    def send_near(self):
-        p, part, near = self.p, self.part, self.near
         self.k2 = self.links.go(part.at[p.yr, :, CB], near.at[0, :, CB], p.YR)
-        self.k3 = self.links.go(part.at[p.yl, :, CA], near.at[1, :, CA], p.YL)
 
     def merge(self):
         p, part, near, far = self.p, self.part, self.near, self.far
@@ -293,11 +292,10 @@
     return jnp.sum(jnp.where(row == r, ref[:, at], 0.0), axis=0, keepdims=True)
 
 
-def assemble_vectors(vectors, conv_weight, conv_bias, gate_bias, decay_param):
-    vectors[0:4, :] = conv_weight[...].astype(F32)
-    vectors[4:5, :] = conv_bias[...].astype(F32)
-    vectors[5:7, :] = gate_bias[...].astype(F32)
-    vectors[7:8, :] = -rate_scale * jnp.log1p(jnp.exp(decay_param[...].astype(F32)))
+def assemble_vectors(vectors, raw):
+    value = raw[...].astype(F32)
+    row = lax.broadcasted_iota(jnp.int32, value.shape, 0)
+    vectors[...] = jnp.where(row == 7, -rate_scale * jnp.log1p(jnp.exp(jnp.where(row == 7, value, 0.0))), value)
 
 
 def mix_forward_kernel(
@@ -311,10 +309,7 @@
     fresh_rows,
     doc_start,
     gain_rows,
-    conv_weight,
-    conv_bias,
-    gate_bias,
-    decay_param,
+    raw_vectors,
     gate_w,
     mix_full_out,
     mlp_full,
@@ -361,20 +356,21 @@
     mine = mix_full.at[p.x, p.c, p.z]
     for j in range(2):
         mine[:, j * CHAN : (j + 1) * CHAN] = mix_in[j]
-    mine[:, 2 * CHAN :] = mix_out[...].astype(F32).T.astype(BF16)
+    mine[:, 2 * CHAN :] = mix_out[...]
     greet([p.seq_at(d) for d in range(1, 8)] + [p.ZR, p.ZL, p.YR, p.YL])
-    mix_gather = Gather(links, p, mix_full)
-    mix_gather.first()
-    down = mlp_out[...].astype(F32).T.astype(BF16)
+    in_gather = Gather(links, p, mix_full.at[:, :, :, :, pl.ds(0, 2 * CHAN)])
+    out_gather = Gather(links, p, mix_full.at[:, :, :, :, pl.ds(2 * CHAN, CHAN)])
+    mlp_gather = Gather(links, p, mlp_full)
+    in_gather.first()
     for f in range(CHUNKS):
         lo, to = f * CHUNK, 3 * f * CHUNK
         mlp_own[:, to : to + CHUNK] = mlp_in[0, :, lo : lo + CHUNK]
         mlp_own[:, to + CHUNK : to + 2 * CHUNK] = mlp_in[1, :, lo : lo + CHUNK]
-        mlp_own[:, to + 2 * CHUNK : to + 3 * CHUNK] = down[:, lo : lo + CHUNK]
+        mlp_own[:, to + 2 * CHUNK : to + 3 * CHUNK] = mlp_out[:, lo : lo + CHUNK]
     own_mlp = pltpu.make_async_copy(mlp_own, mlp_full.at[p.x, p.c, p.z], local.at[0])
     own_mlp.start()
     gains[...] = gain_rows[...].astype(F32)
-    assemble_vectors(vectors, conv_weight, conv_bias, gate_bias, decay_param)
+    assemble_vectors(vectors, raw_vectors)
 
     def norm_rows(first, last):
         def one(k, carry):
@@ -387,16 +383,22 @@
         lax.fori_loop(first, last, one, 0)
 
     norm_rows(0, 8)
-    mix_gather.middle()
-    mix_gather.finish()
-    mix_gather.second()
+    in_gather.middle()
+    in_gather.finish()
+    in_gather.second()
     own_mlp.wait()
     norm_rows(8, 16)
-    mix_gather.middle()
-    mlp_gather = Gather(links, p, mlp_full)
+    in_gather.middle()
+    out_gather.first()
     mlp_gather.first()
-    mix_gather.finish()
-    mix_gather.settle()
+    in_gather.finish()
+    out_gather.middle()
+    out_gather.finish()
+    out_gather.second()
+    mlp_gather.middle()
+    mlp_gather.finish()
+    mlp_gather.second()
+    in_gather.settle()
     saves = []
 
     def save(src, dst):
@@ -404,7 +406,6 @@
         copy.start()
         saves.append(copy)
 
-    save(mix_full, mix_full_out)
     save(normed_in, normed_in_out)
     save(vectors, vectors_out)
 
@@ -413,23 +414,22 @@
         pre[:, at] = dot(normed_in[...], mix_full[:, :, :, :, at].reshape(WIDTH, 256))
         return carry
 
-    lax.fori_loop(0, 5, project, 0)
-    mlp_gather.middle()
-    mlp_gather.finish()
-    mlp_gather.second()
-    save(pre.at[:, pl.ds(0, CHAN)], pre_out)
-
+    lax.fori_loop(2, 5, project, 0)
     for r in range(ROWS):
         ext[r, PAD:, :] = pre[r * SPAN : (r + 1) * SPAN, CHAN : 2 * CHAN].astype(BF16).astype(F32)
         rim_send[r] = ext[r, SPAN : SPAN + PAD, :]
     k_rim = links.go(rim_send, rim_recv, p.seq_at(1))
+    lax.fori_loop(0, 2, project, 0)
+    save(pre.at[:, pl.ds(0, CHAN)], pre_out)
     links.arrived(rim_recv, k_rim, p.seq_at(-1))
     at_start = p.s == 0
     for r in range(ROWS):
         keep = (1 - fresh_rows[r]).astype(F32)
         ext[r, 0:PAD, :] = jnp.where(at_start, 0.0, rim_recv[r])
-        first_rim = conv_state[r].astype(F32) * keep
-        ext[r, PAD - 3 : PAD, :] = jnp.where(at_start, first_rim, rim_recv[r, PAD - 3 : PAD, :])
+        for j in range(CONV - 1):
+            at = slice(PAD - 3 + j, PAD - 2 + j)
+            first_rim = conv_state[j, r : r + 1, :].astype(F32) * keep
+            ext[r, at, :] = jnp.where(at_start, first_rim, rim_recv[r, at, :])
     offset = p.s * SPAN
 
     def conv_chunk(i, carry):
@@ -485,6 +485,8 @@
     keys = [links.go(totals, totals_in.at[p.s], p.seq_at(d)) for d in range(1, 8)]
     save(decay_g, decay_out)
     save(input_g, input_out)
+    out_gather.middle()
+    out_gather.finish()
     row = lax.broadcasted_iota(jnp.int32, (ROWS, CHAN), 0)
     kept = jnp.zeros((ROWS, CHAN), F32)
     for r in range(ROWS):
@@ -513,23 +515,20 @@
     save(mixed, mixed_out)
     save(entering, entering_out)
 
-    def partial(row):
-        left = mixed[pl.ds(pl.multiple_of(row * SPAN, SPAN), SPAN), :]
-
-        def one(n, carry):
-            weights = mix_full[lax.div(n, 2), lax.rem(n, 2), :, :, 2 * CHAN :].reshape(256, CHAN)
-            part[row, :, pl.ds(pl.multiple_of(n * 256, 256), 256)] = dot_nt(left, weights).astype(BF16)
-            return carry
-
-        lax.fori_loop(0, 8, one, 0)
+    out_gather.settle()
+    save(mix_full, mix_full_out)
+
+    def partial(n, carry):
+        weights = mix_full[lax.div(n, 2), lax.rem(n, 2), :, :, 2 * CHAN :].reshape(256, CHAN)
+        product = dot_nt(mixed[...], weights).astype(BF16)
+        part[:, :, pl.ds(pl.multiple_of(n * 256, 256), 256)] = product.reshape(ROWS, SPAN, 256)
+        return carry
 
     reduce = Reduce(links, p, part, far, near)
-    partial(p.y2)
-    reduce.send_far()
-    partial(p.yr)
-    partial(p.yl)
-    reduce.send_near()
-    partial(p.y)
+    lax.fori_loop(0, 4, partial, 0)
+    reduce.send_first()
+    lax.fori_loop(4, 8, partial, 0)
+    reduce.send_second()
     mlp_gather.middle()
     reduce.merge()
     reduce.settle()
@@ -547,8 +546,8 @@
     lax.fori_loop(0, SPAN // 16, norm_mid, 0)
     spread = Spread(links, p, normed_mid)
     spread.start()
+    mlp_gather.finish()
     spread.forward()
-    mlp_gather.finish()
     spread.near()
     spread.far()
     mlp_gather.settle()
@@ -619,13 +618,13 @@
         pltpu.VMEM((2, SPAN, HALF), BF16),
         pltpu.VMEM((2, SPAN, WIDTH), BF16),
         pltpu.SemaphoreType.DMA((16,)),
-        pltpu.SemaphoreType.DMA((128,)),
-        pltpu.SemaphoreType.DMA((128,)),
+        pltpu.SemaphoreType.DMA((184,)),
+        pltpu.SemaphoreType.DMA((184,)),
     ]
     return pl.pallas_call(
         mix_forward_kernel,
         out_shape=outs,
-        in_specs=[vmem()] * 7 + [smem()] * 2 + [vmem()] * 6,
+        in_specs=[vmem()] * 7 + [smem()] * 2 + [vmem()] * 3,
         out_specs=[anyspace()] * 12 + [vmem()] * 2,
         scratch_shapes=scratch,
         compiler_params=params(0),
@@ -646,62 +645,8 @@
     return part[reduce.p.y, at, :].astype(F32) + near[0, at, :].astype(F32) + near[1, at, :].astype(F32)
 
 
-def mid_back_kernel(
-    part, after_own, upstream, gain_rows, d_after_low, d_after_own, gain_mid, far, near, send, recv
-):
-    p = Place()
-    links = Links(send, recv)
-    greet([p.YR, p.YL])
-    reduce = Reduce(links, p, part, far, near)
-    reduce.send_far()
-    reduce.send_near()
-    gain_mid[...] = jnp.zeros_like(gain_mid)
-    gain = gain_rows[1:2, :].astype(F32)
-    reduce.merge()
-    reduce.settle()
-
-    def one(k, carry):
-        at = pl.ds(pl.multiple_of(k * 16, 16), 16)
-        through, share = norm_back_rows(own_sum(reduce, at), after_own[at, :], gain)
-        gain_mid[...] += share[0:8] + share[8:16]
-        total = upstream[p.y, at, :].astype(F32) + through
-        d_after_own[at, :] = total
-        d_after_low[p.y, at, :] = total.astype(BF16)
-        return carry
-
-    lax.fori_loop(0, SPAN // 16, one, 0)
-    spread = Spread(links, p, d_after_low)
-    spread.start()
-    spread.forward()
-    spread.near()
-    spread.far()
-    links.drain()
-
-
-def mid_back(part, after_own, upstream, gains):
-    shape = jax.ShapeDtypeStruct
-    return pl.pallas_call(
-        mid_back_kernel,
-        out_shape=[
-            shape((ROWS, SPAN, WIDTH), BF16),
-            shape((SPAN, WIDTH), F32),
-            shape((8, WIDTH), F32),
-        ],
-        in_specs=[vmem()] * 4,
-        out_specs=[vmem()] * 3,
-        scratch_shapes=[
-            pltpu.VMEM((2, SPAN, HALF), BF16),
-            pltpu.VMEM((2, SPAN, WIDTH), BF16),
-            pltpu.SemaphoreType.DMA((12,)),
-            pltpu.SemaphoreType.DMA((12,)),
-        ],
-        compiler_params=params(1),
-        name="mid_back",
-    )(part, after_own, upstream, gains)
-
-
 def mlp_kernel(
-    normed, upstream, weights, mid_part, out_part, grads, normed_t, upstream_t, d_both, mid_sum, out_sum
+    normed, upstream, weights, mid_part, hidden_out, grads, normed_t, upstream_t, d_both, mid_sum
 ):
     step = pl.program_id(0)
 
@@ -715,7 +660,6 @@
 
         lax.fori_loop(0, WIDTH // 256, turn, 0)
         mid_sum[...] = jnp.zeros_like(mid_sum)
-        out_sum[...] = jnp.zeros_like(out_sum)
 
     gate = dot(normed[...], weights[:, 0:CHUNK])
     up = dot(normed[...], weights[:, CHUNK : 2 * CHUNK])
@@ -725,21 +669,20 @@
     d_both[:, 0:CHUNK] = (d_hidden * up * slope).astype(BF16)
     d_both[:, CHUNK : 2 * CHUNK] = (d_hidden * act).astype(BF16)
     d_both[:, 2 * CHUNK :] = hidden
+    hidden_out[...] = hidden
 
     def tile(n, carry):
         at = pl.ds(pl.multiple_of(n * 256, 256), 256)
         grads[at, 0 : 2 * CHUNK] = dot(normed_t[at, :], d_both[:, 0 : 2 * CHUNK]).astype(BF16)
         grads[at, 2 * CHUNK :] = dot(upstream_t[at, :], d_both[:, 2 * CHUNK :]).astype(BF16)
         mid_sum[:, at] += dot_nt(d_both[:, 0 : 2 * CHUNK], weights[at, 0 : 2 * CHUNK])
-        out_sum[:, at] += dot_nt(d_both[:, 2 * CHUNK :], weights[at, 2 * CHUNK :])
-        return carry
-
-    lax.fori_loop(0, WIDTH // 256, tile, 0)
+        return carry
+
+    lax.fori_loop(0, WIDTH // 256, tile, 0, unroll=2)
 
     @pl.when(step == CHUNKS - 1)
     def _():
         mid_part[...] = mid_sum[...].astype(BF16)
-        out_part[...] = out_sum[...].astype(BF16)
 
 
 def mlp_all(normed, upstream, weights):
@@ -751,21 +694,20 @@
         grid=(CHUNKS,),
         out_shape=[
             shape((TOKENS, WIDTH), BF16),
-            shape((TOKENS, WIDTH), BF16),
+            shape((TOKENS, MLP), BF16),
             shape((WIDTH, MLP_COLS), BF16),
         ],
         in_specs=[whole, whole, block],
-        out_specs=[whole, whole, block],
+        out_specs=[whole, pl.BlockSpec((TOKENS, CHUNK), lambda f: (0, f)), block],
         scratch_shapes=[
             pltpu.VMEM((WIDTH, TOKENS), BF16),
             pltpu.VMEM((WIDTH, TOKENS), BF16),
             pltpu.VMEM((TOKENS, 3 * CHUNK), BF16),
             pltpu.VMEM((TOKENS, WIDTH), F32),
-            pltpu.VMEM((TOKENS, WIDTH), F32),
         ],
         compiler_params=pltpu.CompilerParams(vmem_limit_bytes=VMEM_BYTES),
         cost_estimate=pl.CostEstimate(
-            flops=18 * TOKENS * WIDTH * MLP, bytes_accessed=4 * WIDTH * MLP_COLS, transcendentals=TOKENS * MLP
+            flops=16 * TOKENS * WIDTH * MLP, bytes_accessed=4 * WIDTH * MLP_COLS, transcendentals=TOKENS * MLP
         ),
         name="mlp_all",
     )(normed, upstream, weights)
@@ -887,7 +829,9 @@
 
 
 def back_kernel(
-    d_after_low,
+    mid_part,
+    hidden,
+    mlp_full,
     mix_full,
     states,
     pre,
@@ -898,11 +842,9 @@
     entering,
     mixed,
     normed_in,
-    out_part,
     tokens,
+    upstream,
     after_own,
-    d_after_own,
-    gain_mid,
     gain_rows,
     vectors,
     gate_w,
@@ -914,7 +856,13 @@
     block_sums,
     gain_sums,
     work,
+    small_work,
     own_tokens,
+    own_upstream,
+    out_part,
+    d_after_low,
+    d_after_own,
+    gain_mid,
     d_mixed,
     tail_a,
     d_gates,
@@ -930,13 +878,30 @@
     near_a,
     far_b,
     near_b,
-    sib,
-    far_s,
-    near_s,
-    half_a,
-    half_b,
-    far_2,
-    near_2,
+    far_c,
+    near_c,
+    *rest,
+):
+    n_scatter = 7
+    mix_scratch, rest = rest[:n_scatter], rest[n_scatter:]
+    small_scratch, rest = rest[:n_scatter], rest[n_scatter:]
+    back_steps(
+        mid_part, hidden, mlp_full, mix_full, states, pre, ext, decay_g, input_g, conv_low, entering, mixed,
+        normed_in, tokens, upstream, after_own, gain_rows, vectors, gate_w, doc_start,
+        grad_tokens, block_out, grad_mix, small_sums, block_sums, gain_sums,
+        work, small_work, own_tokens, own_upstream, out_part, d_after_low, d_after_own, gain_mid,
+        d_mixed, tail_a, d_gates, d_both, d_first, small, rim_send, rim_recv, totals, totals_in, after,
+        far_a, near_a, far_b, near_b, far_c, near_c, mix_scratch, small_scratch, *rest,
+    )
+
+
+def back_steps(
+    mid_part, hidden, mlp_full, mix_full, states, pre, ext, decay_g, input_g, conv_low, entering, mixed,
+    normed_in, tokens, upstream, after_own, gain_rows, vectors, gate_w, doc_start,
+    grad_tokens, block_out, grad_mix, small_sums, block_sums, gain_sums,
+    work, small_work, own_tokens, own_upstream, out_part, d_after_low, d_after_own, gain_mid,
+    d_mixed, tail_a, d_gates, d_both, d_first, small, rim_send, rim_recv, totals, totals_in, after,
+    far_a, near_a, far_b, near_b, far_c, near_c, mix_scratch, small_scratch,
     small_all,
     gain_in,
     gain_y,
@@ -948,21 +913,72 @@
 ):
     p = Place()
     links = Links(send, recv)
-    load = pltpu.make_async_copy(mix_full, work.at[:, :, :, :, pl.ds(0, MIX_COLS)], local.at[0])
-    load.start()
-    load_tokens = pltpu.make_async_copy(tokens.at[p.y], own_tokens, local.at[1])
+    loads = []
+    for f in range(CHUNKS):
+        lo = 3 * f * CHUNK + 2 * CHUNK
+        source = mlp_full.at[:, :, :, :, pl.ds(lo, CHUNK)]
+        copy = pltpu.make_async_copy(source, work.at[:, :, :, :, pl.ds(f * CHUNK, CHUNK)], local.at[f])
+        copy.start()
+        loads.append(copy)
+    load_tokens = pltpu.make_async_copy(tokens.at[p.y], own_tokens, local.at[CHUNKS])
     load_tokens.start()
+    load_upstream = pltpu.make_async_copy(upstream.at[p.y], own_upstream, local.at[CHUNKS + 1])
+    load_upstream.start()
     others_y = [{"tensor": lax.rem(p.y + d, 4)} for d in (1, 2, 3)]
     others_z = [{"dp": lax.rem(p.z + d, 4)} for d in (1, 2, 3)]
     greet([p.seq_at(d) for d in range(1, 8)] + others_y + others_z)
-    ahead = Reduce(links, p, out_part, far_b, near_b)
-    ahead.send_far()
-    ahead.send_near()
+    middle = Reduce(links, p, mid_part, far_c, near_c)
+    middle.send_first()
+    middle.send_second()
+    for copy in loads:
+        copy.wait()
+
+    def out_product(n, carry):
+        weights = work[lax.div(n, 2), lax.rem(n, 2), :, :, 0:MLP].reshape(256, MLP)
+        product = dot_nt(hidden[...], weights).astype(BF16)
+        out_part[:, :, pl.ds(pl.multiple_of(n * 256, 256), 256)] = product.reshape(ROWS, SPAN, 256)
+        return carry
+
+    lax.fori_loop(0, 8, out_product, 0)
+    load = pltpu.make_async_copy(mix_full, work, local.at[CHUNKS + 2])
+    load.start()
+    middle.merge()
+    gain_mid[...] = jnp.zeros_like(gain_mid)
+    gain_1 = gain_rows[1:2, :].astype(F32)
+    load_upstream.wait()
+    middle.settle()
+
+    def middle_rows(k, carry):
+        at = pl.ds(pl.multiple_of(k * 16, 16), 16)
+        through, share = norm_back_rows(own_sum(middle, at), after_own[at, :], gain_1)
+        gain_mid[...] += share[0:8] + share[8:16]
+        total = own_upstream[at, :].astype(F32) + through
+        d_after_own[at, :] = total
+        d_after_low[p.y, at, :] = total.astype(BF16)
+        return carry
+
+    lax.fori_loop(0, SPAN // 16, middle_rows, 0)
+    spread_c = Spread(links, p, d_after_low)
+    spread_c.start()
     load.wait()
     rows_low = d_after_low.reshape(TOKENS, WIDTH)
-    for start, size in ((0, 256), (256, 256), (512, 128)):
-        weights = work[:, :, :, :, 2 * CHAN + start : 2 * CHAN + start + size].reshape(WIDTH, size)
-        d_mixed[:, start : start + size] = dot(rows_low[...], weights)
+
+    def mixed_row(row):
+        rows = pl.ds(pl.multiple_of(row * SPAN, SPAN), SPAN)
+        for start, size in ((0, 256), (256, 256), (512, 128)):
+            weights = work[:, :, :, :, 2 * CHAN + start : 2 * CHAN + start + size].reshape(WIDTH, size)
+            d_mixed[rows, start : start + size] = dot(d_after_low[row], weights)
+
+    mixed_row(p.y)
+    spread_c.forward()
+    spread_c.near()
+    mixed_row(p.yl)
+    mixed_row(p.yr)
+    spread_c.far()
+    ahead = Reduce(links, p, out_part, far_b, near_b)
+    ahead.send_first()
+    ahead.send_second()
+    mixed_row(p.y2)
     small[...] = jnp.zeros_like(small)
     totals[...] = jnp.zeros_like(totals)
     gain_in[...] = jnp.zeros_like(gain_in)
@@ -1086,6 +1102,28 @@
 
     lax.fori_loop(0, ROWS * GROUPS, conv_back, 0)
     k_rim = links.go(rim_send, rim_recv, p.seq_at(-1))
+
+    def blocks(j, h):
+        lo = h * LANES
+        product = dot_tn(conv_low[:, lo : lo + 256], d_gates[:, j * CHAN + lo : j * CHAN + lo + 256])
+        for q in range(BLK // 32):
+            row = (j * HEADS + h) * BLK + 32 * q
+            n, inner = row // 64, row % 64
+            piece = product[32 * (h + q) : 32 * (h + q + 1), :].astype(BF16)
+            small_work[n // 8, (n // 4) % 2, n % 4, inner : inner + 32, :] = piece
+
+    for j in range(2):
+        for h in range(HEADS):
+            blocks(j, h)
+    for n in range(20, 32):
+        small_work[n // 8, (n // 4) % 2, n % 4] = jnp.zeros((64, SMALL), BF16)
+    for k, n in enumerate((20, 21, 22)):
+        width = min(256, CHAN - 256 * k)
+        both = jnp.concatenate([small[:, 256 * k : 256 * k + width], jnp.zeros((8, width), F32)], axis=0)
+        small_work[n // 8, (n // 4) % 2, n % 4, 0:16, 0:width] = both.astype(BF16)
+    small_scatter = Scatter(links, p, small_work, *small_scratch)
+    for xx in range(4):
+        small_scatter.give(xx)
     spread_b.forward()
     links.arrived(rim_recv, k_rim, p.seq_at(1))
     for r in range(ROWS):
@@ -1100,10 +1138,14 @@
         d_first[:, :, pl.ds(pl.multiple_of(n * 256, 256), 256)] = product.reshape(ROWS, SPAN, 256)
         return carry
 
-    lax.fori_loop(0, 8, first_part, 0)
     back = Reduce(links, p, d_first, far_a, near_a)
-    back.send_far()
-    back.send_near()
+    lax.fori_loop(0, 4, first_part, 0)
+    back.send_first()
+    lax.fori_loop(4, 8, first_part, 0)
+    back.send_second()
+    for xx in range(4):
+        small_scatter.take(xx)
+    small_scatter.first()
 
     def weight_grads(n):
         at = pl.ds(pl.multiple_of(n * 256, 256), 256)
@@ -1113,25 +1155,7 @@
         out = dot_tn(rows_low[:, at], mixed[...])
         to[:, :, 2 * CHAN : MIX_COLS] = out.astype(BF16).reshape(4, 64, CHAN)
 
-    def blocks(j, h):
-        lo = h * LANES
-        product = dot_tn(conv_low[:, lo : lo + 256], d_gates[:, j * CHAN + lo : j * CHAN + lo + 256])
-        for q in range(BLK // 32):
-            row = (j * HEADS + h) * BLK + 32 * q
-            n, inner = row // 64, row % 64
-            piece = product[32 * (h + q) : 32 * (h + q + 1), :].astype(BF16)
-            work[n // 8, (n // 4) % 2, n % 4, inner : inner + 32, MIX_COLS:] = piece
-
-    for j in range(2):
-        for h in range(HEADS):
-            blocks(j, h)
-    for n in range(20, 32):
-        work[n // 8, (n // 4) % 2, n % 4, :, MIX_COLS:] = jnp.zeros((64, SMALL), BF16)
-    for k, n in enumerate((20, 21, 22)):
-        width = min(256, CHAN - 256 * k)
-        both = jnp.concatenate([small[:, 256 * k : 256 * k + width], jnp.zeros((8, width), F32)], axis=0)
-        work[n // 8, (n // 4) % 2, n % 4, 0:16, MIX_COLS : MIX_COLS + width] = both.astype(BF16)
-    scatter = Scatter(links, p, work, sib, far_s, near_s, half_a, half_b, far_2, near_2)
+    scatter = Scatter(links, p, work, *mix_scratch)
 
     def give(xx, carry):
         weight_grads(xx * 2 + 1 - p.c)
@@ -1144,11 +1168,14 @@
     lax.fori_loop(0, 4, give, 0)
     for xx in range(4):
         scatter.give(xx)
+    small_scatter.merge()
     back.merge()
     lax.fori_loop(0, 4, keep, 0)
+    small_scatter.turn()
     for xx in range(4):
         scatter.take(xx)
     scatter.first()
+    small_scatter.merge_2()
     back.settle()
     load_tokens.wait()
     gain = gain_rows[0:1, :].astype(F32)
@@ -1167,17 +1194,29 @@
         [jnp.sum(gain_in[...], axis=0, keepdims=True), jnp.sum(gain_mid[...], axis=0, keepdims=True)], axis=0
     )
     y_keys = [links.go(gain_y.at[p.y], gain_y.at[p.y], device) for device in others_y]
+
+    def store_small(base, value):
+        small_all[p.x, p.c, p.z, base : base + 32, :] = value.astype(BF16)
+
+    small_scatter.finish(store_small)
+    small_gather = Gather(links, p, small_all)
+    small_gather.first()
     scatter.merge()
     for d in (1, 2, 3):
         links.arrived(gain_y.at[lax.rem(p.y + 4 - d, 4)], y_keys[d - 1], others_y[0])
     gain_z[p.z] = gain_y[0] + gain_y[1] + gain_y[2] + gain_y[3]
     z_keys = [links.go(gain_z.at[p.z], gain_z.at[p.z], device) for device in others_z]
+    small_gather.middle()
+    small_gather.finish()
+    small_gather.second()
+    spread_a.forward()
     scatter.turn()
     for d in (1, 2, 3):
         links.arrived(gain_z.at[lax.rem(p.z + 4 - d, 4)], z_keys[d - 1], others_z[0])
     gain_s[p.s] = gain_z[0] + gain_z[1] + gain_z[2] + gain_z[3]
     s_keys = [links.go(gain_s.at[p.s], gain_s.at[p.s], p.seq_at(d)) for d in range(1, 8)]
-    spread_a.forward()
+    small_gather.middle()
+    small_gather.finish()
     scatter.merge_2()
     for d in range(1, 8):
         links.arrived(gain_s.at[p.seq_at(-d)["seq"]], s_keys[d - 1], p.seq_at(-d))
@@ -1185,21 +1224,8 @@
     for s in range(1, 8):
         total = total + gain_s[s]
     gain_sums[...] = total
-
-    def store(base, value):
-        grad_mix[base : base + 32, :] = value[:, :MIX_COLS]
-        small_all[p.x, p.c, p.z, base : base + 32, :] = value[:, MIX_COLS:].astype(BF16)
-
-    scatter.finish(store)
-    small_gather = Gather(links, p, small_all)
-    small_gather.first()
     spread_b.near()
     spread_b.far()
-    small_gather.middle()
-    small_gather.finish()
-    small_gather.second()
-    small_gather.middle()
-    small_gather.finish()
     small_gather.settle()
     for k, n in enumerate((20, 21, 22)):
         width = min(256, CHAN - 256 * k)
@@ -1208,6 +1234,11 @@
     for n in range(20):
         value = small_all[n // 8, (n // 4) % 2, n % 4].astype(F32)
         block_sums[64 * n : 64 * (n + 1), :] = value
+
+    def store(base, value):
+        grad_mix[base : base + 32, :] = value
+
+    scatter.finish(store)
     spread_a.near()
     spread_a.far()
     links.drain()
@@ -1227,11 +1258,17 @@
             shape((2 * HEADS * BLK, 256), F32),
             shape((2, WIDTH), F32),
         ],
-        in_specs=[vmem(), anyspace()] + [vmem()] * 10 + [anyspace()] + [vmem()] * 6 + [smem()],
+        in_specs=[vmem()] * 2 + [anyspace()] * 2 + [vmem()] * 9 + [anyspace()] * 2 + [vmem()] * 4 + [smem()],
         out_specs=[vmem()] * 6,
         scratch_shapes=[
-            pltpu.VMEM((4, 2, 4, 64, RS_COLS), BF16),
+            pltpu.VMEM((4, 2, 4, 64, MIX_COLS), BF16),
+            pltpu.VMEM((4, 2, 4, 64, SMALL), BF16),
             pltpu.VMEM((SPAN, WIDTH), BF16),
+            pltpu.VMEM((SPAN, WIDTH), BF16),
+            pltpu.VMEM((ROWS, SPAN, WIDTH), BF16),
+            pltpu.VMEM((ROWS, SPAN, WIDTH), BF16),
+            pltpu.VMEM((SPAN, WIDTH), F32),
+            pltpu.VMEM((8, WIDTH), F32),
             pltpu.VMEM(tc, F32),
             pltpu.VMEM(tc, F32),
             pltpu.VMEM((TOKENS, 2 * CHAN), BF16),
@@ -1244,20 +1281,117 @@
             pltpu.VMEM((8, 8, CHAN), F32),
             pltpu.VMEM((8, CHAN), F32),
         ]
-        + pair * 2
-        + Scatter.scratch(RS_COLS)
+        + pair * 3
+        + Scatter.scratch(MIX_COLS)
+        + Scatter.scratch(SMALL)
         + [
             pltpu.VMEM((4, 2, 4, 64, SMALL), BF16),
             pltpu.VMEM((8, WIDTH), F32),
             pltpu.VMEM((4, 2, WIDTH), F32),
             pltpu.VMEM((8, 2, WIDTH), F32),
             pltpu.VMEM((4, 2, WIDTH), F32),
-            pltpu.SemaphoreType.DMA((2,)),
-            pltpu.SemaphoreType.DMA((144,)),
-            pltpu.SemaphoreType.DMA((144,)),
+            pltpu.SemaphoreType.DMA((CHUNKS + 3,)),
+            pltpu.SemaphoreType.DMA((184,)),
+            pltpu.SemaphoreType.DMA((184,)),
         ],
         compiler_params=params(2),
         name="back_all",
+    )(*operands)
+
+
+def finish_kernel(
+    block_in,
+    tokens_in,
+    states_in,
+    mix_sum,
+    small,
+    blocks_in,
+    gains_in,
+    mlp_sum,
+    block_out,
+    states,
+    grad_tokens,
+    grad_gains,
+    grad_mix_in,
+    grad_mix_out,
+    grad_conv,
+    grad_blocks,
+    grad_bias,
+    grad_mlp_in,
+    grad_mlp_out,
+):
+    step = pl.program_id(0)
+    block_out[...] = block_in[...]
+    grad_tokens[...] = tokens_in[...]
+    states[...] = states_in[...]
+    for h in range(HEADS):
+
+        @pl.when(step == h)
+        def _():
+            for j in range(2):
+                grad_blocks[j, 0] = blocks_in[j, 0, :, 32 * h : 32 * h + BLK]
+
+    @pl.when(step == 0)
+    def _():
+        grad_gains[...] = gains_in[...]
+        for j in range(2):
+            grad_mix_in[j] = mix_sum[:, j * CHAN : (j + 1) * CHAN]
+        grad_mix_out[...] = mix_sum[:, 2 * CHAN :]
+        grad_conv[...] = small[0:CONV, :]
+        grad_bias[...] = small[CONV + 1 : CONV + 3, :]
+        for f in range(CHUNKS):
+            lo, at = 3 * f * CHUNK, pl.ds(f * CHUNK, CHUNK)
+            for j in range(2):
+                grad_mlp_in[j, :, at] = mlp_sum[:, lo + j * CHUNK : lo + (j + 1) * CHUNK].astype(F32)
+            grad_mlp_out[:, at] = mlp_sum[:, lo + 2 * CHUNK : lo + 3 * CHUNK].astype(F32)
+
+
+def finish(*operands):
+    shape = jax.ShapeDtypeStruct
+    row = lambda width: pl.BlockSpec((1, SPAN, width), lambda i: (i, 0, 0))
+    whole = lambda *dims: pl.BlockSpec(dims, lambda i: (0,) * len(dims))
+    head = lambda width: pl.BlockSpec((2, 1, BLK, width), lambda i: (0, i, 0, 0))
+    return pl.pallas_call(
+        finish_kernel,
+        grid=(ROWS,),
+        out_shape=[
+            shape((ROWS, SPAN, WIDTH), BF16),
+            shape((ROWS, SPAN, CHAN), F32),
+            shape((ROWS, SPAN, WIDTH), BF16),
+            shape((2, WIDTH), F32),
+            shape((2, 64, CHAN), F32),
+            shape((64, CHAN), F32),
+            shape((CONV, CHAN), F32),
+            shape((2, HEADS, BLK, BLK), F32),
+            shape((2, CHAN), F32),
+            shape((2, 64, MLP), F32),
+            shape((64, MLP), F32),
+        ],
+        in_specs=[
+            row(WIDTH),
+            row(WIDTH),
+            row(CHAN),
+            whole(64, MIX_COLS),
+            whole(8, CHAN),
+            head(256),
+            whole(2, WIDTH),
+            whole(64, MLP_COLS),
+        ],
+        out_specs=[
+            row(WIDTH),
+            row(CHAN),
+            row(WIDTH),
+            whole(2, WIDTH),
+            whole(2, 64, CHAN),
+            whole(64, CHAN),
+            whole(CONV, CHAN),
+            head(BLK),
+            whole(2, CHAN),
+            whole(2, 64, MLP),
+            whole(64, MLP),
+        ],
+        compiler_params=pltpu.CompilerParams(vmem_limit_bytes=VMEM_BYTES),
+        name="finish",
     )(*operands)
 
 
@@ -1286,6 +1420,7 @@
         ],
         axis=1,
     )
+    raw_vectors = jnp.concatenate([conv_weight, conv_bias[None], gate_bias, decay_param[None]], axis=0)
     (
         mix_full,
         mlp_full,
@@ -1304,31 +1439,27 @@
     ) = mix_forward(
         tokens.reshape(TOKENS, WIDTH),
         mix_in,
-        mix_out,
+        mix_out.T,
         mlp_in,
-        mlp_out,
+        mlp_out.T,
         init_state,
-        conv_state,
+        conv_state.transpose(1, 0, 2),
         fresh_rows,
         doc_start,
         norm_gains,
-        conv_weight,
-        conv_bias[None],
-        gate_bias,
-        decay_param[None],
+        raw_vectors,
         gate_w,
     )
-    mid_part, out_part, grad_mlp = mlp_all(
+    mid_part, hidden, grad_mlp = mlp_all(
         normed_mid.reshape(TOKENS, WIDTH),
         cotangent.reshape(TOKENS, WIDTH),
         mlp_full.reshape(WIDTH, MLP_COLS),
     )
     grad_mlp = lax.psum_scatter(grad_mlp, ("seq", "dp"), scatter_dimension=0, tiled=True)
-    d_after_low, d_after_own, gain_mid = mid_back(
-        mid_part.reshape(ROWS, SPAN, WIDTH), after_own, cotangent, norm_gains
-    )
     grad_tokens, block_out, grad_mix, small, blocks, grad_gains = back_all(
-        d_after_low,
+        mid_part.reshape(ROWS, SPAN, WIDTH),
+        hidden,
+        mlp_full,
         mix_full,
         states,
         pre,
@@ -1339,33 +1470,50 @@
         entering,
         mixed,
         normed_in,
-        out_part.reshape(ROWS, SPAN, WIDTH),
         tokens,
+        cotangent,
         after_own,
-        d_after_own,
-        gain_mid,
         norm_gains,
         vectors,
         gate_w,
         doc_start,
     )
-    blocks = blocks.reshape(2, HEADS, BLK, 256)
-    blocks = jnp.stack([blocks[:, h, :, 32 * h : 32 * h + BLK] for h in range(HEADS)], axis=1)
-    grad_mlp = grad_mlp.astype(F32).reshape(64, CHUNKS, 3, CHUNK)
+    (
+        block_out,
+        states,
+        grad_tokens,
+        grad_gains,
+        grad_mix_in,
+        grad_mix_out,
+        grad_conv,
+        grad_blocks,
+        grad_bias,
+        grad_mlp_in,
+        grad_mlp_out,
+    ) = finish(
+        block_out,
+        grad_tokens,
+        states.reshape(ROWS, SPAN, CHAN),
+        grad_mix,
+        small,
+        blocks.reshape(2, HEADS, BLK, 256),
+        grad_gains,
+        grad_mlp,
+    )
     return (
         block_out,
-        states.reshape(ROWS, SPAN, CHAN),
+        states,
         grad_tokens,
         grad_gains,
-        jnp.stack([grad_mix[:, :CHAN], grad_mix[:, CHAN : 2 * CHAN]]),
-        grad_mix[:, 2 * CHAN :].T,
-        small[0:4],
-        small[4],
-        blocks,
-        small[5:7],
-        small[7] * jax.nn.sigmoid(decay_param.astype(F32)),
-        grad_mlp[:, :, 0:2].transpose(2, 0, 1, 3).reshape(2, 64, MLP),
-        grad_mlp[:, :, 2].transpose(1, 2, 0).reshape(MLP, 64),
+        grad_mix_in,
+        grad_mix_out.T,
+        grad_conv,
+        small[CONV],
+        grad_blocks,
+        grad_bias,
+        small[CONV + 3] * jax.nn.sigmoid(decay_param.astype(F32)),
+        grad_mlp_in,
+        grad_mlp_out.T,
     )
 
 

time: 379 us -> 338 us (0.89)
  Pallas kernels: 338 us -> 316 us
  local copies, waits for them, and re-layouts: 23.1 us -> 4.27 us
    pallas_call x1, Pallas kernels: 42.9 us -> 7.27 us  [finish(): pl.pallas_call(finish_kernel, grid=(ROWS,), out_shape=[shape((ROWS, SPAN,...]
    pallas_call x1, Pallas kernels: 118 us -> 143 us  [back_all(): pl.pallas_call(back_kernel, out_shape=[shape((ROWS, SPAN, WIDTH), BF16),...]
    unnamed x26 -> x6, local copies, waits for them, and re-layouts: 10.2 us -> 0.01 us
    pallas_call x1, Pallas kernels: 47.6 us -> 39.4 us  [mlp_all(): pl.pallas_call(mlp_kernel, grid=(CHUNKS,), out_shape=[shape((TOKENS, WIDT...]
  transfers between devices with their start and end apart: 1 -> 1, of which waited for: 0 -> 0; matrix products, arithmetic and copies ran while one was open for 2% -> 1% of each run, Pallas kernels for 43% -> 42%
where the time goes in v3:
time: 338 us; the launch traced here: 337 us
  Pallas kernels  316 us (93%)
  between operations  14.1 us (4%)
  local copies, waits for them, and re-layouts  4.27 us (1%)
    pallas_call x1, Pallas kernels, back_all(): pl.pallas_call(back_kernel, out_shape=[shape((ROWS, SPAN, WIDTH), BF16),...  143 us
    pallas_call x1, Pallas kernels, mix_forward(): pl.pallas_call(mix_forward_kernel, out_shape=outs, in_specs=[vmem()] * 7...  126 us
    pallas_call x1, Pallas kernels, mlp_all(): pl.pallas_call(mlp_kernel, grid=(CHUNKS,), out_shape=[shape((TOKENS, WIDT...  39.4 us
    pallas_call x1, Pallas kernels, finish(): pl.pallas_call(finish_kernel, grid=(ROWS,), out_shape=[shape((ROWS, SPAN,...  7.27 us
  transfers between devices with their start and end apart: 1, of which 0 were waited for; matrix products, arithmetic and copies ran while one was open for 1% of the time, Pallas kernels for 42%

profile of v3, /device:TPU:1, one launch (start us, length us, event | category | flops | bytes accessed | tf_op | source)
XLA Modules:
  0.0 336.6 jit_solution(5300819197741473925)
XLA Ops:
  7.2 0.0 copy-start.2
  7.2 0.0 copy-start.1
  7.2 0.0 reduce-scatter.2.cloned.1.call-start
  7.2 0.7 broadcast_in_dim.6
  7.9 0.7 broadcast_in_dim.7
  8.6 1.2 slice_bitcast_fusion.3
  9.8 0.1 pad_bitcast_fusion.2
  9.9 0.2 pad_bitcast_fusion
  10.1 0.0 copy-done.2
  10.1 0.0 copy-done.1
  10.1 0.6 pad_maximum_fusion.1.raw_vectors
  10.7 1.1 pad_maximum_fusion.gate_w
  11.8 126.4 %mix_forward.1 = (bf16[4,2,4,64,1920]{4,3,2,1,0:T(8,128)(2,1)}, bf16[4,2,4,64,4608]{4,3,2,1,0:T(8,128)(2,1)}, f32[512,640]{1,0:T(8,128)}, f32[512,640]{1,0:T(8,1...) custom-call(bf16[512,2048]{1,0:T(8,128)(2,1)} %bitcast.37, ...), custom_call_target="tpu_custom_call" | custom-call | tf_op jit(solution)/shard_map/mix_forward/pallas_call | solution.py:624
  138.3 39.4 %mlp_all.1 = (bf16[512,2048]{1,0:T(8,128)(2,1)}, bf16[512,1536]{1,0:T(8,128)(2,1)}, bf16[2048,4608]{1,0:T(8,128)(2,1)}) custom-call(bf16[512,2048]{1,0:T(8,128)(2,1)} %bitcast.45, bf16[512,2048]{1,0:T(8,128)(2,1)} %bitcast.39, bf16[2048,4608]{1,0:T(8,128)(2,1)} %bitcast.36), custom_call_target="tpu_custom_call" | custom-call | flops 25769803776 | bytes 37748736 | tf_op jit(solution)/shard_map/mlp_all/pallas_call | solution.py:692
  177.6 0.0 reduce-scatter.2.cloned.1.call-update
  177.7 0.0 copy-start
  177.7 142.7 %back_all.1 = (bf16[4,128,2048]{2,1,0:T(8,128)(2,1)}, bf16[4,128,2048]{2,1,0:T(8,128)(2,1)}, f32[64,1920]{1,0:T(8,128)}, f32[8,640]{1,0:T(8,128)}, f32[1280,256]{1,0:T(8,128)}, /*index=5*/f32[2,2048]{1,0:T(2,128)}) custom-call(bf16[4,128,2048]{2,1,0:T(8,128)(2,1)} %bitcast.40, bf16[512,1536]{1,0:T(8,128)(2,1)} %get-tuple-element.50.hidden, ...), custom_call_target="tpu_custom_call" | custom-call | tf_op jit(solution)/shard_map/back_all/pallas_call | solution.py:1251
  320.4 1.4 slice_reduce_fusion
  321.9 0.0 copy-done
  321.9 0.6 divide_multiply_fusion
  322.5 0.0 reduce-scatter.2.cloned.1.call-done.mlp_sum
  322.5 7.3 %finish.1 = (bf16[4,128,2048]{2,1,0:T(8,128)(2,1)}, f32[4,128,640]{2,1,0:T(8,128)}, bf16[4,128,2048]{2,1,0:T(8,128)(2,1)}, f32[2,2048]{1,0:T(2,128)}, f32[2,64,6...) custom-call(bf16[4,128,2048]{2,1,0:T(8,128)(2,1)} %get-tuple-element, ...), custom_call_target="tpu_custom_call" | custom-call | tf_op jit(solution)/shard_map/finish/pallas_call | solution.py:1354
Async XLA Ops:
  7.2 2.9 copy-start.2
  7.2 2.9 copy-start.1
  7.2 315.3 %reduce-scatter.2.cloned.1.call-start = ((), (), s32[]{:S(2)}) async-start(), calls=%async_computation.1 | async-start | bytes 19464192 | tf_op jit(solution)/shard_map/reduce_scatter | solution.py:1458
  177.7 144.2 %copy-start = (bf16[640]{0:T(1024)(128)(2,1)S(1)}, bf16[640]{0:T(1024)(128)(2,1)}, u32[]{:S(2)}) copy-start(bf16[640]{0:T(1024)(128)(2,1)} %param.28) | copy-start | bytes 3844
Sparse Core Ops, SparseCore 0:
  177.8 126.1 reduce-scatter.1

commit v4 on v3

--- a/solution.py
+++ b/solution.py
@@ -23,6 +23,7 @@
 MLP = 1536
 MIX_COLS = 3 * CHAN
 MLP_COLS = 3 * MLP
+MLP_CUT = 2304
 CHUNK = 256
 CHUNKS = MLP // CHUNK
 SMALL = 256
@@ -65,7 +66,7 @@
     def __init__(self, send, recv):
         self.send, self.recv = send, recv
         self.count = 0
-        self.started = []
+        self.keyed = {}
 
     def go(self, src, dst, device):
         k = self.count
@@ -79,7 +80,7 @@
             device_id_type=MESH,
         )
         copy.start()
-        self.started.append(copy)
+        self.keyed[k] = copy
         return k
 
     def arrived(self, view, k, device):
@@ -93,40 +94,46 @@
         ).wait_recv()
 
     def drain(self):
-        for copy in self.started:
+        for copy in self.keyed.values():
             copy.wait_send()
-        self.started = []
+        self.keyed = {}
+
+    def sent(self, keys):
+        for k in keys:
+            self.keyed.pop(k).wait_send()
 
 
 class Gather:
-    def __init__(self, links, place, out):
-        self.links, self.p, self.out = links, place, out
+    def __init__(self, links, place, out, cut):
+        self.links, self.p = links, place
+        self.out_a = out.at[:, :, :, :, pl.ds(0, cut)]
+        self.out_b = out.at[:, :, :, :, pl.ds(cut, out.shape[-1] - cut)]
         self.to_sibling = []
 
     def _pass_on(self, view_of):
         k = self.links.go(view_of(self.p.c), view_of(self.p.c), self.p.SIB)
         self.to_sibling.append((view_of, k))
 
-    def _ring(self, blk, i, right, left, base):
+    def _ring(self, blk, i, right, left):
         links, p = self.links, self.p
         c = p.c
         ir, il, i2 = lax.rem(i + 1, 4), lax.rem(i + 3, 4), lax.rem(i + 2, 4)
-        a, b = pl.ds(base, 16), pl.ds(base + 16, 16)
+        a, b = pl.ds(0, 32), pl.ds(32, 32)
         k0 = links.go(blk(c, i, a), blk(c, i, a), right)
         k1 = links.go(blk(c, i, b), blk(c, i, b), left)
         k2 = links.go(blk(c, i, b), blk(c, i, b), right)
         k3 = links.go(blk(c, i, a), blk(c, i, a), left)
+        later = []
 
         def middle():
             links.arrived(blk(c, il, a), k0, left)
-            k4 = links.go(blk(c, il, a), blk(c, il, a), right)
+            later.append(links.go(blk(c, il, a), blk(c, il, a), right))
             links.arrived(blk(c, ir, b), k1, right)
-            k5 = links.go(blk(c, ir, b), blk(c, ir, b), left)
+            later.append(links.go(blk(c, ir, b), blk(c, ir, b), left))
             self._pass_on(lambda cc: blk(cc, il, a))
             self._pass_on(lambda cc: blk(cc, ir, b))
-            return k4, k5
-
-        def finish(later):
+
+        def finish():
             for view, k, source in (
                 (lambda cc: blk(cc, il, b), k2, left),
                 (lambda cc: blk(cc, ir, a), k3, right),
@@ -139,22 +146,31 @@
         return middle, finish
 
     def first(self):
-        p, out = self.p, self.out
-        self.x_ring = self._ring(lambda cc, j, r: out.at[j, cc, p.z, r], p.x, p.XR, p.XL, 0)
-        self.z_ring = self._ring(lambda cc, j, r: out.at[p.x, cc, j, r], p.z, p.ZR, p.ZL, 32)
-        self._pass_on(lambda cc: out.at[p.x, cc, p.z])
+        p, a, b = self.p, self.out_a, self.out_b
+        self.ring_a = self._ring(lambda cc, j, r: a.at[j, cc, p.z, r], p.x, p.XR, p.XL)
+        self.ring_b = self._ring(lambda cc, j, r: b.at[p.x, cc, j, r], p.z, p.ZR, p.ZL)
+        self._pass_on(lambda cc: a.at[p.x, cc, p.z])
+        self._pass_on(lambda cc: b.at[p.x, cc, p.z])
+
+    def second_z(self):
+        p, a = self.p, self.out_a
+        self.ring_a = self._ring(lambda cc, j, r: a.at[:, cc, j, r], p.z, p.ZR, p.ZL)
+
+    def second_x(self):
+        p, b = self.p, self.out_b
+        self.ring_b = self._ring(lambda cc, j, r: b.at[j, cc, :, r], p.x, p.XR, p.XL)
 
     def second(self):
-        p, out = self.p, self.out
-        self.x_ring = self._ring(lambda cc, j, r: out.at[:, cc, j, r], p.z, p.ZR, p.ZL, 0)
-        self.z_ring = self._ring(lambda cc, j, r: out.at[j, cc, :, r], p.x, p.XR, p.XL, 32)
+        self.second_z()
+        self.second_x()
 
     def middle(self):
-        self.later = (self.x_ring[0](), self.z_ring[0]())
+        self.ring_a[0]()
+        self.ring_b[0]()
 
     def finish(self):
-        self.x_ring[1](self.later[0])
-        self.z_ring[1](self.later[1])
+        self.ring_a[1]()
+        self.ring_b[1]()
 
     def settle(self):
         for view_of, k in self.to_sibling:
@@ -201,9 +217,16 @@
         self.links, self.p, self.out = links, place, out
 
     def start(self):
+        self.start_first()
+        self.start_second()
+
+    def start_first(self):
         go, out, y, p = self.links.go, self.out, self.p.y, self.p
         self.k0 = go(out.at[y, :, CA], out.at[y, :, CA], p.YR)
         self.k1 = go(out.at[y, :, CB], out.at[y, :, CB], p.YL)
+
+    def start_second(self):
+        go, out, y, p = self.links.go, self.out, self.p.y, self.p
         self.k2 = go(out.at[y, :, CB], out.at[y, :, CB], p.YR)
         self.k3 = go(out.at[y, :, CA], out.at[y, :, CA], p.YL)
 
@@ -358,15 +381,13 @@
         mine[:, j * CHAN : (j + 1) * CHAN] = mix_in[j]
     mine[:, 2 * CHAN :] = mix_out[...]
     greet([p.seq_at(d) for d in range(1, 8)] + [p.ZR, p.ZL, p.YR, p.YL])
-    in_gather = Gather(links, p, mix_full.at[:, :, :, :, pl.ds(0, 2 * CHAN)])
-    out_gather = Gather(links, p, mix_full.at[:, :, :, :, pl.ds(2 * CHAN, CHAN)])
-    mlp_gather = Gather(links, p, mlp_full)
+    in_gather = Gather(links, p, mix_full.at[:, :, :, :, pl.ds(0, 2 * CHAN)], CHAN)
+    out_gather = Gather(links, p, mix_full.at[:, :, :, :, pl.ds(2 * CHAN, CHAN)], 384)
+    mlp_gather = Gather(links, p, mlp_full, MLP_CUT)
     in_gather.first()
-    for f in range(CHUNKS):
-        lo, to = f * CHUNK, 3 * f * CHUNK
-        mlp_own[:, to : to + CHUNK] = mlp_in[0, :, lo : lo + CHUNK]
-        mlp_own[:, to + CHUNK : to + 2 * CHUNK] = mlp_in[1, :, lo : lo + CHUNK]
-        mlp_own[:, to + 2 * CHUNK : to + 3 * CHUNK] = mlp_out[:, lo : lo + CHUNK]
+    for j in range(2):
+        mlp_own[:, j * MLP : (j + 1) * MLP] = mlp_in[j]
+    mlp_own[:, 2 * MLP :] = mlp_out[...]
     own_mlp = pltpu.make_async_copy(mlp_own, mlp_full.at[p.x, p.c, p.z], local.at[0])
     own_mlp.start()
     gains[...] = gain_rows[...].astype(F32)
@@ -395,9 +416,6 @@
     out_gather.middle()
     out_gather.finish()
     out_gather.second()
-    mlp_gather.middle()
-    mlp_gather.finish()
-    mlp_gather.second()
     in_gather.settle()
     saves = []
 
@@ -494,6 +512,9 @@
     state = init_state[...] * kept
     for d in range(1, 8):
         links.arrived(totals_in.at[p.seq_at(-d)["seq"]], keys[d - 1], p.seq_at(-d))
+    mlp_gather.middle()
+    mlp_gather.finish()
+    mlp_gather.second()
     totals_in[p.s] = totals[...]
     for source in range(7):
         both = totals_in[source]
@@ -646,11 +667,24 @@
 
 
 def mlp_kernel(
-    normed, upstream, weights, mid_part, hidden_out, grads, normed_t, upstream_t, d_both, mid_sum
+    normed,
+    upstream,
+    gate_weights,
+    up_weights,
+    down_weights,
+    states_in,
+    d_gate_out,
+    d_up_out,
+    hidden_out,
+    grads,
+    states_out,
+    normed_t,
+    upstream_t,
+    d_both,
 ):
-    step = pl.program_id(0)
-
-    @pl.when(step == 0)
+    states_out[...] = states_in[...]
+
+    @pl.when(pl.program_id(0) == 0)
     def _():
         def turn(n, carry):
             at = pl.ds(pl.multiple_of(n * 256, 256), 256)
@@ -659,58 +693,55 @@
             return carry
 
         lax.fori_loop(0, WIDTH // 256, turn, 0)
-        mid_sum[...] = jnp.zeros_like(mid_sum)
-
-    gate = dot(normed[...], weights[:, 0:CHUNK])
-    up = dot(normed[...], weights[:, CHUNK : 2 * CHUNK])
-    d_hidden = dot(upstream[...], weights[:, 2 * CHUNK :])
+
+    gate = dot(normed[...], gate_weights[...])
+    up = dot(normed[...], up_weights[...])
+    d_hidden = dot(upstream[...], down_weights[...])
     act, slope = gelu_pair(gate)
     hidden = (act * up).astype(BF16)
-    d_both[:, 0:CHUNK] = (d_hidden * up * slope).astype(BF16)
-    d_both[:, CHUNK : 2 * CHUNK] = (d_hidden * act).astype(BF16)
+    d_gate = (d_hidden * up * slope).astype(BF16)
+    d_up = (d_hidden * act).astype(BF16)
+    d_both[:, 0:CHUNK] = d_gate
+    d_both[:, CHUNK : 2 * CHUNK] = d_up
     d_both[:, 2 * CHUNK :] = hidden
+    d_gate_out[...] = d_gate
+    d_up_out[...] = d_up
     hidden_out[...] = hidden
 
     def tile(n, carry):
         at = pl.ds(pl.multiple_of(n * 256, 256), 256)
         grads[at, 0 : 2 * CHUNK] = dot(normed_t[at, :], d_both[:, 0 : 2 * CHUNK]).astype(BF16)
         grads[at, 2 * CHUNK :] = dot(upstream_t[at, :], d_both[:, 2 * CHUNK :]).astype(BF16)
-        mid_sum[:, at] += dot_nt(d_both[:, 0 : 2 * CHUNK], weights[at, 0 : 2 * CHUNK])
         return carry
 
     lax.fori_loop(0, WIDTH // 256, tile, 0, unroll=2)
 
-    @pl.when(step == CHUNKS - 1)
-    def _():
-        mid_part[...] = mid_sum[...].astype(BF16)
-
-
-def mlp_all(normed, upstream, weights):
+
+def mlp_all(normed, upstream, weights, states):
     shape = jax.ShapeDtypeStruct
     whole = pl.BlockSpec((TOKENS, WIDTH), lambda f: (0, 0))
+    part = lambda j: pl.BlockSpec((WIDTH, CHUNK), lambda f: (0, j * CHUNKS + f))
     block = pl.BlockSpec((WIDTH, 3 * CHUNK), lambda f: (0, f))
+    column = pl.BlockSpec((TOKENS, CHUNK), lambda f: (0, f))
+    row = pl.BlockSpec((1, SPAN, CHAN), lambda f: (jnp.minimum(f, ROWS - 1), 0, 0))
     return pl.pallas_call(
         mlp_kernel,
         grid=(CHUNKS,),
-        out_shape=[
-            shape((TOKENS, WIDTH), BF16),
-            shape((TOKENS, MLP), BF16),
-            shape((WIDTH, MLP_COLS), BF16),
-        ],
-        in_specs=[whole, whole, block],
-        out_specs=[whole, pl.BlockSpec((TOKENS, CHUNK), lambda f: (0, f)), block],
+        out_shape=[shape((TOKENS, MLP), BF16)] * 3
+        + [shape((WIDTH, MLP_COLS), BF16), shape((ROWS, SPAN, CHAN), F32)],
+        in_specs=[whole, whole, part(0), part(1), part(2), row],
+        out_specs=[column] * 3 + [block, row],
         scratch_shapes=[
             pltpu.VMEM((WIDTH, TOKENS), BF16),
             pltpu.VMEM((WIDTH, TOKENS), BF16),
             pltpu.VMEM((TOKENS, 3 * CHUNK), BF16),
-            pltpu.VMEM((TOKENS, WIDTH), F32),
         ],
         compiler_params=pltpu.CompilerParams(vmem_limit_bytes=VMEM_BYTES),
         cost_estimate=pl.CostEstimate(
-            flops=16 * TOKENS * WIDTH * MLP, bytes_accessed=4 * WIDTH * MLP_COLS, transcendentals=TOKENS * MLP
+            flops=12 * TOKENS * WIDTH * MLP, bytes_accessed=4 * WIDTH * MLP_COLS, transcendentals=TOKENS * MLP
         ),
         name="mlp_all",
-    )(normed, upstream, weights)
+    )(normed, upstream, weights, weights, weights, states)
 
 
 class Scatter:
@@ -829,22 +860,23 @@
 
 
 def back_kernel(
-    mid_part,
-    hidden,
+    hbm_d_gate,
+    hbm_d_up,
+    hbm_hidden,
     mlp_full,
     mix_full,
-    states,
-    pre,
-    ext,
-    decay_g,
-    input_g,
-    conv_low,
+    hbm_saved_0,
+    hbm_saved_1,
+    hbm_saved_2,
+    hbm_saved_3,
+    hbm_saved_4,
+    hbm_saved_5,
+    hbm_saved_6,
+    hbm_saved_7,
+    hbm_saved_8,
     entering,
-    mixed,
-    normed_in,
     tokens,
     upstream,
-    after_own,
     gain_rows,
     vectors,
     gate_w,
@@ -855,10 +887,21 @@
     small_sums,
     block_sums,
     gain_sums,
+    hidden,
+    states,
+    pre,
+    ext,
+    decay_g,
+    input_g,
+    conv_low,
+    mixed,
+    normed_in,
+    after_own,
     work,
     small_work,
     own_tokens,
     own_upstream,
+    mid_part,
     out_part,
     d_after_low,
     d_after_own,
@@ -867,7 +910,6 @@
     tail_a,
     d_gates,
     d_both,
-    d_first,
     small,
     rim_send,
     rim_recv,
@@ -878,59 +920,109 @@
     near_a,
     far_b,
     near_b,
-    far_c,
-    near_c,
     *rest,
 ):
     n_scatter = 7
     mix_scratch, rest = rest[:n_scatter], rest[n_scatter:]
     small_scratch, rest = rest[:n_scatter], rest[n_scatter:]
+    saved = (
+        (hbm_saved_0, states),
+        (hbm_saved_1, pre),
+        (hbm_saved_2, ext),
+        (hbm_saved_3, decay_g),
+        (hbm_saved_4, input_g),
+        (hbm_saved_5, conv_low),
+        (hbm_saved_6, mixed),
+        (hbm_saved_7, normed_in),
+        (hbm_saved_8, after_own),
+    )
     back_steps(
-        mid_part, hidden, mlp_full, mix_full, states, pre, ext, decay_g, input_g, conv_low, entering, mixed,
-        normed_in, tokens, upstream, after_own, gain_rows, vectors, gate_w, doc_start,
+        (hbm_d_gate, hbm_d_up, hbm_hidden), saved, mlp_full, mix_full, hidden, states, pre, ext, decay_g, input_g,
+        conv_low, entering, mixed, normed_in, tokens, upstream, after_own, gain_rows, vectors, gate_w, doc_start,
         grad_tokens, block_out, grad_mix, small_sums, block_sums, gain_sums,
-        work, small_work, own_tokens, own_upstream, out_part, d_after_low, d_after_own, gain_mid,
-        d_mixed, tail_a, d_gates, d_both, d_first, small, rim_send, rim_recv, totals, totals_in, after,
-        far_a, near_a, far_b, near_b, far_c, near_c, mix_scratch, small_scratch, *rest,
+        work, small_work, own_tokens, own_upstream, mid_part, out_part, d_after_low, d_after_own, gain_mid,
+        d_mixed, tail_a, d_gates, d_both, small, rim_send, rim_recv, totals, totals_in, after,
+        far_a, near_a, far_b, near_b, mix_scratch, small_scratch, *rest,
     )
 
 
 def back_steps(
-    mid_part, hidden, mlp_full, mix_full, states, pre, ext, decay_g, input_g, conv_low, entering, mixed,
-    normed_in, tokens, upstream, after_own, gain_rows, vectors, gate_w, doc_start,
+    mlp_saved, saved, mlp_full, mix_full, hidden, states, pre, ext, decay_g, input_g,
+    conv_low, entering, mixed, normed_in, tokens, upstream, after_own, gain_rows, vectors, gate_w, doc_start,
     grad_tokens, block_out, grad_mix, small_sums, block_sums, gain_sums,
-    work, small_work, own_tokens, own_upstream, out_part, d_after_low, d_after_own, gain_mid,
-    d_mixed, tail_a, d_gates, d_both, d_first, small, rim_send, rim_recv, totals, totals_in, after,
-    far_a, near_a, far_b, near_b, far_c, near_c, mix_scratch, small_scratch,
+    work, small_work, own_tokens, own_upstream, mid_part, out_part, d_after_low, d_after_own, gain_mid,
+    d_mixed, tail_a, d_gates, d_both, small, rim_send, rim_recv, totals, totals_in, after,
+    far_a, near_a, far_b, near_b, mix_scratch, small_scratch,
     small_all,
     gain_in,
     gain_y,
     gain_s,
     gain_z,
     local,
+    tiles,
     send,
     recv,
 ):
     p = Place()
     links = Links(send, recv)
-    loads = []
-    for f in range(CHUNKS):
-        lo = 3 * f * CHUNK + 2 * CHUNK
-        source = mlp_full.at[:, :, :, :, pl.ds(lo, CHUNK)]
-        copy = pltpu.make_async_copy(source, work.at[:, :, :, :, pl.ds(f * CHUNK, CHUNK)], local.at[f])
+    sib = mix_scratch[0]
+    early = (
+        pltpu.make_async_copy(mlp_saved[0], sib.at[pl.ds(0, 2), :, :, pl.ds(0, MLP)], local.at[0]),
+        pltpu.make_async_copy(mlp_saved[1], sib.at[pl.ds(2, 2), :, :, pl.ds(0, MLP)], local.at[1]),
+    )
+    for copy in early:
         copy.start()
-        loads.append(copy)
-    load_tokens = pltpu.make_async_copy(tokens.at[p.y], own_tokens, local.at[CHUNKS])
+
+    def weight_tile(n, j, slot):
+        source = mlp_full.at[n // 2, n % 2, :, :, pl.ds(j * MLP, MLP)]
+        return pltpu.make_async_copy(source, work.at[slot // 2, slot % 2, :, :, pl.ds(0, MLP)], tiles.at[slot])
+
+    fetched = {}
+
+    def fetch(n):
+        for j in range(2):
+            fetched[n, j] = weight_tile(n, j, (2 * n + j) % 8)
+            fetched[n, j].start()
+
+    for n in range(3):
+        fetch(n)
+    hidden_load = pltpu.make_async_copy(mlp_saved[2], hidden, local.at[2])
+    hidden_load.start()
+    saved_loads = [
+        pltpu.make_async_copy(source, target, local.at[3 + k]) for k, (source, target) in enumerate(saved)
+    ]
+    load_tokens = pltpu.make_async_copy(tokens.at[p.y], own_tokens, local.at[12])
     load_tokens.start()
-    load_upstream = pltpu.make_async_copy(upstream.at[p.y], own_upstream, local.at[CHUNKS + 1])
+    load_upstream = pltpu.make_async_copy(upstream.at[p.y], own_upstream, local.at[13])
     load_upstream.start()
     others_y = [{"tensor": lax.rem(p.y + d, 4)} for d in (1, 2, 3)]
     others_z = [{"dp": lax.rem(p.z + d, 4)} for d in (1, 2, 3)]
     greet([p.seq_at(d) for d in range(1, 8)] + others_y + others_z)
-    middle = Reduce(links, p, mid_part, far_c, near_c)
-    middle.send_first()
+    middle = Reduce(links, p, mid_part, far_a, near_a)
+    for copy in early:
+        copy.wait()
+
+    def tile_of(slot):
+        return work[slot // 2, slot % 2, :, :, 0:MLP].reshape(256, MLP)
+
+    for n in range(8):
+        if n + 3 < 8:
+            fetch(n + 3)
+        if n == 4:
+            middle.send_first()
+        for j in range(2):
+            fetched[n, j].wait()
+        at = slice(n * 256, (n + 1) * 256)
+        product = dot_nt(sib[0:2, :, :, 0:MLP].reshape(TOKENS, MLP), tile_of(2 * n % 8)) + dot_nt(
+            sib[2:4, :, :, 0:MLP].reshape(TOKENS, MLP), tile_of((2 * n + 1) % 8)
+        )
+        mid_part[:, :, at] = product.astype(BF16).reshape(ROWS, SPAN, 256)
     middle.send_second()
-    for copy in loads:
+    downs = [weight_tile(n, 2, n) for n in range(8)]
+    for copy in downs + saved_loads:
+        copy.start()
+    hidden_load.wait()
+    for copy in downs:
         copy.wait()
 
     def out_product(n, carry):
@@ -939,10 +1031,13 @@
         out_part[:, :, pl.ds(pl.multiple_of(n * 256, 256), 256)] = product.reshape(ROWS, SPAN, 256)
         return carry
 
-    lax.fori_loop(0, 8, out_product, 0)
-    load = pltpu.make_async_copy(mix_full, work, local.at[CHUNKS + 2])
+    lax.fori_loop(0, 4, out_product, 0)
+    middle.merge()
+    lax.fori_loop(4, 8, out_product, 0)
+    load = pltpu.make_async_copy(mix_full, work, local.at[14])
     load.start()
-    middle.merge()
+    for copy in saved_loads:
+        copy.wait()
     gain_mid[...] = jnp.zeros_like(gain_mid)
     gain_1 = gain_rows[1:2, :].astype(F32)
     load_upstream.wait()
@@ -958,6 +1053,7 @@
         return carry
 
     lax.fori_loop(0, SPAN // 16, middle_rows, 0)
+    links.sent([middle.k0, middle.k1, middle.k2, middle.k3, middle.k4, middle.k5])
     spread_c = Spread(links, p, d_after_low)
     spread_c.start()
     load.wait()
@@ -1045,16 +1141,13 @@
         return carry
 
     lax.fori_loop(0, ROWS * GROUPS, gates_back, 0)
-    ahead.settle()
 
     def ahead_rows(k, carry):
         at = pl.ds(pl.multiple_of(k * 16, 16), 16)
         block_out[p.y, at, :] = (after_own[at, :] + own_sum(ahead, at)).astype(BF16)
         return carry
 
-    lax.fori_loop(0, SPAN // 16, ahead_rows, 0)
     spread_b = Spread(links, p, block_out)
-    spread_b.start()
 
     d_conv = tail_a
     held = None
@@ -1124,7 +1217,6 @@
     small_scatter = Scatter(links, p, small_work, *small_scratch)
     for xx in range(4):
         small_scatter.give(xx)
-    spread_b.forward()
     links.arrived(rim_recv, k_rim, p.seq_at(1))
     for r in range(ROWS):
         last = r * SPAN + SPAN - 8
@@ -1138,7 +1230,11 @@
         d_first[:, :, pl.ds(pl.multiple_of(n * 256, 256), 256)] = product.reshape(ROWS, SPAN, 256)
         return carry
 
+    d_first = mid_part
     back = Reduce(links, p, d_first, far_a, near_a)
+    ahead.settle()
+    lax.fori_loop(0, SPAN // 16, ahead_rows, 0)
+    spread_b.start_first()
     lax.fori_loop(0, 4, first_part, 0)
     back.send_first()
     lax.fori_loop(4, 8, first_part, 0)
@@ -1170,6 +1266,7 @@
         scatter.give(xx)
     small_scatter.merge()
     back.merge()
+    spread_b.start_second()
     lax.fori_loop(0, 4, keep, 0)
     small_scatter.turn()
     for xx in range(4):
@@ -1190,6 +1287,7 @@
     lax.fori_loop(0, SPAN // 16, back_rows, 0)
     spread_a = Spread(links, p, grad_tokens)
     spread_a.start()
+    spread_b.forward()
     gain_y[p.y] = jnp.concatenate(
         [jnp.sum(gain_in[...], axis=0, keepdims=True), jnp.sum(gain_mid[...], axis=0, keepdims=True)], axis=0
     )
@@ -1199,7 +1297,7 @@
         small_all[p.x, p.c, p.z, base : base + 32, :] = value.astype(BF16)
 
     small_scatter.finish(store_small)
-    small_gather = Gather(links, p, small_all)
+    small_gather = Gather(links, p, small_all, 128)
     small_gather.first()
     scatter.merge()
     for d in (1, 2, 3):
@@ -1258,13 +1356,24 @@
             shape((2 * HEADS * BLK, 256), F32),
             shape((2, WIDTH), F32),
         ],
-        in_specs=[vmem()] * 2 + [anyspace()] * 2 + [vmem()] * 9 + [anyspace()] * 2 + [vmem()] * 4 + [smem()],
+        in_specs=[anyspace()] * 14 + [vmem()] + [anyspace()] * 2 + [vmem()] * 3 + [smem()],
         out_specs=[vmem()] * 6,
         scratch_shapes=[
+            pltpu.VMEM((TOKENS, MLP), BF16),
+            pltpu.VMEM(tc, F32),
+            pltpu.VMEM(tc, F32),
+            pltpu.VMEM((ROWS, PAD + SPAN, CHAN), F32),
+            pltpu.VMEM(tc, F32),
+            pltpu.VMEM(tc, F32),
+            pltpu.VMEM(tc, BF16),
+            pltpu.VMEM(tc, BF16),
+            pltpu.VMEM((TOKENS, WIDTH), BF16),
+            pltpu.VMEM((SPAN, WIDTH), F32),
             pltpu.VMEM((4, 2, 4, 64, MIX_COLS), BF16),
             pltpu.VMEM((4, 2, 4, 64, SMALL), BF16),
             pltpu.VMEM((SPAN, WIDTH), BF16),
             pltpu.VMEM((SPAN, WIDTH), BF16),
+            pltpu.VMEM((ROWS, SPAN, WIDTH), BF16),
             pltpu.VMEM((ROWS, SPAN, WIDTH), BF16),
             pltpu.VMEM((ROWS, SPAN, WIDTH), BF16),
             pltpu.VMEM((SPAN, WIDTH), F32),
@@ -1273,7 +1382,6 @@
             pltpu.VMEM(tc, F32),
             pltpu.VMEM((TOKENS, 2 * CHAN), BF16),
             pltpu.VMEM((TOKENS, 2 * CHAN), BF16),
-            pltpu.VMEM((ROWS, SPAN, WIDTH), BF16),
             pltpu.VMEM((8, CHAN), F32),
             pltpu.VMEM((ROWS, PAD, CHAN), F32),
             pltpu.VMEM((ROWS, PAD, CHAN), F32),
@@ -1281,7 +1389,7 @@
             pltpu.VMEM((8, 8, CHAN), F32),
             pltpu.VMEM((8, CHAN), F32),
         ]
-        + pair * 3
+        + pair * 2
         + Scatter.scratch(MIX_COLS)
         + Scatter.scratch(SMALL)
         + [
@@ -1290,7 +1398,8 @@
             pltpu.VMEM((4, 2, WIDTH), F32),
             pltpu.VMEM((8, 2, WIDTH), F32),
             pltpu.VMEM((4, 2, WIDTH), F32),
-            pltpu.SemaphoreType.DMA((CHUNKS + 3,)),
+            pltpu.SemaphoreType.DMA((15,)),
+            pltpu.SemaphoreType.DMA((8,)),
             pltpu.SemaphoreType.DMA((184,)),
             pltpu.SemaphoreType.DMA((184,)),
         ],
@@ -1302,14 +1411,12 @@
 def finish_kernel(
     block_in,
     tokens_in,
-    states_in,
     mix_sum,
     small,
     blocks_in,
     gains_in,
     mlp_sum,
     block_out,
-    states,
     grad_tokens,
     grad_gains,
     grad_mix_in,
@@ -1323,7 +1430,6 @@
     step = pl.program_id(0)
     block_out[...] = block_in[...]
     grad_tokens[...] = tokens_in[...]
-    states[...] = states_in[...]
     for h in range(HEADS):
 
         @pl.when(step == h)
@@ -1356,7 +1462,6 @@
         grid=(ROWS,),
         out_shape=[
             shape((ROWS, SPAN, WIDTH), BF16),
-            shape((ROWS, SPAN, CHAN), F32),
             shape((ROWS, SPAN, WIDTH), BF16),
             shape((2, WIDTH), F32),
             shape((2, 64, CHAN), F32),
@@ -1370,7 +1475,6 @@
         in_specs=[
             row(WIDTH),
             row(WIDTH),
-            row(CHAN),
             whole(64, MIX_COLS),
             whole(8, CHAN),
             head(256),
@@ -1379,7 +1483,6 @@
         ],
         out_specs=[
             row(WIDTH),
-            row(CHAN),
             row(WIDTH),
             whole(2, WIDTH),
             whole(2, 64, CHAN),
@@ -1450,14 +1553,16 @@
         raw_vectors,
         gate_w,
     )
-    mid_part, hidden, grad_mlp = mlp_all(
+    d_gate, d_up, hidden, grad_mlp, states_out = mlp_all(
         normed_mid.reshape(TOKENS, WIDTH),
         cotangent.reshape(TOKENS, WIDTH),
         mlp_full.reshape(WIDTH, MLP_COLS),
+        states.reshape(ROWS, SPAN, CHAN),
     )
     grad_mlp = lax.psum_scatter(grad_mlp, ("seq", "dp"), scatter_dimension=0, tiled=True)
     grad_tokens, block_out, grad_mix, small, blocks, grad_gains = back_all(
-        mid_part.reshape(ROWS, SPAN, WIDTH),
+        d_gate.reshape(2, 4, 64, MLP),
+        d_up.reshape(2, 4, 64, MLP),
         hidden,
         mlp_full,
         mix_full,
@@ -1467,12 +1572,12 @@
         decay_g,
         input_g,
         conv_low,
-        entering,
         mixed,
         normed_in,
+        after_own,
+        entering,
         tokens,
         cotangent,
-        after_own,
         norm_gains,
         vectors,
         gate_w,
@@ -1480,7 +1585,6 @@
     )
     (
         block_out,
-        states,
         grad_tokens,
         grad_gains,
         grad_mix_in,
@@ -1493,7 +1597,6 @@
     ) = finish(
         block_out,
         grad_tokens,
-        states.reshape(ROWS, SPAN, CHAN),
         grad_mix,
         small,
         blocks.reshape(2, HEADS, BLK, 256),
@@ -1502,7 +1605,7 @@
     )
     return (
         block_out,
-        states,
+        states_out,
         grad_tokens,
         grad_gains,
         grad_mix_in,

time: 338 us -> 316 us (0.935)
  Pallas kernels: 316 us -> 295 us
    pallas_call x1, Pallas kernels: 126 us -> 107 us  [mix_forward(): pl.pallas_call(mix_forward_kernel, out_shape=outs, in_specs=[vmem()] * 7...]
    pallas_call x1, Pallas kernels: 39.4 us -> 32.5 us  [mlp_all(): pl.pallas_call(mlp_kernel, grid=(CHUNKS,), out_shape=[shape((TOKENS, MLP)...]
    pallas_call x1, Pallas kernels: 143 us -> 148 us  [back_all(): pl.pallas_call(back_kernel, out_shape=[shape((ROWS, SPAN, WIDTH), BF16),...]
  transfers between devices with their start and end apart: 1 -> 1, of which waited for: 0 -> 0; matrix products, arithmetic and copies ran while one was open for 1% -> 1% of each run, Pallas kernels for 42% -> 47%
where the time goes in v4:
time: 316 us; the launch traced here: 315 us
  Pallas kernels  295 us (93%)
  between operations  14.1 us (4%)
  local copies, waits for them, and re-layouts  4.27 us (1%)
    pallas_call x1, Pallas kernels, back_all(): pl.pallas_call(back_kernel, out_shape=[shape((ROWS, SPAN, WIDTH), BF16),...  148 us
    pallas_call x1, Pallas kernels, mix_forward(): pl.pallas_call(mix_forward_kernel, out_shape=outs, in_specs=[vmem()] * 7...  107 us
    pallas_call x1, Pallas kernels, mlp_all(): pl.pallas_call(mlp_kernel, grid=(CHUNKS,), out_shape=[shape((TOKENS, MLP)...  32.5 us
    pallas_call x1, Pallas kernels, finish(): pl.pallas_call(finish_kernel, grid=(ROWS,), out_shape=[shape((ROWS, SPAN,...  6.55 us
  transfers between devices with their start and end apart: 1, of which 0 were waited for; matrix products, arithmetic and copies ran while one was open for 1% of the time, Pallas kernels for 47%

profile of v4, /device:TPU:1, one launch (start us, length us, event | category | flops | bytes accessed | tf_op | source)
XLA Modules:
  0.0 315.4 jit_solution(17243878307611448115)
XLA Ops:
  7.2 0.0 copy-start.2
  7.2 0.0 copy-start.1
  7.2 0.0 reduce-scatter.2.cloned.1.call-start
  7.2 0.7 broadcast_in_dim.6
  7.9 0.7 broadcast_in_dim.7
  8.6 1.2 slice_bitcast_fusion.3
  9.8 0.1 pad_bitcast_fusion.2
  9.9 0.2 pad_bitcast_fusion
  10.1 0.0 copy-done.2
  10.1 0.0 copy-done.1
  10.1 0.6 pad_maximum_fusion.1.raw_vectors
  10.7 1.1 pad_maximum_fusion.gate_w
  11.8 107.2 %mix_forward.1 = (bf16[4,2,4,64,1920]{4,3,2,1,0:T(8,128)(2,1)}, bf16[4,2,4,64,4608]{4,3,2,1,0:T(8,128)(2,1)}, f32[512,640]{1,0:T(8,128)}, f32[512,640]{1,0:T(8,1...) custom-call(bf16[512,2048]{1,0:T(8,128)(2,1)} %bitcast.40, ...), custom_call_target="tpu_custom_call" | custom-call | tf_op jit(solution)/shard_map/mix_forward/pallas_call | solution.py:645
  119.1 32.5 %mlp_all.1 = (bf16[512,1536]{1,0:T(8,128)(2,1)}, bf16[512,1536]{1,0:T(8,128)(2,1)}, bf16[512,1536]{1,0:T(8,128)(2,1)}, bf16[2048,4608]{1,0:T(8,128)(2,1)}, f32[4,128,640]{2,1,0:T(8,128)}) custom-call(bf16[512,2048]{1,0:T(8,128)(2,1)} %bitcast.49, bf16[512,2048]{1,0:T(8,128)(2,1)} %bitcast.41, bf16[2048,4608]{1,0:T(8,128)(2,1)} %bitcast.37, ...), custom_call_target="tpu_custom_call" | custom-call | flops 19327352832 | bytes 37748736 | tf_op jit(solution)/shard_map/mlp_all/pallas_call | solution.py:727
  151.6 0.0 reduce-scatter.2.cloned.1.call-update
  151.6 0.0 copy-start
  151.6 148.3 %back_all.1 = (bf16[4,128,2048]{2,1,0:T(8,128)(2,1)}, bf16[4,128,2048]{2,1,0:T(8,128)(2,1)}, f32[64,1920]{1,0:T(8,128)}, f32[8,640]{1,0:T(8,128)}, f32[1280,256]{1,0:T(8,128)}, /*index=5*/f32[2,2048]{1,0:T(2,128)}) custom-call(bf16[2,4,64,1536]{3,2,1,0:T(8,128)(2,1)} %bitcast.42, bf16[2,4,64,1536]{3,2,1,0:T(8,128)(2,1)} %bitcast.43, ...), custom_call_target="tpu_custom_call" | custom-call | tf_op jit(solution)/shard_map/back_all/pallas_call | solution.py:1349
  299.9 1.4 slice_reduce_fusion
  301.4 0.0 copy-done
  301.4 0.6 divide_multiply_fusion
  302.0 0.0 reduce-scatter.2.cloned.1.call-done.mlp_sum
  302.0 6.6 %finish.1 = (bf16[4,128,2048]{2,1,0:T(8,128)(2,1)}, bf16[4,128,2048]{2,1,0:T(8,128)(2,1)}, f32[2,2048]{1,0:T(2,128)}, f32[2,64,640]{2,1,0:T(8,128)}, f32[64,640]...) custom-call(bf16[4,128,2048]{2,1,0:T(8,128)(2,1)} %get-tuple-element, ...), custom_call_target="tpu_custom_call" | custom-call | tf_op jit(solution)/shard_map/finish/pallas_call | solution.py:1460
Async XLA Ops:
  7.2 2.9 copy-start.2
  7.2 2.9 copy-start.1
  7.2 294.8 %reduce-scatter.2.cloned.1.call-start = ((), (), s32[]{:S(2)}) async-start(), calls=%async_computation.1 | async-start | bytes 19464192 | tf_op jit(solution)/shard_map/reduce_scatter | solution.py:1562
  151.6 149.8 %copy-start = (bf16[640]{0:T(1024)(128)(2,1)S(1)}, bf16[640]{0:T(1024)(128)(2,1)}, u32[]{:S(2)}) copy-start(bf16[640]{0:T(1024)(128)(2,1)} %param.28) | copy-start | bytes 3844
Sparse Core Ops, SparseCore 0:
  151.7 129.4 reduce-scatter.1

commit v5 on v4

--- a/solution.py
+++ b/solution.py
@@ -195,6 +195,16 @@
         self.k1 = self.links.go(part.at[p.y2, :, CB], self.far.at[1], p.YL)
         self.k2 = self.links.go(part.at[p.yr, :, CB], near.at[0, :, CB], p.YR)
 
+    def send_far(self):
+        p, part = self.p, self.part
+        self.k0 = self.links.go(part.at[p.y2, :, CA], self.far.at[0], p.YR)
+        self.k1 = self.links.go(part.at[p.y2, :, CB], self.far.at[1], p.YL)
+
+    def send_near(self):
+        p, part, near = self.p, self.part, self.near
+        self.k2 = self.links.go(part.at[p.yr, :, CB], near.at[0, :, CB], p.YR)
+        self.k3 = self.links.go(part.at[p.yl, :, CA], near.at[1, :, CA], p.YL)
+
     def merge(self):
         p, part, near, far = self.p, self.part, self.near, self.far
         self.links.arrived(far.at[0], self.k0, p.YL)
@@ -315,10 +325,25 @@
     return jnp.sum(jnp.where(row == r, ref[:, at], 0.0), axis=0, keepdims=True)
 
 
-def assemble_vectors(vectors, raw):
-    value = raw[...].astype(F32)
-    row = lax.broadcasted_iota(jnp.int32, value.shape, 0)
-    vectors[...] = jnp.where(row == 7, -rate_scale * jnp.log1p(jnp.exp(jnp.where(row == 7, value, 0.0))), value)
+def assemble_vectors(vectors, conv_weight, conv_bias, gate_bias, decay_param):
+    vectors[0:4, :] = conv_weight[...].astype(F32)
+    vectors[4:5, :] = conv_bias[...].astype(F32).reshape(1, CHAN)
+    vectors[5:7, :] = gate_bias[...].astype(F32)
+    decay = decay_param[...].astype(F32).reshape(1, CHAN)
+    vectors[7:8, :] = -rate_scale * jnp.log1p(jnp.exp(decay))
+
+
+def assemble_gates(gate_w, gate_blocks):
+    for j in range(2):
+        for h in range(HEADS):
+            before, behind = 32 * h, 96 - 32 * h
+            block = gate_blocks[j, h].astype(F32)
+            parts = [jnp.zeros((BLK, before), F32)] if before else []
+            parts += [block] + ([jnp.zeros((BLK, behind), F32)] if behind else [])
+            wide = jnp.concatenate(parts, axis=1)
+            tall = [jnp.zeros((before, 256), F32)] if before else []
+            tall += [wide] + ([jnp.zeros((behind, 256), F32)] if behind else [])
+            gate_w[j, h] = jnp.concatenate(tall, axis=0).astype(BF16)
 
 
 def mix_forward_kernel(
@@ -332,8 +357,11 @@
     fresh_rows,
     doc_start,
     gain_rows,
-    raw_vectors,
-    gate_w,
+    conv_weight,
+    conv_bias,
+    gate_bias,
+    decay_param,
+    gate_blocks,
     mix_full_out,
     mlp_full,
     states_out,
@@ -346,11 +374,13 @@
     normed_in_out,
     entering_out,
     vectors_out,
+    gate_w_out,
     normed_mid,
     after_own,
     mlp_own,
     gains,
     vectors,
+    gate_w,
     mix_full,
     normed_in,
     pre,
@@ -391,7 +421,8 @@
     own_mlp = pltpu.make_async_copy(mlp_own, mlp_full.at[p.x, p.c, p.z], local.at[0])
     own_mlp.start()
     gains[...] = gain_rows[...].astype(F32)
-    assemble_vectors(vectors, raw_vectors)
+    assemble_vectors(vectors, conv_weight, conv_bias, gate_bias, decay_param)
+    assemble_gates(gate_w, gate_blocks)
 
     def norm_rows(first, last):
         def one(k, carry):
@@ -426,6 +457,7 @@
 
     save(normed_in, normed_in_out)
     save(vectors, vectors_out)
+    save(gate_w, gate_w_out)
 
     def project(n, carry):
         at = pl.ds(pl.multiple_of(n * 256, 256), 256)
@@ -612,6 +644,7 @@
         shape((TOKENS, WIDTH), BF16),
         shape((8, CHAN), F32),
         shape((8, CHAN), F32),
+        shape((2, HEADS, 256, 256), BF16),
         shape((ROWS, SPAN, WIDTH), BF16),
         shape((SPAN, WIDTH), F32),
     ]
@@ -619,6 +652,7 @@
         pltpu.VMEM((64, MLP_COLS), BF16),
         pltpu.VMEM((2, WIDTH), F32),
         pltpu.VMEM((8, CHAN), F32),
+        pltpu.VMEM((2, HEADS, 256, 256), BF16),
         pltpu.VMEM((4, 2, 4, 64, MIX_COLS), BF16),
         pltpu.VMEM((TOKENS, WIDTH), BF16),
         pltpu.VMEM((TOKENS, 2 * CHAN), F32),
@@ -638,15 +672,15 @@
         pltpu.VMEM((ROWS, SPAN, WIDTH), BF16),
         pltpu.VMEM((2, SPAN, HALF), BF16),
         pltpu.VMEM((2, SPAN, WIDTH), BF16),
-        pltpu.SemaphoreType.DMA((16,)),
+        pltpu.SemaphoreType.DMA((20,)),
         pltpu.SemaphoreType.DMA((184,)),
         pltpu.SemaphoreType.DMA((184,)),
     ]
     return pl.pallas_call(
         mix_forward_kernel,
         out_shape=outs,
-        in_specs=[vmem()] * 7 + [smem()] * 2 + [vmem()] * 3,
-        out_specs=[anyspace()] * 12 + [vmem()] * 2,
+        in_specs=[vmem()] * 7 + [smem()] * 2 + [vmem()] * 6,
+        out_specs=[anyspace()] * 13 + [vmem()] * 2,
         scratch_shapes=scratch,
         compiler_params=params(0),
         name="mix_forward",
@@ -1019,11 +1053,14 @@
         mid_part[:, :, at] = product.astype(BF16).reshape(ROWS, SPAN, 256)
     middle.send_second()
     downs = [weight_tile(n, 2, n) for n in range(8)]
-    for copy in downs + saved_loads:
+    for copy in downs:
         copy.start()
+    middle.merge()
     hidden_load.wait()
     for copy in downs:
         copy.wait()
+    for copy in saved_loads:
+        copy.start()
 
     def out_product(n, carry):
         weights = work[lax.div(n, 2), lax.rem(n, 2), :, :, 0:MLP].reshape(256, MLP)
@@ -1031,9 +1068,7 @@
         out_part[:, :, pl.ds(pl.multiple_of(n * 256, 256), 256)] = product.reshape(ROWS, SPAN, 256)
         return carry
 
-    lax.fori_loop(0, 4, out_product, 0)
-    middle.merge()
-    lax.fori_loop(4, 8, out_product, 0)
+    lax.fori_loop(0, 8, out_product, 0)
     load = pltpu.make_async_copy(mix_full, work, local.at[14])
     load.start()
     for copy in saved_loads:
@@ -1067,13 +1102,13 @@
 
     mixed_row(p.y)
     spread_c.forward()
+    ahead = Reduce(links, p, out_part, far_b, near_b)
+    ahead.send_far()
+    ahead.send_near()
     spread_c.near()
     mixed_row(p.yl)
     mixed_row(p.yr)
     spread_c.far()
-    ahead = Reduce(links, p, out_part, far_b, near_b)
-    ahead.send_first()
-    ahead.send_second()
     mixed_row(p.y2)
     small[...] = jnp.zeros_like(small)
     totals[...] = jnp.zeros_like(totals)
@@ -1272,6 +1307,9 @@
     for xx in range(4):
         scatter.take(xx)
     scatter.first()
+    def store_small(base, value):
+        small_all[p.x, p.c, p.z, base : base + 32, :] = value.astype(BF16)
+
     small_scatter.merge_2()
     back.settle()
     load_tokens.wait()
@@ -1287,27 +1325,24 @@
     lax.fori_loop(0, SPAN // 16, back_rows, 0)
     spread_a = Spread(links, p, grad_tokens)
     spread_a.start()
-    spread_b.forward()
+    small_scatter.finish(store_small)
+    small_gather = Gather(links, p, small_all, 128)
+    small_gather.first()
     gain_y[p.y] = jnp.concatenate(
         [jnp.sum(gain_in[...], axis=0, keepdims=True), jnp.sum(gain_mid[...], axis=0, keepdims=True)], axis=0
     )
     y_keys = [links.go(gain_y.at[p.y], gain_y.at[p.y], device) for device in others_y]
 
-    def store_small(base, value):
-        small_all[p.x, p.c, p.z, base : base + 32, :] = value.astype(BF16)
-
-    small_scatter.finish(store_small)
-    small_gather = Gather(links, p, small_all, 128)
-    small_gather.first()
     scatter.merge()
+    small_gather.middle()
+    small_gather.finish()
+    small_gather.second()
+    spread_a.forward()
+    spread_b.forward()
     for d in (1, 2, 3):
         links.arrived(gain_y.at[lax.rem(p.y + 4 - d, 4)], y_keys[d - 1], others_y[0])
     gain_z[p.z] = gain_y[0] + gain_y[1] + gain_y[2] + gain_y[3]
     z_keys = [links.go(gain_z.at[p.z], gain_z.at[p.z], device) for device in others_z]
-    small_gather.middle()
-    small_gather.finish()
-    small_gather.second()
-    spread_a.forward()
     scatter.turn()
     for d in (1, 2, 3):
         links.arrived(gain_z.at[lax.rem(p.z + 4 - d, 4)], z_keys[d - 1], others_z[0])
@@ -1416,14 +1451,17 @@
     blocks_in,
     gains_in,
     mlp_sum,
+    decay_param,
     block_out,
     grad_tokens,
     grad_gains,
     grad_mix_in,
     grad_mix_out,
     grad_conv,
+    grad_conv_bias,
     grad_blocks,
     grad_bias,
+    grad_decay,
     grad_mlp_in,
     grad_mlp_out,
 ):
@@ -1445,6 +1483,9 @@
         grad_mix_out[...] = mix_sum[:, 2 * CHAN :]
         grad_conv[...] = small[0:CONV, :]
         grad_bias[...] = small[CONV + 1 : CONV + 3, :]
+        grad_conv_bias[...] = small[CONV : CONV + 1, :].reshape(CHAN)
+        slope = jax.nn.sigmoid(decay_param[...].astype(F32))
+        grad_decay[...] = small[CONV + 3 : CONV + 4, :].reshape(CHAN) * slope
         for f in range(CHUNKS):
             lo, at = 3 * f * CHUNK, pl.ds(f * CHUNK, CHUNK)
             for j in range(2):
@@ -1467,8 +1508,10 @@
             shape((2, 64, CHAN), F32),
             shape((64, CHAN), F32),
             shape((CONV, CHAN), F32),
+            shape((CHAN,), F32),
             shape((2, HEADS, BLK, BLK), F32),
             shape((2, CHAN), F32),
+            shape((CHAN,), F32),
             shape((2, 64, MLP), F32),
             shape((64, MLP), F32),
         ],
@@ -1480,6 +1523,7 @@
             head(256),
             whole(2, WIDTH),
             whole(64, MLP_COLS),
+            whole(CHAN),
         ],
         out_specs=[
             row(WIDTH),
@@ -1488,8 +1532,10 @@
             whole(2, 64, CHAN),
             whole(64, CHAN),
             whole(CONV, CHAN),
+            whole(CHAN),
             head(BLK),
             whole(2, CHAN),
+            whole(CHAN),
             whole(2, 64, MLP),
             whole(64, MLP),
         ],
@@ -1516,14 +1562,6 @@
     mlp_out,
     cotangent,
 ):
-    gate_w = jnp.stack(
-        [
-            jnp.pad(gate_blocks[:, h], ((0, 0), (32 * h, 96 - 32 * h), (32 * h, 96 - 32 * h)))
-            for h in range(HEADS)
-        ],
-        axis=1,
-    )
-    raw_vectors = jnp.concatenate([conv_weight, conv_bias[None], gate_bias, decay_param[None]], axis=0)
     (
         mix_full,
         mlp_full,
@@ -1537,6 +1575,7 @@
         normed_in,
         entering,
         vectors,
+        gate_w,
         normed_mid,
         after_own,
     ) = mix_forward(
@@ -1550,8 +1589,11 @@
         fresh_rows,
         doc_start,
         norm_gains,
-        raw_vectors,
-        gate_w,
+        conv_weight,
+        conv_bias,
+        gate_bias,
+        decay_param,
+        gate_blocks,
     )
     d_gate, d_up, hidden, grad_mlp, states_out = mlp_all(
         normed_mid.reshape(TOKENS, WIDTH),
@@ -1590,8 +1632,10 @@
         grad_mix_in,
         grad_mix_out,
         grad_conv,
+        grad_conv_bias,
         grad_blocks,
         grad_bias,
+        grad_decay,
         grad_mlp_in,
         grad_mlp_out,
     ) = finish(
@@ -1602,6 +1646,7 @@
         blocks.reshape(2, HEADS, BLK, 256),
         grad_gains,
         grad_mlp,
+        decay_param,
     )
     return (
         block_out,
@@ -1611,10 +1656,10 @@
         grad_mix_in,
         grad_mix_out.T,
         grad_conv,
-        small[CONV],
+        grad_conv_bias,
         grad_blocks,
         grad_bias,
-        small[CONV + 3] * jax.nn.sigmoid(decay_param.astype(F32)),
+        grad_decay,
         grad_mlp_in,
         grad_mlp_out.T,
     )

time: 316 us -> 304 us (0.962)
  Pallas kernels: 295 us -> 290 us
  local copies, waits for them, and re-layouts: 4.27 us -> 0 us
    pallas_call x1, Pallas kernels: 148 us -> 144 us  [back_all(): pl.pallas_call(back_kernel, out_shape=[shape((ROWS, SPAN, WIDTH), BF16),...]
  transfers between devices with their start and end apart: 1 -> 1, of which waited for: 0 -> 0; matrix products, arithmetic and copies ran while one was open for 1% -> 0% of each run, Pallas kernels for 47% -> 47%
where the time goes in v5:
time: 304 us
  Pallas kernels  290 us (95%)
  between operations  14.1 us (5%)
    pallas_call x1, Pallas kernels, back_all(): pl.pallas_call(back_kernel, out_shape=[shape((ROWS, SPAN, WIDTH), BF16),...  144 us
    pallas_call x1, Pallas kernels, mix_forward(): pl.pallas_call(mix_forward_kernel, out_shape=outs, in_specs=[vmem()] * 7...  107 us
    pallas_call x1, Pallas kernels, mlp_all(): pl.pallas_call(mlp_kernel, grid=(CHUNKS,), out_shape=[shape((TOKENS, MLP)...  32.5 us
    pallas_call x1, Pallas kernels, finish(): pl.pallas_call(finish_kernel, grid=(ROWS,), out_shape=[shape((ROWS, SPAN,...  6.59 us
  transfers between devices with their start and end apart: 1, of which 0 were waited for; matrix products, arithmetic and copies ran while one was open for 0% of the time, Pallas kernels for 47%

profile of v5, /device:TPU:1, one launch (start us, length us, event | category | flops | bytes accessed | tf_op | source)
XLA Modules:
  0.0 304.0 jit_solution(10588438161472752984)
XLA Ops:
  7.2 0.0 reduce-scatter.2.cloned.1.call-start
  7.2 107.3 %mix_forward.1 = (bf16[4,2,4,64,1920]{4,3,2,1,0:T(8,128)(2,1)}, bf16[4,2,4,64,4608]{4,3,2,1,0:T(8,128)(2,1)}, f32[512,640]{1,0:T(8,128)}, f32[512,640]{1,0:T(8,1...) custom-call(bf16[512,2048]{1,0:T(8,128)(2,1)} %bitcast.16, ...), custom_call_target="tpu_custom_call" | custom-call | tf_op jit(solution)/shard_map/mix_forward/pallas_call | solution.py:679
  114.5 32.5 %mlp_all.1 = (bf16[512,1536]{1,0:T(8,128)(2,1)}, bf16[512,1536]{1,0:T(8,128)(2,1)}, bf16[512,1536]{1,0:T(8,128)(2,1)}, bf16[2048,4608]{1,0:T(8,128)(2,1)}, f32[4,128,640]{2,1,0:T(8,128)}) custom-call(bf16[512,2048]{1,0:T(8,128)(2,1)} %bitcast.25, bf16[512,2048]{1,0:T(8,128)(2,1)} %bitcast.17, bf16[2048,4608]{1,0:T(8,128)(2,1)} %bitcast.13, ...), custom_call_target="tpu_custom_call" | custom-call | flops 19327352832 | bytes 37748736 | tf_op jit(solution)/shard_map/mlp_all/pallas_call | solution.py:761
  147.0 0.0 reduce-scatter.2.cloned.1.call-update
  147.0 143.5 %back_all.1 = (bf16[4,128,2048]{2,1,0:T(8,128)(2,1)}, bf16[4,128,2048]{2,1,0:T(8,128)(2,1)}, f32[64,1920]{1,0:T(8,128)}, f32[8,640]{1,0:T(8,128)}, f32[1280,256]{1,0:T(8,128)}, /*index=5*/f32[2,2048]{1,0:T(2,128)}) custom-call(bf16[2,4,64,1536]{3,2,1,0:T(8,128)(2,1)} %bitcast.18, bf16[2,4,64,1536]{3,2,1,0:T(8,128)(2,1)} %bitcast.19, ...), custom_call_target="tpu_custom_call" | custom-call | tf_op jit(solution)/shard_map/back_all/pallas_call | solution.py:1384
  290.5 0.0 reduce-scatter.2.cloned.1.call-done.mlp_sum
  290.6 6.6 %finish.1 = (bf16[4,128,2048]{2,1,0:T(8,128)(2,1)}, bf16[4,128,2048]{2,1,0:T(8,128)(2,1)}, f32[2,2048]{1,0:T(2,128)}, f32[2,64,640]{2,1,0:T(8,128)}, f32[64,640]...) custom-call(bf16[4,128,2048]{2,1,0:T(8,128)(2,1)} %get-tuple-element, ...), custom_call_target="tpu_custom_call" | custom-call | tf_op jit(solution)/shard_map/finish/pallas_call | solution.py:1501
Async XLA Ops:
  7.2 283.4 %reduce-scatter.2.cloned.1.call-start = ((), (), s32[]{:S(2)}) async-start(), calls=%async_computation.1 | async-start | bytes 19464192 | tf_op jit(solution)/shard_map/reduce_scatter | solution.py:1604
Sparse Core Ops, SparseCore 0:
  147.2 134.5 reduce-scatter.1

commit v6 on v5

--- a/solution.py
+++ b/solution.py
@@ -182,80 +182,88 @@
 
 
 class Reduce:
-    def __init__(self, links, place, part, far, near):
+    def __init__(self, links, place, part, far, near, start=0, size=SPAN):
         self.links, self.p, self.part, self.far, self.near = links, place, part, far, near
+        self.rows, self.span = pl.ds(start, size), slice(start, start + size)
 
     def send_first(self):
-        p, part, near = self.p, self.part, self.near
-        self.k0 = self.links.go(part.at[p.y2, :, CA], self.far.at[0], p.YR)
-        self.k3 = self.links.go(part.at[p.yl, :, CA], near.at[1, :, CA], p.YL)
+        p, part, near, rows = self.p, self.part, self.near, self.rows
+        self.k0 = self.links.go(part.at[p.y2, rows, CA], self.far.at[0, rows], p.YR)
+        self.k3 = self.links.go(part.at[p.yl, rows, CA], near.at[1, rows, CA], p.YL)
 
     def send_second(self):
-        p, part, near = self.p, self.part, self.near
-        self.k1 = self.links.go(part.at[p.y2, :, CB], self.far.at[1], p.YL)
-        self.k2 = self.links.go(part.at[p.yr, :, CB], near.at[0, :, CB], p.YR)
-
-    def send_far(self):
-        p, part = self.p, self.part
-        self.k0 = self.links.go(part.at[p.y2, :, CA], self.far.at[0], p.YR)
-        self.k1 = self.links.go(part.at[p.y2, :, CB], self.far.at[1], p.YL)
-
-    def send_near(self):
-        p, part, near = self.p, self.part, self.near
-        self.k2 = self.links.go(part.at[p.yr, :, CB], near.at[0, :, CB], p.YR)
-        self.k3 = self.links.go(part.at[p.yl, :, CA], near.at[1, :, CA], p.YL)
+        self.send_second_far()
+        self.send_second_near()
+
+    def send_second_far(self):
+        p, part, rows = self.p, self.part, self.rows
+        self.k1 = self.links.go(part.at[p.y2, rows, CB], self.far.at[1, rows], p.YL)
+
+    def send_second_near(self):
+        p, part, near, rows = self.p, self.part, self.near, self.rows
+        self.k2 = self.links.go(part.at[p.yr, rows, CB], near.at[0, rows, CB], p.YR)
 
     def merge(self):
-        p, part, near, far = self.p, self.part, self.near, self.far
-        self.links.arrived(far.at[0], self.k0, p.YL)
-        far[0] = (far[0].astype(F32) + part[p.yr, :, 0:HALF].astype(F32)).astype(BF16)
-        self.k4 = self.links.go(far.at[0], near.at[0, :, CA], p.YR)
-        self.links.arrived(far.at[1], self.k1, p.YR)
-        far[1] = (far[1].astype(F32) + part[p.yl, :, HALF:WIDTH].astype(F32)).astype(BF16)
-        self.k5 = self.links.go(far.at[1], near.at[1, :, CB], p.YL)
+        p, part, near, far, rows, span = self.p, self.part, self.near, self.far, self.rows, self.span
+        self.links.arrived(far.at[0, rows], self.k0, p.YL)
+        far[0, span] = (far[0, span].astype(F32) + part[p.yr, span, 0:HALF].astype(F32)).astype(BF16)
+        self.k4 = self.links.go(far.at[0, rows], near.at[0, rows, CA], p.YR)
+        self.links.arrived(far.at[1, rows], self.k1, p.YR)
+        far[1, span] = (far[1, span].astype(F32) + part[p.yl, span, HALF:WIDTH].astype(F32)).astype(BF16)
+        self.k5 = self.links.go(far.at[1, rows], near.at[1, rows, CB], p.YL)
 
     def settle(self):
-        p, near = self.p, self.near
-        self.links.arrived(near.at[0, :, CB], self.k2, p.YL)
-        self.links.arrived(near.at[1, :, CA], self.k3, p.YR)
-        self.links.arrived(near.at[0, :, CA], self.k4, p.YL)
-        self.links.arrived(near.at[1, :, CB], self.k5, p.YR)
+        p, near, rows = self.p, self.near, self.rows
+        self.links.arrived(near.at[0, rows, CB], self.k2, p.YL)
+        self.links.arrived(near.at[1, rows, CA], self.k3, p.YR)
+        self.links.arrived(near.at[0, rows, CA], self.k4, p.YL)
+        self.links.arrived(near.at[1, rows, CB], self.k5, p.YR)
+
+    def keys(self):
+        return [self.k0, self.k1, self.k2, self.k3, self.k4, self.k5]
 
 
 class Spread:
-    def __init__(self, links, place, out):
-        self.links, self.p, self.out = links, place, out
+    def __init__(self, links, place, out, start=0, size=SPAN):
+        self.links, self.p, self.out, self.rows = links, place, out, pl.ds(start, size)
+
+    def _go(self, y, columns, device):
+        view = self.out.at[y, self.rows, columns]
+        return self.links.go(view, view, device)
+
+    def _wait(self, y, columns, k, device):
+        self.links.arrived(self.out.at[y, self.rows, columns], k, device)
 
     def start(self):
         self.start_first()
         self.start_second()
 
     def start_first(self):
-        go, out, y, p = self.links.go, self.out, self.p.y, self.p
-        self.k0 = go(out.at[y, :, CA], out.at[y, :, CA], p.YR)
-        self.k1 = go(out.at[y, :, CB], out.at[y, :, CB], p.YL)
+        p = self.p
+        self.k0 = self._go(p.y, CA, p.YR)
+        self.k1 = self._go(p.y, CB, p.YL)
 
     def start_second(self):
-        go, out, y, p = self.links.go, self.out, self.p.y, self.p
-        self.k2 = go(out.at[y, :, CB], out.at[y, :, CB], p.YR)
-        self.k3 = go(out.at[y, :, CA], out.at[y, :, CA], p.YL)
+        p = self.p
+        self.k2 = self._go(p.y, CB, p.YR)
+        self.k3 = self._go(p.y, CA, p.YL)
 
     def forward(self):
-        go, out, p, arrived = self.links.go, self.out, self.p, self.links.arrived
-        arrived(out.at[p.yl, :, CA], self.k0, p.YL)
-        self.k4 = go(out.at[p.yl, :, CA], out.at[p.yl, :, CA], p.YR)
-        arrived(out.at[p.yr, :, CB], self.k1, p.YR)
-        self.k5 = go(out.at[p.yr, :, CB], out.at[p.yr, :, CB], p.YL)
+        p = self.p
+        self._wait(p.yl, CA, self.k0, p.YL)
+        self.k4 = self._go(p.yl, CA, p.YR)
+        self._wait(p.yr, CB, self.k1, p.YR)
+        self.k5 = self._go(p.yr, CB, p.YL)
 
     def near(self):
-        out, p, arrived = self.out, self.p, self.links.arrived
-        arrived(out.at[p.yl, :, CB], self.k2, p.YL)
-        arrived(out.at[p.yr, :, CA], self.k3, p.YR)
+        p = self.p
+        self._wait(p.yl, CB, self.k2, p.YL)
+        self._wait(p.yr, CA, self.k3, p.YR)
 
     def far(self):
-        out, p, arrived = self.out, self.p, self.links.arrived
-        arrived(out.at[p.y2, :, CA], self.k4, p.YL)
-        arrived(out.at[p.y2, :, CB], self.k5, p.YR)
+        p = self.p
+        self._wait(p.y2, CA, self.k4, p.YL)
+        self._wait(p.y2, CB, self.k5, p.YR)
 
 
 def dot(a, b):
@@ -748,7 +756,7 @@
         grads[at, 2 * CHUNK :] = dot(upstream_t[at, :], d_both[:, 2 * CHUNK :]).astype(BF16)
         return carry
 
-    lax.fori_loop(0, WIDTH // 256, tile, 0, unroll=2)
+    lax.fori_loop(0, WIDTH // 256, tile, 0, unroll=4)
 
 
 def mlp_all(normed, upstream, weights, states):
@@ -1032,7 +1040,7 @@
     others_y = [{"tensor": lax.rem(p.y + d, 4)} for d in (1, 2, 3)]
     others_z = [{"dp": lax.rem(p.z + d, 4)} for d in (1, 2, 3)]
     greet([p.seq_at(d) for d in range(1, 8)] + others_y + others_z)
-    middle = Reduce(links, p, mid_part, far_a, near_a)
+    middles = [Reduce(links, p, mid_part, far_a, near_a, t, SPAN // 2) for t in (0, SPAN // 2)]
     for copy in early:
         copy.wait()
 
@@ -1043,7 +1051,8 @@
         if n + 3 < 8:
             fetch(n + 3)
         if n == 4:
-            middle.send_first()
+            for middle in middles:
+                middle.send_first()
         for j in range(2):
             fetched[n, j].wait()
         at = slice(n * 256, (n + 1) * 256)
@@ -1051,11 +1060,15 @@
             sib[2:4, :, :, 0:MLP].reshape(TOKENS, MLP), tile_of((2 * n + 1) % 8)
         )
         mid_part[:, :, at] = product.astype(BF16).reshape(ROWS, SPAN, 256)
-    middle.send_second()
+    for middle in middles:
+        middle.send_second_far()
+    middles[0].send_second_near()
     downs = [weight_tile(n, 2, n) for n in range(8)]
     for copy in downs:
         copy.start()
-    middle.merge()
+    middles[0].merge()
+    middles[1].send_second_near()
+    middles[1].merge()
     hidden_load.wait()
     for copy in downs:
         copy.wait()
@@ -1076,21 +1089,23 @@
     gain_mid[...] = jnp.zeros_like(gain_mid)
     gain_1 = gain_rows[1:2, :].astype(F32)
     load_upstream.wait()
-    middle.settle()
 
     def middle_rows(k, carry):
         at = pl.ds(pl.multiple_of(k * 16, 16), 16)
-        through, share = norm_back_rows(own_sum(middle, at), after_own[at, :], gain_1)
+        through, share = norm_back_rows(own_sum(middles[0], at), after_own[at, :], gain_1)
         gain_mid[...] += share[0:8] + share[8:16]
         total = own_upstream[at, :].astype(F32) + through
         d_after_own[at, :] = total
         d_after_low[p.y, at, :] = total.astype(BF16)
         return carry
 
-    lax.fori_loop(0, SPAN // 16, middle_rows, 0)
-    links.sent([middle.k0, middle.k1, middle.k2, middle.k3, middle.k4, middle.k5])
-    spread_c = Spread(links, p, d_after_low)
-    spread_c.start()
+    spreads_c = []
+    for t, middle in enumerate(middles):
+        middle.settle()
+        lax.fori_loop(4 * t, 4 * t + 4, middle_rows, 0)
+        links.sent(middle.keys())
+        spreads_c.append(Spread(links, p, d_after_low, t * SPAN // 2, SPAN // 2))
+        spreads_c[t].start()
     load.wait()
     rows_low = d_after_low.reshape(TOKENS, WIDTH)
 
@@ -1101,14 +1116,17 @@
             d_mixed[rows, start : start + size] = dot(d_after_low[row], weights)
 
     mixed_row(p.y)
-    spread_c.forward()
+    for spread_c in spreads_c:
+        spread_c.forward()
     ahead = Reduce(links, p, out_part, far_b, near_b)
-    ahead.send_far()
-    ahead.send_near()
-    spread_c.near()
+    ahead.send_first()
+    ahead.send_second()
+    for spread_c in spreads_c:
+        spread_c.near()
     mixed_row(p.yl)
     mixed_row(p.yr)
-    spread_c.far()
+    for spread_c in spreads_c:
+        spread_c.far()
     mixed_row(p.y2)
     small[...] = jnp.zeros_like(small)
     totals[...] = jnp.zeros_like(totals)
@@ -1266,14 +1284,17 @@
         return carry
 
     d_first = mid_part
-    back = Reduce(links, p, d_first, far_a, near_a)
+    backs = [Reduce(links, p, d_first, far_a, near_a, t, SPAN // 2) for t in (0, SPAN // 2)]
     ahead.settle()
     lax.fori_loop(0, SPAN // 16, ahead_rows, 0)
     spread_b.start_first()
     lax.fori_loop(0, 4, first_part, 0)
-    back.send_first()
+    for back in backs:
+        back.send_first()
     lax.fori_loop(4, 8, first_part, 0)
-    back.send_second()
+    for back in backs:
+        back.send_second_far()
+    backs[0].send_second_near()
     for xx in range(4):
         small_scatter.take(xx)
     small_scatter.first()
@@ -1300,7 +1321,9 @@
     for xx in range(4):
         scatter.give(xx)
     small_scatter.merge()
-    back.merge()
+    backs[0].merge()
+    backs[1].send_second_near()
+    backs[1].merge()
     spread_b.start_second()
     lax.fori_loop(0, 4, keep, 0)
     small_scatter.turn()
@@ -1311,20 +1334,22 @@
         small_all[p.x, p.c, p.z, base : base + 32, :] = value.astype(BF16)
 
     small_scatter.merge_2()
-    back.settle()
     load_tokens.wait()
     gain = gain_rows[0:1, :].astype(F32)
 
     def back_rows(k, carry):
         at = pl.ds(pl.multiple_of(k * 16, 16), 16)
-        through, share = norm_back_rows(own_sum(back, at), own_tokens[at, :].astype(F32), gain)
+        through, share = norm_back_rows(own_sum(backs[0], at), own_tokens[at, :].astype(F32), gain)
         gain_in[...] += share[0:8] + share[8:16]
         grad_tokens[p.y, at, :] = (d_after_own[at, :] + through).astype(BF16)
         return carry
 
-    lax.fori_loop(0, SPAN // 16, back_rows, 0)
-    spread_a = Spread(links, p, grad_tokens)
-    spread_a.start()
+    spreads_a = []
+    for t, back in enumerate(backs):
+        back.settle()
+        lax.fori_loop(4 * t, 4 * t + 4, back_rows, 0)
+        spreads_a.append(Spread(links, p, grad_tokens, t * SPAN // 2, SPAN // 2))
+        spreads_a[t].start()
     small_scatter.finish(store_small)
     small_gather = Gather(links, p, small_all, 128)
     small_gather.first()
@@ -1337,7 +1362,8 @@
     small_gather.middle()
     small_gather.finish()
     small_gather.second()
-    spread_a.forward()
+    for spread_a in spreads_a:
+        spread_a.forward()
     spread_b.forward()
     for d in (1, 2, 3):
         links.arrived(gain_y.at[lax.rem(p.y + 4 - d, 4)], y_keys[d - 1], others_y[0])
@@ -1372,8 +1398,9 @@
         grad_mix[base : base + 32, :] = value
 
     scatter.finish(store)
-    spread_a.near()
-    spread_a.far()
+    for spread_a in spreads_a:
+        spread_a.near()
+        spread_a.far()
     links.drain()
 
 
@@ -1435,8 +1462,8 @@
             pltpu.VMEM((4, 2, WIDTH), F32),
             pltpu.SemaphoreType.DMA((15,)),
             pltpu.SemaphoreType.DMA((8,)),
-            pltpu.SemaphoreType.DMA((184,)),
-            pltpu.SemaphoreType.DMA((184,)),
+            pltpu.SemaphoreType.DMA((224,)),
+            pltpu.SemaphoreType.DMA((224,)),
         ],
         compiler_params=params(2),
         name="back_all",

time: 304 us -> 302 us (level)
  no operation moved by 1% of the time
where the time goes in v6:
time: 302 us; the launch traced here: 301 us
  Pallas kernels  287 us (95%)
  between operations  14.1 us (5%)
    pallas_call x1, Pallas kernels, back_all(): pl.pallas_call(back_kernel, out_shape=[shape((ROWS, SPAN, WIDTH), BF16),...  143 us
    pallas_call x1, Pallas kernels, mix_forward(): pl.pallas_call(mix_forward_kernel, out_shape=outs, in_specs=[vmem()] * 7...  107 us
    pallas_call x1, Pallas kernels, mlp_all(): pl.pallas_call(mlp_kernel, grid=(CHUNKS,), out_shape=[shape((TOKENS, MLP)...  30.5 us
    pallas_call x1, Pallas kernels, finish(): pl.pallas_call(finish_kernel, grid=(ROWS,), out_shape=[shape((ROWS, SPAN,...  6.59 us
  transfers between devices with their start and end apart: 1, of which 0 were waited for; matrix products, arithmetic and copies ran while one was open for 0% of the time, Pallas kernels for 47%

profile of v6, /device:TPU:1, one launch (start us, length us, event | category | flops | bytes accessed | tf_op | source)
XLA Modules:
  0.0 301.3 jit_solution(9416727488926992723)
XLA Ops:
  7.2 0.0 reduce-scatter.2.cloned.1.call-start
  7.2 107.3 %mix_forward.1 = (bf16[4,2,4,64,1920]{4,3,2,1,0:T(8,128)(2,1)}, bf16[4,2,4,64,4608]{4,3,2,1,0:T(8,128)(2,1)}, f32[512,640]{1,0:T(8,128)}, f32[512,640]{1,0:T(8,1...) custom-call(bf16[512,2048]{1,0:T(8,128)(2,1)} %bitcast.16, ...), custom_call_target="tpu_custom_call" | custom-call | tf_op jit(solution)/shard_map/mix_forward/pallas_call | solution.py:687
  114.5 30.5 %mlp_all.1 = (bf16[512,1536]{1,0:T(8,128)(2,1)}, bf16[512,1536]{1,0:T(8,128)(2,1)}, bf16[512,1536]{1,0:T(8,128)(2,1)}, bf16[2048,4608]{1,0:T(8,128)(2,1)}, f32[4,128,640]{2,1,0:T(8,128)}) custom-call(bf16[512,2048]{1,0:T(8,128)(2,1)} %bitcast.25, bf16[512,2048]{1,0:T(8,128)(2,1)} %bitcast.17, bf16[2048,4608]{1,0:T(8,128)(2,1)} %bitcast.13, ...), custom_call_target="tpu_custom_call" | custom-call | flops 19327352832 | bytes 37748736 | tf_op jit(solution)/shard_map/mlp_all/pallas_call | solution.py:769
  145.0 0.0 reduce-scatter.2.cloned.1.call-update
  145.0 142.8 %back_all.1 = (bf16[4,128,2048]{2,1,0:T(8,128)(2,1)}, bf16[4,128,2048]{2,1,0:T(8,128)(2,1)}, f32[64,1920]{1,0:T(8,128)}, f32[8,640]{1,0:T(8,128)}, f32[1280,256]{1,0:T(8,128)}, /*index=5*/f32[2,2048]{1,0:T(2,128)}) custom-call(bf16[2,4,64,1536]{3,2,1,0:T(8,128)(2,1)} %bitcast.18, bf16[2,4,64,1536]{3,2,1,0:T(8,128)(2,1)} %bitcast.19, ...), custom_call_target="tpu_custom_call" | custom-call | tf_op jit(solution)/shard_map/back_all/pallas_call | solution.py:1411
  287.8 0.0 reduce-scatter.2.cloned.1.call-done.mlp_sum
  287.9 6.6 %finish.1 = (bf16[4,128,2048]{2,1,0:T(8,128)(2,1)}, bf16[4,128,2048]{2,1,0:T(8,128)(2,1)}, f32[2,2048]{1,0:T(2,128)}, f32[2,64,640]{2,1,0:T(8,128)}, f32[64,640]...) custom-call(bf16[4,128,2048]{2,1,0:T(8,128)(2,1)} %get-tuple-element, ...), custom_call_target="tpu_custom_call" | custom-call | tf_op jit(solution)/shard_map/finish/pallas_call | solution.py:1528
Async XLA Ops:
  7.2 280.7 %reduce-scatter.2.cloned.1.call-start = ((), (), s32[]{:S(2)}) async-start(), calls=%async_computation.1 | async-start | bytes 19464192 | tf_op jit(solution)/shard_map/reduce_scatter | solution.py:1631
Sparse Core Ops, SparseCore 0:
  145.1 137.1 reduce-scatter.1
